TPU v7x, 256 devices: a whole 4x4x8 slice. The times are simulated.
256 devices in a mesh: dp: 16 (over z, core), expert: 16 (over y, x).
Axes of the slice: x: 4, y: 4, z: 8, core: 2. Of those that a mesh axis runs over, the one named last changes fastest.
Arguments:
- tokens: bfloat16 [32768, 768], P(('dp', 'expert')), may hold values from -6 to 6
- routes: int32 [32768, 2], P(('dp', 'expert')), may hold values from 0 to 15, all different within a row; in each aligned block of 128 rows (0 to 127, 128 to 255, ...) at most 20 rows name the same one
- route_gates: float32 [32768, 2], P(('dp', 'expert')), may hold values from 0.25 to 1
- cotangent: bfloat16 [32768, 768], P(('dp', 'expert')), may hold values from -6 to 6
- gate_weight: bfloat16 [16, 3072, 768], P('expert', 'dp'), may hold values from -0.21875 to 0.21875
- up_weight: bfloat16 [16, 3072, 768], P('expert', 'dp'), may hold values from -0.21875 to 0.21875
- down_weight: bfloat16 [16, 3072, 768], P('expert', 'dp'), may hold values from -0.109375 to 0.109375
Outputs:
- mixed_output: bfloat16 [32768, 768], P(('dp', 'expert'))
- token_grads: bfloat16 [32768, 768], P(('dp', 'expert'))
- gate_grad: float32 [16, 3072, 768], P('expert', 'dp')
- up_grad: float32 [16, 3072, 768], P('expert', 'dp')
- down_grad: float32 [16, 3072, 768], P('expert', 'dp')
Inputs may be any that keep to these rules, and one draw needn't show every extreme that they name: Each token names 2 different experts; no expert is named by more than 20 routes of the tokens of one device.
All inputs are finite; a program needn't handle non-finite values.
Results may differ from a plain program's by a relative error of at most 0.02.
Values may be sent and summed in bfloat16 or wider, within the bound.
No kernel may reach another device: no remote copies, remote signals or barrier semaphores. Data moves between devices by JAX's collectives and lax.ppermute only.
A program may use at most 128 MiB of HBM per device.

v0:
```python
import jax
import jax.numpy as jnp
from jax import lax
from jax.sharding import PartitionSpec as P


def slot_matrix(routes, expert_count, capacity):
    flat_routes = routes.reshape(-1)
    labels = jnp.arange(expert_count, dtype=jnp.int32)
    hit_table = (flat_routes[:, None] == labels[None, :]).astype(jnp.int32)
    before = jnp.cumsum(hit_table, axis=0) - hit_table
    target = flat_routes * capacity + jnp.sum(before * hit_table, axis=1)
    slot_ids = jnp.arange(expert_count * capacity, dtype=jnp.int32)
    placer = (target[:, None] == slot_ids[None, :]).astype(jnp.bfloat16)
    return placer.reshape(routes.shape[0], routes.shape[1], expert_count * capacity)


def contract_rows(left_side, right_side):
    return lax.dot_general(
        left_side, right_side, (((0,), (0,)), ((), ())), preferred_element_type=jnp.float32
    )


def contract_last(left_side, right_side):
    return lax.dot_general(
        left_side, right_side, (((1,), (1,)), ((), ())), preferred_element_type=jnp.float32
    )


def expert_forward(token_rows, w_gate, w_up, w_down):
    pre_gate = contract_last(token_rows, w_gate)
    pre_up = contract_last(token_rows, w_up)
    sigmoid_gate = jax.nn.sigmoid(pre_gate)
    active = pre_gate * sigmoid_gate
    silu_slope = sigmoid_gate * (1.0 + pre_gate * (1.0 - sigmoid_gate))
    hidden = (active * pre_up).astype(jnp.bfloat16)
    expert_out = jnp.dot(hidden, w_down, preferred_element_type=jnp.float32).astype(jnp.bfloat16)
    return (expert_out, hidden, pre_up, active, silu_slope)


def expert_backward(grad_rows, pre_up, active, silu_slope, w_gate, w_up, w_down):
    grad_hidden = contract_last(grad_rows, w_down)
    grad_gate = (grad_hidden * pre_up * silu_slope).astype(jnp.bfloat16)
    grad_up = (grad_hidden * active).astype(jnp.bfloat16)
    grad_input = (
        jnp.dot(grad_gate, w_gate, preferred_element_type=jnp.float32)
        + jnp.dot(grad_up, w_up, preferred_element_type=jnp.float32)
    ).astype(jnp.bfloat16)
    return (grad_input, grad_gate, grad_up)


def weight_sums(token_rows, grad_rows, hidden, grad_gate, grad_up):
    terms = (
        contract_rows(grad_gate, token_rows),
        contract_rows(grad_up, token_rows),
        contract_rows(hidden, grad_rows),
    )
    return (
        lax.psum_scatter(
            terms[0].astype(jnp.bfloat16), "dp", scatter_dimension=0, tiled=True
        ).astype(jnp.float32),
        lax.psum_scatter(
            terms[1].astype(jnp.bfloat16), "dp", scatter_dimension=0, tiled=True
        ).astype(jnp.float32),
        lax.psum_scatter(
            terms[2].astype(jnp.bfloat16), "dp", scatter_dimension=0, tiled=True
        ).astype(jnp.float32),
    )


def per_device(tokens, routes, route_gates, cotangent, gate_weight, up_weight, down_weight):
    expert_count = lax.axis_size("expert")
    data_count = lax.axis_size("dp")
    tok_rows = tokens.shape[0]
    model_dim = tokens.shape[1]
    choose = routes.shape[1]
    capacity = tok_rows * choose * 5 // (4 * expert_count)
    flat_rows = expert_count * capacity
    placer = slot_matrix(routes, expert_count, capacity)
    route_cotangent = (cotangent.astype(jnp.float32)[:, None, :] * route_gates[:, :, None]).astype(
        jnp.bfloat16
    )
    sent_rows = jnp.einsum("tks,td->sd", placer, tokens, preferred_element_type=jnp.float32)
    sent_rows = sent_rows.astype(jnp.bfloat16).reshape(expert_count, capacity, model_dim)
    sent_grads = jnp.einsum(
        "tks,tkd->sd", placer, route_cotangent, preferred_element_type=jnp.float32
    )
    sent_grads = sent_grads.astype(jnp.bfloat16).reshape(expert_count, capacity, model_dim)
    gathered = (
        lax.all_gather(gate_weight, "dp", axis=1, tiled=True),
        lax.all_gather(up_weight, "dp", axis=1, tiled=True),
        lax.all_gather(down_weight, "dp", axis=1, tiled=True),
    )
    w_gate = gathered[0][0]
    w_up = gathered[1][0]
    w_down = gathered[2][0]
    arrived = lax.all_to_all(sent_rows, "expert", split_axis=0, concat_axis=0, tiled=True)
    expert_rows = arrived.reshape(flat_rows, model_dim)
    expert_out, hidden, pre_up, active, silu_slope = expert_forward(
        expert_rows, w_gate, w_up, w_down
    )
    returned = lax.all_to_all(
        expert_out.reshape(expert_count, capacity, model_dim),
        "expert",
        split_axis=0,
        concat_axis=0,
        tiled=True,
    )
    arrived_grads = lax.all_to_all(sent_grads, "expert", split_axis=0, concat_axis=0, tiled=True)
    expert_grads = arrived_grads.reshape(flat_rows, model_dim)
    grad_input, grad_gate, grad_up = expert_backward(
        expert_grads, pre_up, active, silu_slope, w_gate, w_up, w_down
    )
    grad_totals = weight_sums(expert_rows, expert_grads, hidden, grad_gate, grad_up)
    returned_grads = lax.all_to_all(
        grad_input.reshape(expert_count, capacity, model_dim),
        "expert",
        split_axis=0,
        concat_axis=0,
        tiled=True,
    )
    picked = jnp.einsum(
        "tks,sd->tkd",
        placer,
        returned.reshape(flat_rows, model_dim),
        preferred_element_type=jnp.float32,
    )
    layer_out = jnp.sum(route_gates[:, :, None] * picked, axis=1).astype(jnp.bfloat16)
    picked_grads = jnp.einsum(
        "tks,sd->tkd",
        placer,
        returned_grads.reshape(flat_rows, model_dim),
        preferred_element_type=jnp.float32,
    )
    input_grads = jnp.sum(picked_grads, axis=1).astype(jnp.bfloat16)
    grad_scale = float(tok_rows * choose * data_count) ** (-0.5)
    gate_total, up_total, down_total = grad_totals
    return (
        layer_out,
        input_grads,
        (gate_total * grad_scale)[None],
        (up_total * grad_scale)[None],
        (down_total * grad_scale)[None],
    )


def solution(mesh):
    in_specs = (
        P(("dp", "expert"), None),
        P(("dp", "expert"), None),
        P(("dp", "expert"), None),
        P(("dp", "expert"), None),
        P("expert", "dp", None),
        P("expert", "dp", None),
        P("expert", "dp", None),
    )
    out_specs = (
        P(("dp", "expert"), None),
        P(("dp", "expert"), None),
        P("expert", "dp", None),
        P("expert", "dp", None),
        P("expert", "dp", None),
    )
    return jax.shard_map(
        per_device, mesh=mesh, in_specs=in_specs, out_specs=out_specs, check_vma=False
    )
```

profile of v0, /device:TPU:1, one launch (start us, length us, event | category | flops | bytes accessed | tf_op | source)
XLA Modules:
  0.0 355.0 jit_solution(11072329065213143620)
XLA Ops:
  7.2 0.0 copy-start
  7.2 0.0 all-gather.6.cloned.1.call-start
  7.2 0.7 all-gather.6.cloned.1.call-update
  7.9 0.0 all-gather.8.cloned.1.call-start
  8.0 0.7 all-gather.8.cloned.1.call-update
  8.7 0.0 all-gather.4.cloned.1.call-start
  8.7 0.7 all-gather.4.cloned.1.call-update
  9.4 0.8 copy.26
  10.2 0.1 eq.69
  10.3 0.1 eq.65
  10.5 0.6 reduce-window.6
  11.1 0.2 slice_reduce_fusion
  11.3 0.1 fusion.35
  11.4 0.1 reduce_sum.39
  11.5 0.1 copy.29
  11.6 1.0 convert_element_type.73
  12.6 0.7 multiply_add_fusion
  13.3 1.0 fusion.19
  14.3 0.9 reshape.103
  15.2 7.6 %all-to-all-start.2 = ((bf16[16,20,768]{2,1,0:T(8,128)(2,1)}), bf16[16,20,768]{2,1,0:T(8,128)(2,1)S(1)}, u32[]{:S(2)}, u32[]{:S(2)}) async-start(bf16[16,20,768]{2,1,0:T(8,128)(2,1)} %reshape.103), calls=%async_computation.2 | async-start | bytes 1179648 | tf_op jit(solution)/shard_map/all_to_all | solution.py:109
  22.9 0.0 copy-done
  22.9 0.3 fusion.37
  23.2 0.9 reshape.99
  24.1 9.8 %all-to-all-done.2 = bf16[16,20,768]{2,1,0:T(8,128)(2,1)S(1)} async-done(((bf16[16,20,768]{2,1,0:T(8,128)(2,1)}), bf16[16,20,768]{2,1,0:T(8,128)(2,1)S(1)}, u32[]{:S(2)}, u32[]{:S(2)}) %all-to-all-start.2) | async-done | bytes 491552 | tf_op jit(solution)/shard_map/all_to_all | solution.py:109
  33.9 3.7 %all-to-all-start = ((bf16[16,20,768]{2,1,0:T(8,128)(2,1)}), bf16[16,20,768]{2,1,0:T(8,128)(2,1)S(1)}, u32[]{:S(2)}, u32[]{:S(2)}) async-start(bf16[16,20,768]{2,1,0:T(8,128)(2,1)} %reshape.99), calls=%async_computation | async-start | bytes 1179648 | tf_op jit(solution)/shard_map/all_to_all | solution.py:97
  37.6 0.0 reduce-scatter.4.cloned.1.call-start
  37.7 0.1 reshape.104
  37.8 10.4 %all-to-all-done = bf16[16,20,768]{2,1,0:T(8,128)(2,1)S(1)} async-done(((bf16[16,20,768]{2,1,0:T(8,128)(2,1)}), bf16[16,20,768]{2,1,0:T(8,128)(2,1)S(1)}, u32[]{:S(2)}, u32[]{:S(2)}) %all-to-all-start) | async-done | bytes 491552 | tf_op jit(solution)/shard_map/all_to_all | solution.py:97
  48.2 0.1 reshape.100
  48.3 8.6 %all-gather.6.cloned.1.call-done = bf16[1,3072,768]{2,1,0:T(8,128)(2,1)} async-done(((bf16[1,192,768]{2,1,0:T(8,128)(2,1)}), bf16[1,3072,768]{2,1,0:T(8,128)(2,1)}) %all-gather.6.cloned.1.call-update) | async-done | bytes 4718608 | tf_op jit(solution)/shard_map/all_gather | solution.py:91
  56.9 6.0 %fusion.6 = f32[320,3072]{1,0:T(8,128)} fusion(bf16[320,768]{1,0:T(8,128)(2,1)S(1)} %reshape.100, bf16[1,3072,768]{2,1,0:T(8,128)(2,1)} %all-gather.6.cloned.1.call-done), kind=kOutput, calls=%fused_computation.9 | convolution fusion | flops 1509949440 | bytes 9142272 | tf_op jit(solution)/shard_map/dot_general | solution.py:25
  62.9 37.2 %all-gather.8.cloned.1.call-done = bf16[1,3072,768]{2,1,0:T(8,128)(2,1)} async-done(((bf16[1,192,768]{2,1,0:T(8,128)(2,1)}), bf16[1,3072,768]{2,1,0:T(8,128)(2,1)}) %all-gather.8.cloned.1.call-update) | async-done | bytes 4718608 | tf_op jit(solution)/shard_map/all_gather | solution.py:92
  100.0 6.0 %fusion = f32[320,3072]{1,0:T(8,128)} fusion(bf16[320,768]{1,0:T(8,128)(2,1)S(1)} %reshape.104, bf16[1,3072,768]{2,1,0:T(8,128)(2,1)} %all-gather.8.cloned.1.call-done), kind=kOutput, calls=%fused_computation.3 | convolution fusion | flops 1509949440 | bytes 9142272 | tf_op jit(solution)/shard_map/dot_general | solution.py:25
  106.0 37.2 %all-gather.4.cloned.1.call-done = bf16[1,3072,768]{2,1,0:T(8,128)(2,1)} async-done(((bf16[1,192,768]{2,1,0:T(8,128)(2,1)}), bf16[1,3072,768]{2,1,0:T(8,128)(2,1)}) %all-gather.4.cloned.1.call-update) | async-done | bytes 4718608 | tf_op jit(solution)/shard_map/all_gather | solution.py:90
  143.2 8.9 %multiply_convert_fusion.1 = (bf16[320,3072]{1,0:T(8,128)(2,1)S(1)}, bf16[320,3072]{1,0:T(8,128)(2,1)}, bf16[320,3072]{1,0:T(8,128)(2,1)S(1)}) fusion(f32[320,3072]{1,0:T(8,128)} %fusion, f32[320,3072]{1,0:T(8,128)} %fusion.6, bf16[320,768]{1,0:T(8,128)(2,1)S(1)} %reshape.100, bf16[1,3072,768]{2,1,0:T(8,128)(2,1)} %all-gather.4.cloned.1.call-done), kind=kOutput, calls=%fused_computation.16 | convolution fusion | flops 1524695040 | bytes 18972672 | tf_op jit(solution)/shard_map/dot_general | solution.py:25
  152.2 1.3 copy-done.2
  153.5 4.3 %convolution_convert_fusion.2 = bf16[3072,768]{1,0:T(8,128)(2,1)} fusion(bf16[320,3072]{1,0:T(8,128)(2,1)S(1)} %get-tuple-element.5, bf16[320,768]{1,0:T(8,128)(2,1)S(1)} %reshape.100), kind=kOutput, calls=%fused_computation.2 | convolution fusion | flops 1512308736 | bytes 7176192 | tf_op jit(solution)/shard_map/dot_general | solution.py:19
  157.8 0.0 reduce-scatter.4.cloned.1.call-update
  157.8 0.0 reduce-scatter.6.cloned.1.call-start
  157.8 6.4 %convolution_convert_fusion.1 = bf16[3072,768]{1,0:T(8,128)(2,1)} fusion(bf16[320,3072]{1,0:T(8,128)(2,1)} %get-tuple-element.6, bf16[320,768]{1,0:T(8,128)(2,1)S(1)} %reshape.100), kind=kOutput, calls=%fused_computation.1 | convolution fusion | flops 1512308736 | bytes 7176192 | tf_op jit(solution)/shard_map/dot_general | solution.py:19
  164.2 0.0 reduce-scatter.6.cloned.1.call-update
  164.2 0.2 reduce-scatter.8.cloned.1.call-start
  164.5 4.3 %convolution_convert_fusion = bf16[3072,768]{1,0:T(8,128)(2,1)} fusion(bf16[320,3072]{1,0:T(8,128)(2,1)S(1)} %get-tuple-element.7, bf16[320,768]{1,0:T(8,128)(2,1)S(1)} %reshape.104), kind=kOutput, calls=%fused_computation | convolution fusion | flops 1512308736 | bytes 7176192 | tf_op jit(solution)/shard_map/dot_general | solution.py:19
  168.8 0.0 reduce-scatter.8.cloned.1.call-update
  168.8 4.8 %fusion.4 = f32[320,768]{1,0:T(8,128)S(1)} fusion(bf16[320,3072]{1,0:T(8,128)(2,1)} %get-tuple-element.6, bf16[1,3072,768]{2,1,0:T(8,128)(2,1)} %all-gather.6.cloned.1.call-done), kind=kOutput, calls=%fused_computation.7 | convolution fusion | flops 1509949440 | bytes 7667712 | tf_op jit(solution)/shard_map/dot_general | solution.py:47
  173.6 4.1 %fusion.16 = bf16[320,768]{1,0:T(8,128)(2,1)S(1)} fusion(f32[320,768]{1,0:T(8,128)S(1)} %fusion.4, bf16[320,3072]{1,0:T(8,128)(2,1)S(1)} %copy-done.3, bf16[1,3072,768]{2,1,0:T(8,128)(2,1)} %all-gather.4.cloned.1.call-done), kind=kOutput, calls=%fused_computation.23 | convolution fusion | flops 1510440960 | bytes 8159232 | tf_op jit(solution)/shard_map/dot_general | solution.py:46
  177.8 0.9 reshape.105
  178.7 6.5 %all-to-all-start.3 = ((bf16[16,20,768]{2,1,0:T(8,128)(2,1)}), bf16[16,20,768]{2,1,0:T(8,128)(2,1)S(1)}, u32[]{:S(2)}, u32[]{:S(2)}) async-start(bf16[16,20,768]{2,1,0:T(8,128)(2,1)} %reshape.105), calls=%async_computation.3 | async-start | bytes 1179648 | tf_op jit(solution)/shard_map/all_to_all | solution.py:115
  185.2 4.1 %fusion.20 = bf16[320,768]{1,0:T(8,128)(2,1)S(1)} fusion(bf16[320,3072]{1,0:T(8,128)(2,1)S(1)} %get-tuple-element.7, bf16[1,3072,768]{2,1,0:T(8,128)(2,1)} %all-gather.8.cloned.1.call-done), kind=kOutput, calls=%fused_computation.25 | convolution fusion | flops 1510195200 | bytes 7176192 | tf_op jit(solution)/shard_map/dot_general | solution.py:37
  189.3 0.0 copy-start.1
  189.3 0.9 reshape.101
  190.2 6.5 %all-to-all-done.3 = bf16[16,20,768]{2,1,0:T(8,128)(2,1)S(1)} async-done(((bf16[16,20,768]{2,1,0:T(8,128)(2,1)}), bf16[16,20,768]{2,1,0:T(8,128)(2,1)S(1)}, u32[]{:S(2)}, u32[]{:S(2)}) %all-to-all-start.3) | async-done | bytes 491552 | tf_op jit(solution)/shard_map/all_to_all | solution.py:115
  196.7 3.6 %all-to-all-start.1 = ((bf16[16,20,768]{2,1,0:T(8,128)(2,1)}), bf16[16,20,768]{2,1,0:T(8,128)(2,1)S(1)}, u32[]{:S(2)}, u32[]{:S(2)}) async-start(bf16[16,20,768]{2,1,0:T(8,128)(2,1)} %reshape.101), calls=%async_computation.1 | async-start | bytes 1179648 | tf_op jit(solution)/shard_map/all_to_all | solution.py:102
  200.3 0.1 reshape.109
  200.4 10.5 %all-to-all-done.1 = bf16[16,20,768]{2,1,0:T(8,128)(2,1)S(1)} async-done(((bf16[16,20,768]{2,1,0:T(8,128)(2,1)}), bf16[16,20,768]{2,1,0:T(8,128)(2,1)S(1)}, u32[]{:S(2)}, u32[]{:S(2)}) %all-to-all-start.1) | async-done | bytes 491552 | tf_op jit(solution)/shard_map/all_to_all | solution.py:102
  211.0 0.1 reshape.107
  211.1 1.1 convolution_reduce_fusion
  212.2 1.1 fusion.23
  213.3 3.9 %reduce-scatter.4.cloned.1.call-done = bf16[192,768]{1,0:T(8,128)(2,1)} async-done(((bf16[3072,768]{1,0:T(8,128)(2,1)}), bf16[192,768]{1,0:T(8,128)(2,1)}) %reduce-scatter.4.cloned.1.call-update) | async-done | bytes 294928 | tf_op jit(solution)/shard_map/reduce_scatter | solution.py:59
  217.2 1.8 multiply_bitcast_fusion.2
  219.0 62.5 %reduce-scatter.6.cloned.1.call-done = bf16[192,768]{1,0:T(8,128)(2,1)} async-done(((bf16[3072,768]{1,0:T(8,128)(2,1)}), bf16[192,768]{1,0:T(8,128)(2,1)}) %reduce-scatter.6.cloned.1.call-update) | async-done | bytes 294928 | tf_op jit(solution)/shard_map/reduce_scatter | solution.py:62
  281.5 1.8 multiply_bitcast_fusion.1
  283.3 63.0 %reduce-scatter.8.cloned.1.call-done = bf16[192,768]{1,0:T(8,128)(2,1)} async-done(((bf16[3072,768]{1,0:T(8,128)(2,1)}), bf16[192,768]{1,0:T(8,128)(2,1)}) %reduce-scatter.8.cloned.1.call-update) | async-done | bytes 294928 | tf_op jit(solution)/shard_map/reduce_scatter | solution.py:65
  346.3 1.8 multiply_bitcast_fusion
  (8 shorter events, 0.1 us)
Async XLA Ops:
  7.2 15.7 %copy-start = (bf16[128,768]{1,0:T(8,128)(2,1)S(1)}, bf16[128,768]{1,0:T(8,128)(2,1)}, u32[]{:S(2)}) copy-start(bf16[128,768]{1,0:T(8,128)(2,1)} %param.7) | copy-start | bytes 589828
  7.2 49.7 %all-gather.6.cloned.1.call-start = ((), (), s32[]{:S(2)}) async-start(), calls=%async_computation.8 | async-start | bytes 5013504 | tf_op jit(solution)/shard_map/all_gather | solution.py:91
  7.9 92.1 %all-gather.8.cloned.1.call-start = ((), (), s32[]{:S(2)}) async-start(), calls=%async_computation.9 | async-start | bytes 5013504 | tf_op jit(solution)/shard_map/all_gather | solution.py:92
  8.7 134.6 %all-gather.4.cloned.1.call-start = ((), (), s32[]{:S(2)}) async-start(), calls=%async_computation.7 | async-start | bytes 5013504 | tf_op jit(solution)/shard_map/all_gather | solution.py:90
  15.2 18.7 %all-to-all-start.2 = ((bf16[16,20,768]{2,1,0:T(8,128)(2,1)}), bf16[16,20,768]{2,1,0:T(8,128)(2,1)S(1)}, u32[]{:S(2)}, u32[]{:S(2)}) async-start(bf16[16,20,768]{2,1,0:T(8,128)(2,1)} %reshape.103), calls=%async_computation.2 | async-start | bytes 1179648 | tf_op jit(solution)/shard_map/all_to_all | solution.py:109
  33.9 14.3 %all-to-all-start = ((bf16[16,20,768]{2,1,0:T(8,128)(2,1)}), bf16[16,20,768]{2,1,0:T(8,128)(2,1)S(1)}, u32[]{:S(2)}, u32[]{:S(2)}) async-start(bf16[16,20,768]{2,1,0:T(8,128)(2,1)} %reshape.99), calls=%async_computation | async-start | bytes 1179648 | tf_op jit(solution)/shard_map/all_to_all | solution.py:97
  37.6 179.5 %reduce-scatter.4.cloned.1.call-start = ((), (), s32[]{:S(2)}) async-start(), calls=%async_computation.10 | async-start | bytes 5013504 | tf_op jit(solution)/shard_map/reduce_scatter | solution.py:59
  152.2 1.3 copy-start.2
  157.8 123.7 %reduce-scatter.6.cloned.1.call-start = ((), (), s32[]{:S(2)}) async-start(), calls=%async_computation.11 | async-start | bytes 5013504 | tf_op jit(solution)/shard_map/reduce_scatter | solution.py:62
  164.2 182.1 %reduce-scatter.8.cloned.1.call-start = ((), (), s32[]{:S(2)}) async-start(), calls=%async_computation.12 | async-start | bytes 5013504 | tf_op jit(solution)/shard_map/reduce_scatter | solution.py:65
  168.8 4.8 %copy-start.3 = (bf16[320,3072]{1,0:T(8,128)(2,1)S(1)}, bf16[320,3072]{1,0:T(8,128)(2,1)}, u32[]{:S(2)}) copy-start(bf16[320,3072]{1,0:T(8,128)(2,1)} %copy-done.2) | copy-start | bytes 5898244
  178.7 18.1 %all-to-all-start.3 = ((bf16[16,20,768]{2,1,0:T(8,128)(2,1)}), bf16[16,20,768]{2,1,0:T(8,128)(2,1)S(1)}, u32[]{:S(2)}, u32[]{:S(2)}) async-start(bf16[16,20,768]{2,1,0:T(8,128)(2,1)} %reshape.105), calls=%async_computation.3 | async-start | bytes 1179648 | tf_op jit(solution)/shard_map/all_to_all | solution.py:115
  189.3 22.9 %copy-start.1 = (f32[128,2]{0,1:T(2,128)S(1)}, f32[128,2]{0,1:T(2,128)}, u32[]{:S(2)}) copy-start(f32[128,2]{0,1:T(2,128)} %param.9) | copy-start | bytes 3076
  196.7 14.2 %all-to-all-start.1 = ((bf16[16,20,768]{2,1,0:T(8,128)(2,1)}), bf16[16,20,768]{2,1,0:T(8,128)(2,1)S(1)}, u32[]{:S(2)}, u32[]{:S(2)}) async-start(bf16[16,20,768]{2,1,0:T(8,128)(2,1)} %reshape.101), calls=%async_computation.1 | async-start | bytes 1179648 | tf_op jit(solution)/shard_map/all_to_all | solution.py:102
Sparse Core Ops, SparseCore 0:
  9.8 46.9 all-gather.5
  58.7 41.3 all-gather.7
  101.9 41.3 all-gather.3
  157.9 59.2 reduce-scatter.3
  219.6 61.8 reduce-scatter.5
  283.9 62.3 reduce-scatter.7
where the time goes:
time: 358 us; the launch traced here: 355 us
  waiting for transfers between devices  252 us (70%)
  matrix products  52.5 us (15%)
  starting transfers between devices  21.8 us (6%)
  between operations  14.3 us (4%)
  other arithmetic  7.87 us (2%)
  local copies, waits for them, and re-layouts  6.8 us (2%)
    reduce_scatter x1, waiting for transfers between devices, weight_sums(): lax.psum_scatter(terms[2].astype(jnp.bfloat16), 'dp', scatter_dimension=0...  63 us
    reduce_scatter x1, waiting for transfers between devices, weight_sums(): lax.psum_scatter(terms[1].astype(jnp.bfloat16), 'dp', scatter_dimension=0...  62.5 us
    all_gather x1, waiting for transfers between devices, per_device(): lax.all_gather(gate_weight, 'dp', axis=1, tiled=True)  37.2 us
    all_gather x1, waiting for transfers between devices, per_device(): lax.all_gather(down_weight, 'dp', axis=1, tiled=True)  37.2 us
    dot_general x3, matrix products, contract_last(): lax.dot_general(left_side, right_side, (((1,), (1,)), ((), ())), preferre...  21 us
    dot_general x3, matrix products, contract_rows(): lax.dot_general(left_side, right_side, (((0,), (0,)), ((), ())), preferre...  15 us
    all_to_all x1, waiting for transfers between devices, per_device(): lax.all_to_all(expert_out.reshape(expert_count, capacity, model_dim), 'ex...  10.5 us
    all_to_all x1, waiting for transfers between devices, per_device(): lax.all_to_all(sent_rows, 'expert', split_axis=0, concat_axis=0, tiled=True)  10.4 us
  transfers between devices with their start and end apart: 10, of which 10 were waited for; matrix products, arithmetic and copies ran while one was open for 14% of the time, Pallas kernels for 0%

commit v1 on v0

v1 whole, which is shorter than its diff:
```python
import functools

import jax
import jax.numpy as jnp
from jax import lax
from jax.experimental import pallas as pl
from jax.experimental.pallas import tpu as pltpu
from jax.sharding import Mesh, PartitionSpec as P

BF16 = jnp.bfloat16
F32 = jnp.float32
CORES = 2
GROUP = 4
PEAK_PER_US = 1.15e9
FAR_US = 5.0
NEAR_US = 1.0
MERGE_US = 30.0
VMEM_BYTES = 60 * 1024 * 1024


def dot_nn(a, b):
    return lax.dot_general(a, b, (((1,), (0,)), ((), ())), preferred_element_type=F32)


def dot_nt(a, b):
    return lax.dot_general(a, b, (((1,), (1,)), ((), ())), preferred_element_type=F32)


def dot_tn(a, b):
    return lax.dot_general(a, b, (((0,), (0,)), ((), ())), preferred_element_type=F32)


def whole(count):
    return [pl.BlockSpec(memory_space=pltpu.VMEM) for _ in range(count)]


def kernel_call(body, out_shapes, micros, operands, scratch=(), loads=False, stores=0):
    in_hbm = [pl.BlockSpec(memory_space=pl.ANY)]
    return pl.pallas_call(
        body,
        out_shape=out_shapes,
        in_specs=in_hbm * len(operands) if loads else whole(len(operands)),
        out_specs=in_hbm * stores + whole(len(out_shapes) - stores),
        scratch_shapes=list(scratch),
        compiler_params=pltpu.CompilerParams(vmem_limit_bytes=VMEM_BYTES),
        cost_estimate=pl.CostEstimate(
            flops=int(micros * PEAK_PER_US), bytes_accessed=0, transcendentals=0
        ),
    )(*operands)


def start_copy(src, dst, sem):
    copy = pltpu.make_async_copy(src, dst, sem)
    copy.start()
    return copy


def route_info(routes, gates_row, experts, stride):
    tokens = routes.shape[1]
    routes = [routes[k : k + 1, :] for k in range(2)]
    expert_ids = lax.broadcasted_iota(jnp.int32, (experts, tokens), 0)
    hits = [(expert_ids == r).astype(F32) for r in routes]
    row = lax.broadcasted_iota(jnp.int32, (tokens, tokens), 0)
    col = lax.broadcasted_iota(jnp.int32, (tokens, tokens), 1)
    before = dot_nn((hits[0] + hits[1]).astype(BF16), (row < col).astype(F32).astype(BF16))
    slots, gates = [], []
    for k in range(2):
        rank = jnp.sum(before * hits[k], axis=0, keepdims=True)
        slots.append(routes[k] * stride + rank.astype(jnp.int32))
        gates.append(jnp.sum(jnp.where(row == col, gates_row[k : k + 1, :], 0.0), axis=1, keepdims=True))
    return slots, gates


def pack_info(routes, gates_row, width):
    blank = jnp.zeros((1, width - 2 * routes.shape[1]), F32)
    parts = []
    for k in range(2):
        rest = gates_row[k : k + 1, :]
        for _ in range(3):
            part = rest.astype(BF16).astype(F32)
            parts.append(part)
            rest = rest - part
    first = jnp.concatenate([routes[0:1, :].astype(F32), routes[1:2, :].astype(F32), blank], axis=1)
    second = jnp.concatenate(parts, axis=1)
    return jnp.concatenate([first, second, jnp.zeros((14, width), F32)], axis=0).astype(BF16)


def unpack_info(block, tokens):
    block = block.astype(F32)
    cut = lambda row, i: block[row : row + 1, i * tokens : (i + 1) * tokens]
    routes = jnp.concatenate([cut(0, 0), cut(0, 1)], axis=0).astype(jnp.int32)
    gates = [cut(1, 3 * k) + cut(1, 3 * k + 1) + cut(1, 3 * k + 2) for k in range(2)]
    return routes, jnp.concatenate(gates, axis=0)


def dispatch_body(experts, cap, far, *refs):
    stride = 2 * cap
    if far:
        packed_ref, out_ref = refs
        tokens = packed_ref.shape[0] // 2 - 8
        routes, gates_row = unpack_info(packed_ref[2 * tokens :, :], tokens)
        own = packed_ref[:tokens, :]
        cot = packed_ref[tokens : 2 * tokens, :]
    else:
        routes_ref, gates_ref, tokens_ref, cot_ref, *w_refs, out_ref, packed_ref, shard_ref = refs
        tokens, width = tokens_ref.shape
        routes, gates_row = routes_ref[...], gates_ref[...]
        own, cot = tokens_ref[...], cot_ref[...]
        part = w_refs[0].shape[1] // 2
        for half in range(2):
            for m, ref in enumerate(w_refs):
                to = (3 * half + m) * part
                shard_ref[to : to + part, :] = ref[0, half * part : (half + 1) * part, :]
        packed_ref[:tokens, :] = own
        packed_ref[tokens : 2 * tokens, :] = cot
        packed_ref[2 * tokens :, :] = pack_info(routes, gates_row, width)
    slots, gates = route_info(routes, gates_row, experts, stride)
    row_ids = lax.broadcasted_iota(jnp.int32, (experts * stride, tokens), 0)
    gated = [(cot.astype(F32) * gates[k]).astype(BF16) for k in range(2)]
    place_x = ((row_ids == slots[0]) | (row_ids == slots[1])).astype(F32).astype(BF16)
    place_g = [(row_ids == slots[k] + cap).astype(F32).astype(BF16) for k in range(2)]
    left = jnp.concatenate([place_x] + place_g, axis=1)
    right = jnp.concatenate([own] + gated, axis=0)
    out_ref[...] = dot_nn(left, right).astype(BF16)


def combine_body(experts, cap, far, *refs):
    stride = 2 * cap
    if far:
        packed_ref, rows_ref, both_ref = refs
        tokens = both_ref.shape[0] // 2
        routes, gates_row = unpack_info(packed_ref[2 * tokens :, :], tokens)
    else:
        routes_ref, gates_ref, rows_ref, share_ref, mixed_ref, grads_ref = refs
        tokens = mixed_ref.shape[0]
        routes, gates_row = routes_ref[...], gates_ref[...]
    slots, gates = route_info(routes, gates_row, experts, stride)
    row_ids = lax.broadcasted_iota(jnp.int32, (experts * stride, tokens), 0)
    rows = rows_ref[...]
    pick = [(row_ids == slots[k]).astype(F32).astype(BF16) for k in range(2)]
    pick_g = ((row_ids == slots[0] + cap) | (row_ids == slots[1] + cap)).astype(F32).astype(BF16)
    mixed = gates[0] * dot_tn(pick[0], rows) + gates[1] * dot_tn(pick[1], rows)
    grads = dot_tn(pick_g, rows)
    if far:
        both_ref[:tokens, :] = mixed.astype(BF16)
        both_ref[tokens:, :] = grads.astype(BF16)
    else:
        mixed_ref[...] = (mixed + share_ref[:tokens, :].astype(F32)).astype(BF16)
        grads_ref[...] = (grads + share_ref[tokens:, :].astype(F32)).astype(BF16)


def split_matrix(cap):
    size = GROUP * 2 * cap
    out = lax.broadcasted_iota(jnp.int32, (size, size), 0)
    src = lax.broadcasted_iota(jnp.int32, (size, size), 1)
    second = (out >= size // 2).astype(jnp.int32)
    inner = out - second * (size // 2)
    wanted = (inner // cap) * (2 * cap) + inner % cap + second * cap
    return (src == wanted).astype(F32).astype(BF16)


def lane_chunks(size):
    step = 256 if size % 256 == 0 else 384
    return [(at, min(at + step, size)) for at in range(0, size, step)]


def activations(x, g, w_gate, w_up, w_down):
    pre_gate = dot_nt(x, w_gate)
    pre_up = dot_nt(x, w_up)
    grad_hidden = dot_nt(g, w_down)
    sig = jax.nn.sigmoid(pre_gate)
    active = pre_gate * sig
    slope = sig * (1.0 + pre_gate * (1.0 - sig))
    return (
        (active * pre_up).astype(BF16),
        (grad_hidden * pre_up * slope).astype(BF16),
        (grad_hidden * active).astype(BF16),
    )


def piece_cuts(refs, part):
    cuts, to = [], 0
    for number, ref in enumerate(refs):
        for at in range(0, ref.shape[0], 3 * part):
            cuts += [(number, at + m * part, m, to) for m in range(3)]
            to += part
    return cuts


def rows_body(cap, part, raw, last, pieces, *refs):
    refs = list(refs)

    def take(number):
        taken = refs[:number]
        del refs[:number]
        return taken

    given = take(2 if raw else 4)
    w_refs = take(pieces)
    acts_out = take(3)
    kept_out = take(2) if raw else None
    results = take(2)
    loaded, w_all, acts = take(3)
    kept = take(1)[0] if raw else loaded
    sums = take(0 if raw else 2)
    load_sems, w_sems, sum_sems, acts_sems, kept_sems = take(5)
    loads = [start_copy(given[i], loaded.at[i], load_sems.at[i]) for i in range(2)]
    w_loads = []
    for index, (number, row, m, to) in enumerate(piece_cuts(w_refs, part)):
        src = w_refs[number].at[pl.ds(row, part), :]
        w_loads.append(start_copy(src, w_all.at[m, pl.ds(to, part), :], w_sems.at[index]))
    if not raw:
        sum_loads = [start_copy(given[2 + i], sums[i], sum_sems.at[i]) for i in range(2)]
    stores = []
    total = loaded.shape[1]
    half = total // 2
    block = GROUP * 2 * cap
    split = split_matrix(cap)
    for index in range(2):
        loads[index].wait()
        if raw:
            for at in range(0, total, block):
                parted = dot_nn(split, loaded[index, at : at + block, :]).astype(BF16)
                to = index * half + at // 2
                for i in range(2):
                    kept[i, to : to + block // 2, :] = parted[i * block // 2 : (i + 1) * block // 2]
    if raw:
        stores += [start_copy(kept.at[i], kept_out[i], kept_sems.at[i]) for i in range(2)]
    for copy in w_loads:
        copy.wait()
    for lo, hi in lane_chunks(w_all.shape[1]):
        values = activations(
            kept[0], kept[1], w_all[0, lo:hi, :], w_all[1, lo:hi, :], w_all[2, lo:hi, :]
        )
        for m in range(3):
            acts[m, :, lo:hi] = values[m]
    stores += [start_copy(acts.at[m], acts_out[m], acts_sems.at[m]) for m in range(3)]
    out = dot_nn(acts[0], w_all[2])
    grad_in = dot_nn(acts[1], w_all[0]) + dot_nn(acts[2], w_all[1])
    if not raw:
        for copy in sum_loads:
            copy.wait()
        out = out + sums[0][...]
        grad_in = grad_in + sums[1][...]
    if last:
        for index, ref in enumerate(results):
            for at in range(0, total, block):
                rows = slice(index * half + at // 2, index * half + (at + block) // 2)
                both = jnp.concatenate([out[rows, :], grad_in[rows, :]], axis=0).astype(BF16)
                ref[at : at + block, :] = dot_tn(split, both).astype(BF16)
    else:
        results[0][...] = out
        results[1][...] = grad_in
    for copy in stores:
        copy.wait()


def rows_call(cap, part, last, given, pieces, micros):
    raw = len(given) == 2
    total, width = given[0].shape
    count = len(pieces)
    size = sum(p.shape[0] for p in pieces) // 3
    row16 = jax.ShapeDtypeStruct((total, width), BF16)
    row32 = jax.ShapeDtypeStruct((total, width), F32)
    shapes = [jax.ShapeDtypeStruct((total, size), BF16)] * 3
    shapes += [row16] * (2 if raw else 0)
    shapes += [row16 if last else row32] * 2
    scratch = [pltpu.VMEM((2, total, width), BF16), pltpu.VMEM((3, size, width), BF16)]
    scratch += [pltpu.VMEM((3, total, size), BF16)]
    scratch += [pltpu.VMEM((2, total, width), BF16)] if raw else [pltpu.VMEM((total, width), F32)] * 2
    scratch += [pltpu.SemaphoreType.DMA((n,)) for n in (2, 6 * count, 2, 3, 2)]
    body = functools.partial(rows_body, cap, part, raw, last, count)
    operands = list(given) + list(pieces)
    results = kernel_call(body, shapes, micros, operands, scratch, True, 5 if raw else 3)
    return results[:3], results[3:-2], results[-2:]


def terms_body(part, pieces, *refs):
    rows_in, acts_in, t_out = refs[:4], refs[4:13], refs[13 : 13 + pieces]
    rows, near_a, near_b, far, t_all, row_sems, act_sems, t_sems = refs[13 + pieces :]
    size = far.shape[2]
    edge = near_a.shape[2]
    order = ((1, 0), (2, 0), (0, 1))
    row_loads, act_loads = {}, {}
    for m, (act, kind) in enumerate(order):
        if kind not in row_loads:
            row_loads[kind] = [
                start_copy(rows_in[2 * i + kind], rows.at[2 * i + kind], row_sems.at[2 * i + kind])
                for i in range(2)
            ]
        act_loads[m] = [
            start_copy(acts_in[3 * i + act], dst.at[act], act_sems.at[3 * i + act])
            for i, dst in enumerate((near_a, near_b, far))
        ]
    stores = []
    for m, (act, kind) in enumerate(order):
        for copy in row_loads.pop(kind, []) + act_loads[m]:
            copy.wait()
        for lo in range(0, size, 256):
            hi = min(lo + 256, size)
            parts = []
            if lo < edge:
                parts.append(dot_tn(near_a[act, :, lo : min(hi, edge)], rows[kind]))
            if hi > edge:
                parts.append(dot_tn(near_b[act, :, max(lo, edge) - edge : hi - edge], rows[kind]))
            near = parts[0] if len(parts) == 1 else jnp.concatenate(parts, axis=0)
            t_all[m, lo:hi, :] = (near + dot_tn(far[act, :, lo:hi], rows[2 + kind])).astype(BF16)
        for index, (number, row, which, at) in enumerate(piece_cuts(t_out, part)):
            if which == m:
                src = t_all.at[m, pl.ds(at, part), :]
                stores.append(start_copy(src, t_out[number].at[pl.ds(row, part), :], t_sems.at[index]))
    for copy in stores:
        copy.wait()


def terms_call(part, rows, acts, pieces, micros):
    total, width = rows[0].shape
    sizes = [a[0].shape[1] for a in acts]
    shapes = [jax.ShapeDtypeStruct(p.shape, BF16) for p in pieces]
    scratch = [pltpu.VMEM((4, total, width), BF16)]
    scratch += [pltpu.VMEM((3, total, n), BF16) for n in sizes]
    scratch += [pltpu.VMEM((3, sizes[2], width), BF16)]
    scratch += [pltpu.SemaphoreType.DMA((n,)) for n in (4, 9, 6 * len(pieces))]
    operands = list(rows) + [a for group in acts for a in group]
    body = functools.partial(terms_body, part, len(pieces))
    return kernel_call(body, shapes, micros, operands, scratch, True, len(pieces))


def final_body(scale, *refs):
    inputs, outputs = refs[:3], refs[3:]
    part = inputs[0].shape[0] // 6
    for half in range(2):
        for m in range(3):
            rows = slice((3 * half + m) * part, (3 * half + m + 1) * part)
            total = sum(ref[rows, :].astype(F32) for ref in inputs)
            outputs[m][0, half * part : (half + 1) * part, :] = total * scale


def rounded_sum(a, b):
    return (a.astype(F32) + b.astype(F32)).astype(BF16)


def per_device(tokens, routes, route_gates, cotangent, gate_weight, up_weight, down_weight):
    experts = lax.axis_size("expert")
    ring = lax.axis_size("z")
    tok_rows, width = tokens.shape
    choose = routes.shape[1]
    cap = tok_rows * choose * 5 // (4 * experts)
    rows = experts * 2 * cap
    hidden = gate_weight.shape[1]

    def along(value, step):
        return lax.ppermute(value, "z", [(i, (i + step) % ring) for i in range(ring)])

    def opposite(value):
        return along(value, ring // 2)

    def other_core(value):
        return lax.ppermute(value, "core", [(0, 1), (1, 0)])

    def exchange(value):
        moved = lax.all_to_all(
            value.reshape(experts, 2 * cap, width), "expert", split_axis=0, concat_axis=0, tiled=True
        )
        return moved.reshape(rows, width)

    def after(value, *others):
        return lax.optimization_barrier((value, *others))[0]

    def dispatch(micros, far, *given):
        sent = jax.ShapeDtypeStruct((rows, width), BF16)
        packed = jax.ShapeDtypeStruct((2 * tok_rows + 16, width), BF16)
        shard = jax.ShapeDtypeStruct((3 * hidden, width), BF16)
        body = functools.partial(dispatch_body, experts, cap, far)
        return kernel_call(body, [sent] if far else [sent, packed, shard], micros, given)

    def summed(outs):
        return rounded_sum(outs[0], other_core(outs[1]))

    def combine(micros, far, info, sums, share=()):
        returned = exchange(sums)
        one = jax.ShapeDtypeStruct((tok_rows, width), BF16)
        both = jax.ShapeDtypeStruct((2 * tok_rows, width), BF16)
        body = functools.partial(combine_body, experts, cap, far)
        return kernel_call(body, [both] if far else [one] * 2, micros, (*info, returned, *share))

    near_info = (routes.T, route_gates.T)
    near_sent, packed, own = dispatch(
        2.0, False, *near_info, tokens, cotangent, gate_weight, up_weight, down_weight
    )
    far_packed = opposite(packed)
    near = exchange(near_sent)

    part = hidden // 2
    left, right = along(own, 1), along(own, -1)
    far_left, far_right = along(left[: 3 * part], 1), along(right[3 * part :], -1)

    far_sent = dispatch(FAR_US, True, far_packed)[0]
    far = exchange(after(far_sent, near))
    near_swapped = other_core(after(near, far_sent, left))
    near_a, near_rows, near_sums = rows_call(cap, part, False, (near, near_swapped), [own, left], NEAR_US)
    far = after(far, near_sums[0], far_left, far_right)
    pieces = [own, left, right, far_left, far_right]
    far_acts, far_rows, far_outs = rows_call(cap, part, True, (far, other_core(far)), pieces, 10.0)
    near_sums = [after(a, far_outs[0]) for a in near_sums]
    far_outs = summed(far_outs)
    near_b, _, near_outs = rows_call(cap, part, True, (*near_rows, *near_sums), pieces[2:], 6.0)
    t_own, t_left, t_right, t_far_left, t_far_right = terms_call(
        part, (*near_rows, *far_rows), (near_a, [after(a, far_outs) for a in near_b], far_acts), pieces, 7.0
    )

    from_right = along(t_far_left, -1)
    from_left = along(t_far_right, 1)
    to_left = jnp.concatenate([rounded_sum(t_left[: 3 * part], from_right), t_left[3 * part :]])
    to_right = jnp.concatenate([t_right[: 3 * part], rounded_sum(t_right[3 * part :], from_left)])
    scale = float(tok_rows * choose * ring * CORES) ** (-0.5)
    grads = kernel_call(
        functools.partial(final_body, scale),
        [jax.ShapeDtypeStruct((1, hidden, width), F32)] * 3,
        2.0,
        (t_own, along(to_left, -1), along(to_right, 1)),
    )

    far_share = combine(MERGE_US, True, (far_packed,), far_outs)[0]
    near_outs = after(summed(near_outs), far_share)
    mixed, token_grads = combine(2.0, False, near_info, near_outs, (opposite(far_share),))
    return (mixed, token_grads, *grads)


def solution(mesh):
    data, experts = mesh.shape["dp"], mesh.shape["expert"]
    fine = Mesh(mesh.devices.reshape(data // CORES, CORES, experts), ("z", "core", "expert"))
    by_token = P(("z", "core", "expert"), None)
    by_weight = P("expert", ("z", "core"), None)
    return jax.shard_map(
        per_device,
        mesh=fine,
        in_specs=(by_token, by_token, by_token, by_token, by_weight, by_weight, by_weight),
        out_specs=(by_token, by_token, by_weight, by_weight, by_weight),
        check_vma=False,
    )
```

time: 358 us -> 176 us (0.49)
  the two profiles are of different devices: /device:TPU:1 before, /device:TPU:96 now
where the time goes in v1:
time: 176 us; the launch traced here: 175 us
  waiting for transfers between devices  69.9 us (40%)
  Pallas kernels  53.3 us (30%)
  starting transfers between devices  41.3 us (23%)
  local copies, waits for them, and re-layouts  6.24 us (4%)
  other arithmetic  3.62 us (2%)
    ppermute x10, waiting for transfers between devices, along(): lax.ppermute(value, 'z', [(i, (i + step) % ring) for i in range(ring)])  61.7 us
    pallas_call x9, Pallas kernels, kernel_call(): pl.pallas_call(body, out_shape=out_shapes, in_specs=in_hbm * len(operands...  53.3 us
    all_to_all x4, starting transfers between devices, exchange(): lax.all_to_all(value.reshape(experts, 2 * cap, width), 'expert', split_ax...  22.9 us
    ppermute x10, starting transfers between devices, along(): lax.ppermute(value, 'z', [(i, (i + step) % ring) for i in range(ring)])  17.4 us
    all_to_all x4, waiting for transfers between devices, exchange(): lax.all_to_all(value.reshape(experts, 2 * cap, width), 'expert', split_ax...  5.64 us
    unnamed x28, local copies, waits for them, and re-layouts  5.11 us
  transfers between devices with their start and end apart: 18, of which 11 were waited for; matrix products, arithmetic and copies ran while one was open for 3% of the time, Pallas kernels for 21%

profile of v1, /device:TPU:96, one launch (start us, length us, event | category | flops | bytes accessed | tf_op | source)
XLA Modules:
  0.0 175.3 jit_solution(4459789203399947660)
XLA Ops:
  0.6 3.5 %shard_map.110 = (bf16[640,768]{1,0:T(8,128)(2,1)}, bf16[272,768]{1,0:T(8,128)(2,1)}, bf16[576,768]{1,0:T(8,128)(2,1)}) custom-call(s32[2,128]{1,0:T(2,128)} %bitcast.18, f32[2,128]{1,0:T(2,128)} %bitcast.20, bf16[128,768]{1,0:T(8,128)(2,1)} %refs_2_.1, bf16[128,768]{1,0:T(8,128)(2,1)} %refs_3_.1, bf16[1,192,768]{2,1,0:T(8,128)(2,1)} %refs_4_.1, ...), custom_call_target="tpu_custom_call" | custom-call | flops 2300000000 | tf_op jit(solution)/shard_map/pallas_call | solution.py:39
  4.1 4.5 %collective-permute-start = (bf16[272,768]{1,0:T(8,128)(2,1)}, bf16[272,768]{1,0:T(8,128)(2,1)S(1)}, u32[]{:S(2)}, u32[]{:S(2)}) collective-permute-start(bf16[272,768]{1,0:T(8,128)(2,1)} %get-tuple-element.47), channel_id=1, source_target_pairs={{0,128},{32,160},{64,192},{96,224},{128,0},{160,32},{192,64},{224,... | collective-permute-start | bytes 1253384 | tf_op jit(solution)/shard_map/ppermute | solution.py:353
  8.6 7.0 %all-to-all-start = ((bf16[16,40,768]{2,1,0:T(8,128)(2,1)}), bf16[16,40,768]{2,1,0:T(8,128)(2,1)S(1)}, u32[]{:S(2)}, u32[]{:S(2)}) async-start(bf16[16,40,768]{2,1,0:T(8,128)(2,1)} %bitcast.17), calls=%async_computation | async-start | bytes 1966080 | tf_op jit(solution)/shard_map/all_to_all | solution.py:362
  15.6 0.1 collective-permute-start.1
  15.7 2.0 %collective-permute-start.4 = (bf16[576,768]{1,0:T(8,128)(2,1)}, bf16[576,768]{1,0:T(8,128)(2,1)S(1)}, u32[]{:S(2)}, u32[]{:S(2)}) collective-permute-start(bf16[576,768]{1,0:T(8,128)(2,1)} %get-tuple-element.48.refs_2_), channel_id=1, source_target_pairs={{0,224},{32,0},{64,32},{96,64},{128,96},{160,128},{192,160},{224,1... | collective-permute-start | bytes 2654216 | tf_op jit(solution)/shard_map/ppermute | solution.py:353
  17.7 9.2 %collective-permute-done.refs_0_ = bf16[272,768]{1,0:T(8,128)(2,1)S(1)} collective-permute-done((bf16[272,768]{1,0:T(8,128)(2,1)}, bf16[272,768]{1,0:T(8,128)(2,1)S(1)}, u32[]{:S(2)}, u32[]{:S(2)}) %collective-permute-start) | collective-permute-done | bytes 417824 | tf_op jit(solution)/shard_map/ppermute | solution.py:353
  26.9 0.8 copy-done.12
  27.7 2.8 %shard_map.111 = bf16[640,768]{1,0:T(8,128)(2,1)} custom-call(bf16[272,768]{1,0:T(8,128)(2,1)} %copy-done.12), custom_call_target="tpu_custom_call" | custom-call | flops 5750000128 | tf_op jit(solution)/shard_map/pallas_call | solution.py:39
  30.5 16.6 %collective-permute-done.1.refs_3_ = bf16[576,768]{1,0:T(8,128)(2,1)S(1)} collective-permute-done((bf16[576,768]{1,0:T(8,128)(2,1)}, bf16[576,768]{1,0:T(8,128)(2,1)S(1)}, u32[]{:S(2)}, u32[]{:S(2)}) %collective-permute-start.1) | collective-permute-done | bytes 884768 | tf_op jit(solution)/shard_map/ppermute | solution.py:353
  47.1 0.0 all-to-all-done
  47.1 0.1 collective-permute-start.2
  47.2 0.8 copy-done.9
  48.0 7.0 %all-to-all-start.1 = ((bf16[16,40,768]{2,1,0:T(8,128)(2,1)}), bf16[16,40,768]{2,1,0:T(8,128)(2,1)S(1)}, u32[]{:S(2)}, u32[]{:S(2)}) async-start(bf16[16,40,768]{2,1,0:T(8,128)(2,1)} %bitcast.15), calls=%async_computation.1 | async-start | bytes 1966080 | tf_op jit(solution)/shard_map/all_to_all | solution.py:362
  55.1 0.0 collective-permute-done.4.refs_4_
  55.1 0.0 copy-start.8
  55.1 0.8 collective-permute-start.5
  56.0 1.0 slice.24
  57.0 2.5 %collective-permute-start.3 = (bf16[288,768]{1,0:T(8,128)(2,1)S(1)}, bf16[288,768]{1,0:T(8,128)(2,1)}, u32[]{:S(2)}, u32[]{:S(2)}) collective-permute-start(bf16[288,768]{1,0:T(8,128)(2,1)S(1)} %slice.24), channel_id=1, source_target_pairs={{0,32},{32,64},{64,96},{96,128},{128,160},{160,192},{192,224},{224... | collective-permute-start | bytes 1327112 | tf_op jit(solution)/shard_map/ppermute | solution.py:353
  59.6 0.0 collective-permute-done.2.refs_1_
  59.6 0.0 copy-done.1
  59.6 7.9 %shard_map.112 = (bf16[640,384]{1,0:T(8,128)(2,1)}, bf16[640,384]{1,0:T(8,128)(2,1)}, bf16[640,384]{1,0:T(8,128)(2,1)}, bf16[640,768]{1,0:T(8,128)(2,1)}, bf16[6...) custom-call(bf16[640,768]{1,0:T(8,128)(2,1)} %bitcast.13, ...), custom_call_target="tpu_custom_call" | custom-call | flops 1150000000 | tf_op jit(solution)/shard_map/pallas_call | solution.py:39
  67.5 0.5 collective-permute-done.5.refs_6_
  68.0 0.7 collective-permute-done.3.refs_5_
  68.7 3.0 %all-to-all-done.1 = bf16[16,40,768]{2,1,0:T(8,128)(2,1)S(1)} async-done(((bf16[16,40,768]{2,1,0:T(8,128)(2,1)}), bf16[16,40,768]{2,1,0:T(8,128)(2,1)S(1)}, u32[]{:S(2)}, u32[]{:S(2)}) %all-to-all-start.1) | async-done | bytes 983072 | tf_op jit(solution)/shard_map/all_to_all | solution.py:362
  71.8 0.0 collective-permute-start.6
  71.8 2.6 %collective-permute-done.6.refs_1_ = bf16[640,768]{1,0:T(8,128)(2,1)S(1)} collective-permute-done((bf16[640,768]{1,0:T(8,128)(2,1)S(1)}, bf16[640,768]{1,0:T(8,128)(2,1)S(1)}, u32[]{:S(2)}, u32[]{:S(2)}) %collective-permute-start.6) | collective-permute-done | bytes 983072 | tf_op jit(solution)/shard_map/ppermute | solution.py:359
  74.3 0.0 copy-done
  74.4 1.0 copy-done.10
  75.4 11.1 %shard_map.113 = (bf16[640,768]{1,0:T(8,128)(2,1)}, bf16[640,768]{1,0:T(8,128)(2,1)}, bf16[640,768]{1,0:T(8,128)(2,1)}, bf16[640,768]{1,0:T(8,128)(2,1)}, bf16[6...) custom-call(bf16[640,768]{1,0:T(8,128)(2,1)} %bitcast.11, bf16[640,768]{1,0:T(8,128)(2,1)} %copy-done.10, ...), custom_call_target="tpu_custom_call" | custom-call | flops 11500000256 | tf_op jit(solution)/shard_map/pallas_call | solution.py:39
  86.5 0.2 collective-permute-start.8
  86.7 9.1 %shard_map.114 = (bf16[640,384]{1,0:T(8,128)(2,1)}, bf16[640,384]{1,0:T(8,128)(2,1)}, bf16[640,384]{1,0:T(8,128)(2,1)}, bf16[640,768]{1,0:T(8,128)(2,1)}, bf16[640,768]{1,0:T(8,128)(2,1)}) custom-call(bf16[640,768]{1,0:T(8,128)(2,1)} %get-tuple-element.50.refs_0_, bf16[640,768]{1,0:T(8,128)(2,1)} %get-tuple-element.51.refs_1_, ...), custom_call_target="tpu_custom_call" | custom-call | flops 6899999744 | tf_op jit(solution)/shard_map/pallas_call | solution.py:39
  95.8 0.7 collective-permute-start.7
  96.5 0.0 collective-permute-done.8
  96.5 1.2 add_convert_fusion
  97.7 10.2 %shard_map.117 = (bf16[576,768]{1,0:T(8,128)(2,1)}, bf16[576,768]{1,0:T(8,128)(2,1)}, bf16[576,768]{1,0:T(8,128)(2,1)}, bf16[288,768]{1,0:T(8,128)(2,1)}, bf16[288,768]{1,0:T(8,128)(2,1)}) custom-call(bf16[640,768]{1,0:T(8,128)(2,1)} %get-tuple-element.50.refs_0_, bf16[640,768]{1,0:T(8,128)(2,1)} %get-tuple-element.51.refs_1_, ...), custom_call_target="tpu_custom_call" | custom-call | flops 8049999872 | tf_op jit(solution)/shard_map/pallas_call | solution.py:39
  107.9 0.0 copy-start.2
  107.9 3.0 %collective-permute-start.12 = (bf16[288,768]{1,0:T(8,128)(2,1)}, bf16[288,768]{1,0:T(8,128)(2,1)S(1)}, u32[]{:S(2)}, u32[]{:S(2)}) collective-permute-start(bf16[288,768]{1,0:T(8,128)(2,1)} %get-tuple-element.83), channel_id=1, source_target_pairs={{0,32},{32,64},{64,96},{96,128},{128,160},{160,192},{192,224},{224... | collective-permute-start | bytes 1327112 | tf_op jit(solution)/shard_map/ppermute | solution.py:353
  110.9 4.5 %all-to-all-start.2 = ((bf16[16,40,768]{2,1,0:T(8,128)(2,1)}), bf16[16,40,768]{2,1,0:T(8,128)(2,1)S(1)}, u32[]{:S(2)}, u32[]{:S(2)}) async-start(bf16[16,40,768]{2,1,0:T(8,128)(2,1)} %bitcast.6), calls=%async_computation.2 | async-start | bytes 1966080 | tf_op jit(solution)/shard_map/all_to_all | solution.py:362
  115.5 0.1 collective-permute-start.10
  115.6 0.0 collective-permute-done.7
  115.6 0.0 copy-done.2
  115.6 1.2 add_convert_fusion.1
  116.8 0.4 copy-done.7
  117.3 3.7 %collective-permute-done.12 = bf16[288,768]{1,0:T(8,128)(2,1)S(1)} collective-permute-done((bf16[288,768]{1,0:T(8,128)(2,1)}, bf16[288,768]{1,0:T(8,128)(2,1)S(1)}, u32[]{:S(2)}, u32[]{:S(2)}) %collective-permute-start.12) | collective-permute-done | bytes 442400 | tf_op jit(solution)/shard_map/ppermute | solution.py:353
  121.0 0.1 add_convert_fusion.2
  121.1 0.1 pad_maximum_fusion.1
  121.2 3.7 %collective-permute-start.13 = (bf16[576,768]{1,0:T(8,128)(2,1)S(1)}, bf16[576,768]{1,0:T(8,128)(2,1)S(1)}, u32[]{:S(2)}, u32[]{:S(2)}) collective-permute-start(bf16[576,768]{1,0:T(8,128)(2,1)S(1)} %pad_maximum_fusion.1), channel_id=1, source_target_pairs={{0,32},{32,64},{64,96},{96,128},{128,160},{160,192},{192,224},{224... | collective-permute-start | bytes 2654216 | tf_op jit(solution)/shard_map/ppermute | solution.py:353
  124.8 3.8 %collective-permute-done.10 = bf16[288,768]{1,0:T(8,128)(2,1)S(1)} collective-permute-done((bf16[288,768]{1,0:T(8,128)(2,1)}, bf16[288,768]{1,0:T(8,128)(2,1)S(1)}, u32[]{:S(2)}, u32[]{:S(2)}) %collective-permute-start.10) | collective-permute-done | bytes 442400 | tf_op jit(solution)/shard_map/ppermute | solution.py:353
  128.6 0.1 add_convert_fusion.3
  128.7 1.0 pad_maximum_fusion
  129.7 0.0 collective-permute-start.11
  129.7 2.6 %all-to-all-done.2 = bf16[16,40,768]{2,1,0:T(8,128)(2,1)S(1)} async-done(((bf16[16,40,768]{2,1,0:T(8,128)(2,1)}), bf16[16,40,768]{2,1,0:T(8,128)(2,1)S(1)}, u32[]{:S(2)}, u32[]{:S(2)}) %all-to-all-start.2) | async-done | bytes 983072 | tf_op jit(solution)/shard_map/all_to_all | solution.py:362
  132.3 0.9 copy-done.3
  133.3 2.9 %shard_map.115 = bf16[256,768]{1,0:T(8,128)(2,1)} custom-call(bf16[272,768]{1,0:T(8,128)(2,1)} %copy-done.12, bf16[640,768]{1,0:T(8,128)(2,1)} %bitcast.14), custom_call_target="tpu_custom_call" | custom-call | flops 34500001792 | tf_op jit(solution)/shard_map/pallas_call | solution.py:39
  136.2 4.3 %all-to-all-start.3 = ((bf16[16,40,768]{2,1,0:T(8,128)(2,1)}), bf16[16,40,768]{2,1,0:T(8,128)(2,1)S(1)}, u32[]{:S(2)}, u32[]{:S(2)}) async-start(bf16[16,40,768]{2,1,0:T(8,128)(2,1)} %bitcast.8), calls=%async_computation.3 | async-start | bytes 1966080 | tf_op jit(solution)/shard_map/all_to_all | solution.py:362
  140.5 0.6 collective-permute-start.9
  141.2 11.5 %collective-permute-done.13.refs_2_ = bf16[576,768]{1,0:T(8,128)(2,1)S(1)} collective-permute-done((bf16[576,768]{1,0:T(8,128)(2,1)S(1)}, bf16[576,768]{1,0:T(8,128)(2,1)S(1)}, u32[]{:S(2)}, u32[]{:S(2)}) %collective-permute-start.13) | collective-permute-done | bytes 884768 | tf_op jit(solution)/shard_map/ppermute | solution.py:353
  152.7 15.6 %collective-permute-done.11.refs_1_ = bf16[576,768]{1,0:T(8,128)(2,1)} collective-permute-done((bf16[576,768]{1,0:T(8,128)(2,1)}, bf16[576,768]{1,0:T(8,128)(2,1)}, u32[]{:S(2)}, u32[]{:S(2)}) %collective-permute-start.11) | collective-permute-done | bytes 884768 | tf_op jit(solution)/shard_map/ppermute | solution.py:353
  168.3 3.0 %shard_map.118 = (f32[1,192,768]{2,1,0:T(8,128)}, f32[1,192,768]{2,1,0:T(8,128)}, f32[1,192,768]{2,1,0:T(8,128)}) custom-call(bf16[576,768]{1,0:T(8,128)(2,1)} %get-tuple-element.79.refs_0_, bf16[576,768]{1,0:T(8,128)(2,1)} %collective-permute-done.11.refs_1_, bf16[576,768]{1,0:T(8,128)(2,1)} %copy-done.11), custom_call_target="tpu_custom_call" | custom-call | flops 2300000000 | tf_op jit(solution)/shard_map/pallas_call | solution.py:39
  171.3 0.0 collective-permute-done.9.refs_3_
  171.3 0.0 all-to-all-done.3
  171.4 0.7 copy-done.13
  172.1 0.3 copy-done.4
  172.4 2.8 %shard_map.116 = (bf16[128,768]{1,0:T(8,128)(2,1)}, bf16[128,768]{1,0:T(8,128)(2,1)}) custom-call(s32[2,128]{1,0:T(2,128)} %bitcast.19, f32[2,128]{1,0:T(2,128)} %bitcast.21, bf16[640,768]{1,0:T(8,128)(2,1)} %bitcast.16, bf16[256,768]{1,0:T(8,128)(2,1)} %copy-done.13), custom_call_target="tpu_custom_call" | custom-call | flops 2300000000 | tf_op jit(solution)/shard_map/pallas_call | solution.py:39
  (19 shorter events, 0.1 us)
Async XLA Ops:
  4.1 22.8 %collective-permute-start = (bf16[272,768]{1,0:T(8,128)(2,1)}, bf16[272,768]{1,0:T(8,128)(2,1)S(1)}, u32[]{:S(2)}, u32[]{:S(2)}) collective-permute-start(bf16[272,768]{1,0:T(8,128)(2,1)} %get-tuple-element.47), channel_id=1, source_target_pairs={{0,128},{32,160},{64,192},{96,224},{128,0},{160,32},{192,64},{224,... | collective-permute-start | bytes 1253384 | tf_op jit(solution)/shard_map/ppermute | solution.py:353
  8.6 38.5 %all-to-all-start = ((bf16[16,40,768]{2,1,0:T(8,128)(2,1)}), bf16[16,40,768]{2,1,0:T(8,128)(2,1)S(1)}, u32[]{:S(2)}, u32[]{:S(2)}) async-start(bf16[16,40,768]{2,1,0:T(8,128)(2,1)} %bitcast.17), calls=%async_computation | async-start | bytes 1966080 | tf_op jit(solution)/shard_map/all_to_all | solution.py:362
  15.6 31.5 %collective-permute-start.1 = (bf16[576,768]{1,0:T(8,128)(2,1)}, bf16[576,768]{1,0:T(8,128)(2,1)S(1)}, u32[]{:S(2)}, u32[]{:S(2)}) collective-permute-start(bf16[576,768]{1,0:T(8,128)(2,1)} %get-tuple-element.48.refs_2_), channel_id=1, source_target_pairs={{0,32},{32,64},{64,96},{96,128},{128,160},{160,192},{192,224},{224... | collective-permute-start | bytes 2654216 | tf_op jit(solution)/shard_map/ppermute | solution.py:353
  15.7 39.4 %collective-permute-start.4 = (bf16[576,768]{1,0:T(8,128)(2,1)}, bf16[576,768]{1,0:T(8,128)(2,1)S(1)}, u32[]{:S(2)}, u32[]{:S(2)}) collective-permute-start(bf16[576,768]{1,0:T(8,128)(2,1)} %get-tuple-element.48.refs_2_), channel_id=1, source_target_pairs={{0,224},{32,0},{64,32},{96,64},{128,96},{160,128},{192,160},{224,1... | collective-permute-start | bytes 2654216 | tf_op jit(solution)/shard_map/ppermute | solution.py:353
  26.9 0.8 copy-start.12
  47.1 0.9 copy-start.9
  47.1 12.5 %copy-start.1 = (bf16[16,40,768]{2,1,0:T(8,128)(2,1)}, bf16[16,40,768]{2,1,0:T(8,128)(2,1)S(1)}, u32[]{:S(2)}) copy-start(bf16[16,40,768]{2,1,0:T(8,128)(2,1)S(1)} %all-to-all-done) | copy-start | bytes 2949124
  47.1 12.5 %collective-permute-start.2 = (bf16[640,768]{1,0:T(8,128)(2,1)S(1)}, bf16[640,768]{1,0:T(8,128)(2,1)}, u32[]{:S(2)}, u32[]{:S(2)}) collective-permute-start(bf16[640,768]{1,0:T(8,128)(2,1)S(1)} %bitcast.12), channel_id=1, source_target_pairs={{0,16},{16,0},{1,17},{17,1},{2,18},{18,2},{3,19},{19,3},{4,20},{20... | collective-permute-start | bytes 2949128 | tf_op jit(solution)/shard_map/ppermute | solution.py:359
  48.0 23.7 %all-to-all-start.1 = ((bf16[16,40,768]{2,1,0:T(8,128)(2,1)}), bf16[16,40,768]{2,1,0:T(8,128)(2,1)S(1)}, u32[]{:S(2)}, u32[]{:S(2)}) async-start(bf16[16,40,768]{2,1,0:T(8,128)(2,1)} %bitcast.15), calls=%async_computation.1 | async-start | bytes 1966080 | tf_op jit(solution)/shard_map/all_to_all | solution.py:362
  55.1 12.4 %copy-start.8 = (bf16[576,768]{1,0:T(8,128)(2,1)}, bf16[576,768]{1,0:T(8,128)(2,1)S(1)}, u32[]{:S(2)}) copy-start(bf16[576,768]{1,0:T(8,128)(2,1)S(1)} %collective-permute-done.4.refs_4_) | copy-start | bytes 2654212
  55.1 12.9 %collective-permute-start.5 = (bf16[288,768]{1,0:T(8,128)(2,1)S(1)}, bf16[288,768]{1,0:T(8,128)(2,1)}, u32[]{:S(2)}, u32[]{:S(2)}) collective-permute-start(bf16[288,768]{1,0:T(8,128)(2,1)S(1)} %slice.25), channel_id=1, source_target_pairs={{0,224},{32,0},{64,32},{96,64},{128,96},{160,128},{192,160},{224,1... | collective-permute-start | bytes 1327112 | tf_op jit(solution)/shard_map/ppermute | solution.py:353
  57.0 11.7 %collective-permute-start.3 = (bf16[288,768]{1,0:T(8,128)(2,1)S(1)}, bf16[288,768]{1,0:T(8,128)(2,1)}, u32[]{:S(2)}, u32[]{:S(2)}) collective-permute-start(bf16[288,768]{1,0:T(8,128)(2,1)S(1)} %slice.24), channel_id=1, source_target_pairs={{0,32},{32,64},{64,96},{96,128},{128,160},{160,192},{192,224},{224... | collective-permute-start | bytes 1327112 | tf_op jit(solution)/shard_map/ppermute | solution.py:353
  71.8 2.6 %copy-start = (bf16[16,40,768]{2,1,0:T(8,128)(2,1)}, bf16[16,40,768]{2,1,0:T(8,128)(2,1)S(1)}, u32[]{:S(2)}) copy-start(bf16[16,40,768]{2,1,0:T(8,128)(2,1)S(1)} %all-to-all-done.1) | copy-start | bytes 2949124
  71.8 2.6 %collective-permute-start.6 = (bf16[640,768]{1,0:T(8,128)(2,1)S(1)}, bf16[640,768]{1,0:T(8,128)(2,1)S(1)}, u32[]{:S(2)}, u32[]{:S(2)}) collective-permute-start(bf16[640,768]{1,0:T(8,128)(2,1)S(1)} %bitcast.10), channel_id=1, source_target_pairs={{0,16},{16,0},{1,17},{17,1},{2,18},{18,2},{3,19},{19,3},{4,20},{20... | collective-permute-start | bytes 2949128 | tf_op jit(solution)/shard_map/ppermute | solution.py:359
  74.3 1.0 copy-start.10
  86.5 10.0 %collective-permute-start.8 = (bf16[640,768]{1,0:T(8,128)(2,1)}, bf16[640,768]{1,0:T(8,128)(2,1)S(1)}, u32[]{:S(2)}, u32[]{:S(2)}) collective-permute-start(bf16[640,768]{1,0:T(8,128)(2,1)} %get-tuple-element.61), channel_id=1, source_target_pairs={{0,16},{16,0},{1,17},{17,1},{2,18},{18,2},{3,19},{19,3},{4,20},{20... | collective-permute-start | bytes 2949128 | tf_op jit(solution)/shard_map/ppermute | solution.py:359
  86.7 9.8 %copy-start.5 = (bf16[640,768]{1,0:T(8,128)(2,1)S(1)}, bf16[640,768]{1,0:T(8,128)(2,1)}, u32[]{:S(2)}) copy-start(bf16[640,768]{1,0:T(8,128)(2,1)} %get-tuple-element.55) | copy-start | bytes 2949124
  95.8 19.8 %collective-permute-start.7 = (bf16[640,768]{1,0:T(8,128)(2,1)}, bf16[640,768]{1,0:T(8,128)(2,1)S(1)}, u32[]{:S(2)}, u32[]{:S(2)}) collective-permute-start(bf16[640,768]{1,0:T(8,128)(2,1)} %get-tuple-element.60), channel_id=1, source_target_pairs={{0,16},{16,0},{1,17},{17,1},{2,18},{18,2},{3,19},{19,3},{4,20},{20... | collective-permute-start | bytes 2949128 | tf_op jit(solution)/shard_map/ppermute | solution.py:359
  107.9 7.7 %copy-start.2 = (bf16[640,768]{1,0:T(8,128)(2,1)S(1)}, bf16[640,768]{1,0:T(8,128)(2,1)}, u32[]{:S(2)}) copy-start(bf16[640,768]{1,0:T(8,128)(2,1)} %get-tuple-element.59) | copy-start | bytes 2949124
  107.9 13.1 %collective-permute-start.12 = (bf16[288,768]{1,0:T(8,128)(2,1)}, bf16[288,768]{1,0:T(8,128)(2,1)S(1)}, u32[]{:S(2)}, u32[]{:S(2)}) collective-permute-start(bf16[288,768]{1,0:T(8,128)(2,1)} %get-tuple-element.83), channel_id=1, source_target_pairs={{0,32},{32,64},{64,96},{96,128},{128,160},{160,192},{192,224},{224... | collective-permute-start | bytes 1327112 | tf_op jit(solution)/shard_map/ppermute | solution.py:353
  110.9 21.4 %all-to-all-start.2 = ((bf16[16,40,768]{2,1,0:T(8,128)(2,1)}), bf16[16,40,768]{2,1,0:T(8,128)(2,1)S(1)}, u32[]{:S(2)}, u32[]{:S(2)}) async-start(bf16[16,40,768]{2,1,0:T(8,128)(2,1)} %bitcast.6), calls=%async_computation.2 | async-start | bytes 1966080 | tf_op jit(solution)/shard_map/all_to_all | solution.py:362
  115.5 1.3 copy-start.6
  115.5 1.8 %copy-start.7 = (bf16[576,768]{1,0:T(8,128)(2,1)S(1)}, bf16[576,768]{1,0:T(8,128)(2,1)}, u32[]{:S(2)}) copy-start(bf16[576,768]{1,0:T(8,128)(2,1)} %get-tuple-element.82) | copy-start | bytes 2654212
  115.5 13.1 %collective-permute-start.10 = (bf16[288,768]{1,0:T(8,128)(2,1)}, bf16[288,768]{1,0:T(8,128)(2,1)S(1)}, u32[]{:S(2)}, u32[]{:S(2)}) collective-permute-start(bf16[288,768]{1,0:T(8,128)(2,1)} %get-tuple-element.81), channel_id=1, source_target_pairs={{0,224},{32,0},{64,32},{96,64},{128,96},{160,128},{192,160},{224,1... | collective-permute-start | bytes 1327112 | tf_op jit(solution)/shard_map/ppermute | solution.py:353
  121.2 31.5 %collective-permute-start.13 = (bf16[576,768]{1,0:T(8,128)(2,1)S(1)}, bf16[576,768]{1,0:T(8,128)(2,1)S(1)}, u32[]{:S(2)}, u32[]{:S(2)}) collective-permute-start(bf16[576,768]{1,0:T(8,128)(2,1)S(1)} %pad_maximum_fusion.1), channel_id=1, source_target_pairs={{0,32},{32,64},{64,96},{96,128},{128,160},{160,192},{192,224},{224... | collective-permute-start | bytes 2654216 | tf_op jit(solution)/shard_map/ppermute | solution.py:353
  129.7 38.6 %collective-permute-start.11 = (bf16[576,768]{1,0:T(8,128)(2,1)}, bf16[576,768]{1,0:T(8,128)(2,1)}, u32[]{:S(2)}, u32[]{:S(2)}) collective-permute-start(bf16[576,768]{1,0:T(8,128)(2,1)} %pad_maximum_fusion), channel_id=1, source_target_pairs={{0,224},{32,0},{64,32},{96,64},{128,96},{160,128},{192,160},{224,1... | collective-permute-start | bytes 2654216 | tf_op jit(solution)/shard_map/ppermute | solution.py:353
  132.3 0.9 copy-start.3
  136.2 35.1 %all-to-all-start.3 = ((bf16[16,40,768]{2,1,0:T(8,128)(2,1)}), bf16[16,40,768]{2,1,0:T(8,128)(2,1)S(1)}, u32[]{:S(2)}, u32[]{:S(2)}) async-start(bf16[16,40,768]{2,1,0:T(8,128)(2,1)} %bitcast.8), calls=%async_computation.3 | async-start | bytes 1966080 | tf_op jit(solution)/shard_map/all_to_all | solution.py:362
  140.5 30.8 %collective-permute-start.9 = (bf16[256,768]{1,0:T(8,128)(2,1)}, bf16[256,768]{1,0:T(8,128)(2,1)S(1)}, u32[]{:S(2)}, u32[]{:S(2)}) collective-permute-start(bf16[256,768]{1,0:T(8,128)(2,1)} %shard_map.115), channel_id=1, source_target_pairs={{0,128},{32,160},{64,192},{96,224},{128,0},{160,32},{192,64},{224,... | collective-permute-start | bytes 1179656 | tf_op jit(solution)/shard_map/ppermute | solution.py:353
  152.7 15.6 %copy-start.11 = (bf16[576,768]{1,0:T(8,128)(2,1)}, bf16[576,768]{1,0:T(8,128)(2,1)S(1)}, u32[]{:S(2)}) copy-start(bf16[576,768]{1,0:T(8,128)(2,1)S(1)} %collective-permute-done.13.refs_2_) | copy-start | bytes 2654212
  171.3 0.8 copy-start.13
  171.4 1.1 copy-start.4

commit v2 on v1

v2 whole, which is shorter than its diff:
```python
import functools

import jax
import jax.numpy as jnp
from jax import lax
from jax.experimental import pallas as pl
from jax.experimental.pallas import tpu as pltpu
from jax.sharding import Mesh, PartitionSpec as P

BF16 = jnp.bfloat16
F32 = jnp.float32
CORES = 2
GROUP = 4
ROW_STEP = 64
PEAK_PER_US = 1.15e9
FAR_US = 5.0
NEAR_US = 20.0
MERGE_US = 30.0
SHARE_US = 10.0
LATE_US = 8.0
EARLY_US = 8.0
VMEM_BYTES = 60 * 1024 * 1024


def dot_nn(a, b):
    return lax.dot_general(a, b, (((1,), (0,)), ((), ())), preferred_element_type=F32)


def dot_nt(a, b):
    return lax.dot_general(a, b, (((1,), (1,)), ((), ())), preferred_element_type=F32)


def dot_tn(a, b):
    return lax.dot_general(a, b, (((0,), (0,)), ((), ())), preferred_element_type=F32)


def whole(count):
    return [pl.BlockSpec(memory_space=pltpu.VMEM) for _ in range(count)]


def kernel_call(body, out_shapes, micros, operands, scratch=(), loads=0, stores=0):
    in_hbm = [pl.BlockSpec(memory_space=pltpu.HBM)]
    return pl.pallas_call(
        body,
        out_shape=out_shapes,
        in_specs=whole(len(operands) - loads) + in_hbm * loads,
        out_specs=in_hbm * stores + whole(len(out_shapes) - stores),
        scratch_shapes=list(scratch),
        compiler_params=pltpu.CompilerParams(vmem_limit_bytes=VMEM_BYTES),
        cost_estimate=pl.CostEstimate(
            flops=int(micros * PEAK_PER_US), bytes_accessed=0, transcendentals=0
        ),
    )(*operands)


def start_copy(src, dst, sem):
    copy = pltpu.make_async_copy(src, dst, sem)
    copy.start()
    return copy


def route_info(routes, gates_row, experts, stride):
    tokens = routes.shape[1]
    routes = [routes[k : k + 1, :] for k in range(2)]
    expert_ids = lax.broadcasted_iota(jnp.int32, (experts, tokens), 0)
    hits = [(expert_ids == r).astype(F32) for r in routes]
    row = lax.broadcasted_iota(jnp.int32, (tokens, tokens), 0)
    col = lax.broadcasted_iota(jnp.int32, (tokens, tokens), 1)
    before = dot_nn((hits[0] + hits[1]).astype(BF16), (row < col).astype(F32).astype(BF16))
    slots, gates = [], []
    for k in range(2):
        rank = jnp.sum(before * hits[k], axis=0, keepdims=True)
        slots.append(routes[k] * stride + rank.astype(jnp.int32))
        gates.append(jnp.sum(jnp.where(row == col, gates_row[k : k + 1, :], 0.0), axis=1, keepdims=True))
    return slots, gates


def pack_info(routes, gates_row, width):
    blank = jnp.zeros((1, width - 2 * routes.shape[1]), F32)
    parts = []
    for k in range(2):
        rest = gates_row[k : k + 1, :]
        for _ in range(3):
            part = rest.astype(BF16).astype(F32)
            parts.append(part)
            rest = rest - part
    first = jnp.concatenate([routes[0:1, :].astype(F32), routes[1:2, :].astype(F32), blank], axis=1)
    second = jnp.concatenate(parts, axis=1)
    return jnp.concatenate([first, second, jnp.zeros((14, width), F32)], axis=0).astype(BF16)


def unpack_info(block, tokens):
    block = block.astype(F32)
    cut = lambda row, i: block[row : row + 1, i * tokens : (i + 1) * tokens]
    routes = jnp.concatenate([cut(0, 0), cut(0, 1)], axis=0).astype(jnp.int32)
    gates = [cut(1, 3 * k) + cut(1, 3 * k + 1) + cut(1, 3 * k + 2) for k in range(2)]
    return routes, jnp.concatenate(gates, axis=0)


def dispatch_body(experts, cap, far, *refs):
    stride = 2 * cap
    if far:
        packed_ref, out_ref = refs
        tokens = packed_ref.shape[0] // 2 - 8
        routes, gates_row = unpack_info(packed_ref[2 * tokens :, :], tokens)
        own = packed_ref[:tokens, :]
        cot = packed_ref[tokens : 2 * tokens, :]
    else:
        routes_ref, gates_ref, tokens_ref, cot_ref, *w_refs, out_ref, packed_ref, first_ref, second_ref = refs
        tokens, width = tokens_ref.shape
        routes, gates_row = routes_ref[...], gates_ref[...]
        own, cot = tokens_ref[...], cot_ref[...]
        part = w_refs[0].shape[1] // 2
        for half, half_ref in enumerate((first_ref, second_ref)):
            for m, ref in enumerate(w_refs):
                rows = ref[0, half * part : (half + 1) * part, :]
                half_ref[m * part : (m + 1) * part, :] = rows
        packed_ref[:tokens, :] = own
        packed_ref[tokens : 2 * tokens, :] = cot
        packed_ref[2 * tokens :, :] = pack_info(routes, gates_row, width)
    slots, gates = route_info(routes, gates_row, experts, stride)
    row_ids = lax.broadcasted_iota(jnp.int32, (experts * stride, tokens), 0)
    gated = [(cot.astype(F32) * gates[k]).astype(BF16) for k in range(2)]
    place_x = ((row_ids == slots[0]) | (row_ids == slots[1])).astype(F32).astype(BF16)
    place_g = [(row_ids == slots[k] + cap).astype(F32).astype(BF16) for k in range(2)]
    left = jnp.concatenate([place_x] + place_g, axis=1)
    right = jnp.concatenate([own] + gated, axis=0)
    out_ref[...] = dot_nn(left, right).astype(BF16)


def combine_body(experts, cap, far, *refs):
    stride = 2 * cap
    if far:
        packed_ref, rows_ref, both_ref = refs
        tokens = both_ref.shape[0] // 2
        routes, gates_row = unpack_info(packed_ref[2 * tokens :, :], tokens)
    else:
        routes_ref, gates_ref, rows_ref, *share_refs, mixed_ref, grads_ref = refs
        tokens = mixed_ref.shape[0]
        routes, gates_row = routes_ref[...], gates_ref[...]
    slots, gates = route_info(routes, gates_row, experts, stride)
    row_ids = lax.broadcasted_iota(jnp.int32, (experts * stride, tokens), 0)
    rows = rows_ref[...]
    pick = [(row_ids == slots[k]).astype(F32).astype(BF16) for k in range(2)]
    pick_g = ((row_ids == slots[0] + cap) | (row_ids == slots[1] + cap)).astype(F32).astype(BF16)
    mixed = gates[0] * dot_tn(pick[0], rows) + gates[1] * dot_tn(pick[1], rows)
    grads = dot_tn(pick_g, rows)
    if far:
        both_ref[:tokens, :] = mixed.astype(BF16)
        both_ref[tokens:, :] = grads.astype(BF16)
    else:
        mixed_ref[...] = (mixed + share_refs[0][...]).astype(BF16)
        grads_ref[...] = (grads + share_refs[1][...]).astype(BF16)


def split_matrix(cap):
    size = GROUP * 2 * cap
    out = lax.broadcasted_iota(jnp.int32, (size, size), 0)
    src = lax.broadcasted_iota(jnp.int32, (size, size), 1)
    second = (out >= size // 2).astype(jnp.int32)
    inner = out - second * (size // 2)
    wanted = (inner // cap) * (2 * cap) + inner % cap + second * cap
    return (src == wanted).astype(F32).astype(BF16)


def lane_chunks(size):
    step = 256 if size % 256 == 0 else 384
    return [(at, min(at + step, size)) for at in range(0, size, step)]


def activations(x_ref, g_ref, w_all, acts, lo, hi):
    pre_gate = dot_nt(x_ref[...], w_all[0, lo:hi, :])
    pre_up = dot_nt(x_ref[...], w_all[1, lo:hi, :])
    grad_hidden = dot_nt(g_ref[...], w_all[2, lo:hi, :])
    for at in range(0, x_ref.shape[0], ROW_STEP):
        rows = slice(at, at + ROW_STEP)
        gate, up, grad = pre_gate[rows], pre_up[rows], grad_hidden[rows]
        sig = 0.5 * jnp.tanh(0.5 * gate) + 0.5
        active = gate * sig
        slope = sig + active * (1.0 - sig)
        acts[0, rows, lo:hi] = (active * up).astype(BF16)
        acts[1, rows, lo:hi] = (grad * up * slope).astype(BF16)
        acts[2, rows, lo:hi] = (grad * active).astype(BF16)


def piece_cuts(refs, part):
    cuts, to = [], 0
    for number, ref in enumerate(refs):
        for at in range(0, ref.shape[0], 3 * part):
            cuts += [(number, at + m * part, m, to) for m in range(3)]
            to += part
    return cuts


def merge_rows(cap, out, grad_in, results):
    split = split_matrix(cap)
    block = split.shape[0]
    half = out.shape[0] // 2
    for index, ref in enumerate(results):
        for at in range(0, 2 * half, block):
            rows = slice(index * half + at // 2, index * half + (at + block) // 2)
            both = jnp.concatenate([out[rows, :], grad_in[rows, :]], axis=0).astype(BF16)
            ref[at : at + block, :] = dot_tn(split, both).astype(BF16)


class Pending:
    def __init__(self):
        self.copies = {}

    def add(self, name, src, dst, sem):
        self.copies.setdefault(name, []).append(start_copy(src, dst, sem))

    def pieces(self, w_refs, part, w_all, w_sems, matrix):
        for index, (number, row, m, to) in enumerate(piece_cuts(w_refs, part)):
            if m == matrix:
                src = w_refs[number].at[pl.ds(row, part), :]
                self.add(m, src, w_all.at[m, pl.ds(to, part), :], w_sems.at[index])

    def __call__(self, *names):
        for name in names:
            for copy in self.copies.pop(name, ()):
                copy.wait()


def rows_body(cap, part, last, pieces, *refs):
    given, w_refs, refs = refs[:2], refs[2 : 2 + pieces], refs[2 + pieces :]
    acts_out, kept_out, results = refs[:3], refs[3:5], refs[5:7]
    loaded, w_all, acts, kept, load_sems, w_sems, acts_sems, kept_sems = refs[7:]
    ready = Pending()
    for i in range(2):
        ready.add(("rows", i), given[i], loaded.at[i], load_sems.at[i])
    for m in range(3):
        ready.pieces(w_refs, part, w_all, w_sems, m)
    total = loaded.shape[1]
    half = total // 2
    split = split_matrix(cap)
    block = split.shape[0]
    for index in range(2):
        ready(("rows", index))
        for at in range(0, total, block):
            parted = dot_nn(split, loaded[index, at : at + block, :]).astype(BF16)
            to = index * half + at // 2
            for i in range(2):
                kept[i, to : to + block // 2, :] = parted[i * block // 2 : (i + 1) * block // 2]
    for i in range(2):
        ready.add("out", kept.at[i], kept_out[i], kept_sems.at[i])
    ready(0, 1, 2)
    for lo, hi in lane_chunks(w_all.shape[1]):
        activations(kept.at[0], kept.at[1], w_all, acts, lo, hi)
    for m in range(3):
        ready.add("out", acts.at[m], acts_out[m], acts_sems.at[m])
    out = dot_nn(acts[0], w_all[2])
    grad_in = dot_nn(acts[1], w_all[0]) + dot_nn(acts[2], w_all[1])
    if last:
        merge_rows(cap, out, grad_in, results)
    else:
        results[0][...] = out.astype(BF16)
        results[1][...] = grad_in.astype(BF16)
    ready("out")


def rows_call(cap, part, last, given, pieces, micros):
    total, width = given[0].shape
    count = len(pieces)
    size = count * part
    row16 = jax.ShapeDtypeStruct((total, width), BF16)
    shapes = [jax.ShapeDtypeStruct((total, size), BF16)] * 3 + [row16] * 4
    scratch = [pltpu.VMEM((2, total, width), BF16), pltpu.VMEM((3, size, width), BF16)]
    scratch += [pltpu.VMEM((3, total, size), BF16), pltpu.VMEM((2, total, width), BF16)]
    scratch += [pltpu.SemaphoreType.DMA((n,)) for n in (2, 3 * count, 3, 2)]
    body = functools.partial(rows_body, cap, part, last, count)
    operands = list(given) + list(pieces)
    results = kernel_call(body, shapes, micros, operands, scratch, len(operands), 5)
    return results[:3], results[3:5], results[5:]


def term_group(part, near, far, rows, t_all, t_out, t_sems, ready):
    for m, (act, kind) in enumerate(((1, 0), (2, 0), (0, 1))):
        ready("xg"[kind], "xg"[kind] + "far", ("acts", act))
        for lo, hi in lane_chunks(near.shape[2]):
            term = dot_tn(near[act, :, lo:hi], rows[kind]) + dot_tn(far[act, :, lo:hi], rows[2 + kind])
            t_all[m, lo:hi, :] = term.astype(BF16)
        for index, (which, at, number, row) in enumerate(t_out.cuts):
            if which == m:
                src = t_all.at[m, pl.ds(at, part), :]
                ready.add("out", src, t_out.refs[number].at[pl.ds(row, part), :], t_sems.at[index])


class Outputs:
    def __init__(self, refs, order, part):
        self.refs = refs
        each = refs[0].shape[0] // (3 * part)
        self.cuts = [
            (m, unit * part, place // each, (place % each) * 3 * part + m * part)
            for place, unit in enumerate(order)
            for m in range(3)
        ]


def late_body(part, early, late, order, *refs):
    rows_in, acts_in, w_refs, refs = refs[:4], refs[4:7], refs[7 : 7 + late], refs[7 + late :]
    t_out, acts_out, refs = refs[:2], refs[2:5], refs[5:]
    rows, near, far, w_all, t_all, row_sems, far_sems, w_sems, t_sems, near_sems = refs
    size = near.shape[2]
    ready = Pending()
    ready.add("x", rows_in[0], rows.at[0], row_sems.at[0])
    ready.pieces(w_refs, part, w_all, w_sems, 0)
    ready.pieces(w_refs, part, w_all, w_sems, 1)
    ready.add("g", rows_in[1], rows.at[1], row_sems.at[1])
    ready.pieces(w_refs, part, w_all, w_sems, 2)
    for i, name in ((2, "xfar"), (3, "gfar")):
        ready.add(name, rows_in[i], rows.at[i], row_sems.at[i])
    for act in (1, 2, 0):
        src = acts_in[act].at[:, pl.ds(early * part, size)]
        ready.add(("acts", act), src, far.at[act], far_sems.at[act])
    ready("x", "g", 0, 1, 2)
    for lo, hi in lane_chunks(size):
        activations(rows.at[0], rows.at[1], w_all, near, lo, hi)
    for m in range(3):
        ready.add("out", near.at[m], acts_out[m], near_sems.at[m])
    ready("xfar", "gfar", ("acts", 0), ("acts", 1), ("acts", 2))
    term_group(part, near, far, rows, t_all, Outputs(t_out, order, part), t_sems, ready)
    ready("out")


def late_call(part, rows, acts, early, late, order, micros):
    total, width = rows[0].shape
    count = len(late)
    size = count * part
    row_acts = jax.ShapeDtypeStruct((total, size), BF16)
    shapes = [jax.ShapeDtypeStruct((3 * size // 2, width), BF16)] * 2 + [row_acts] * 3
    scratch = [
        pltpu.VMEM((4, total, width), BF16),
        pltpu.VMEM((3, total, size), BF16),
        pltpu.VMEM((3, total, size), BF16),
        pltpu.VMEM((3, size, width), BF16),
        pltpu.VMEM((3, size, width), BF16),
    ]
    scratch += [pltpu.SemaphoreType.DMA((n,)) for n in (4, 3, 3 * count, 3 * count, 3)]
    operands = [*rows, *acts, *late]
    body = functools.partial(late_body, part, len(early), count, order)
    results = kernel_call(body, shapes, micros, operands, scratch, len(operands), len(shapes))
    return results[:2], results[2:]


def early_body(cap, part, early, late, *refs):
    refs = list(refs)

    def take(number):
        taken = refs[:number]
        del refs[:number]
        return taken

    rows_in, sums_in, near_in, acts_in, more_in, w_refs = (take(n) for n in (4, 2, 3, 3, 3, late))
    t_out, results = take(early), take(2)
    rows, sums, near, far, more, w_all, t_all = take(7)
    row_sems, sum_sems, near_sems, far_sems, more_sems, w_sems, t_sems = refs
    size = near.shape[2]
    ready = Pending()
    for act, kind in ((1, 0), (2, None), (0, 1)):
        if kind is not None:
            for i, name in ((kind, "xg"[kind]), (2 + kind, "xg"[kind] + "far")):
                ready.add(name, rows_in[i], rows.at[i], row_sems.at[i])
        ready.add(("acts", act), near_in[act], near.at[act], near_sems.at[act])
        src = acts_in[act].at[:, pl.ds(0, size)]
        ready.add(("acts", act), src, far.at[act], far_sems.at[act])
    for act, m in ((0, 2), (1, 0), (2, 1)):
        ready.add("more", more_in[act], more.at[act], more_sems.at[act])
        ready.pieces(w_refs, part, w_all, w_sems, m)
    for i in range(2):
        ready.add("more", sums_in[i], sums.at[i], sum_sems.at[i])
    t_out = Outputs(t_out, range(early), part)
    term_group(part, near, far, rows, t_all, t_out, t_sems, ready)
    ready("more", 0, 1, 2)
    merge_rows(
        cap,
        sums[0].astype(F32) + dot_nn(more[0], w_all[2]),
        sums[1].astype(F32) + dot_nn(more[1], w_all[0]) + dot_nn(more[2], w_all[1]),
        results,
    )
    ready("out")


def early_call(cap, part, rows, sums, near, far, more, early, late, micros):
    total, width = rows[0].shape
    size = len(early) * part
    rest = len(late) * part
    row16 = jax.ShapeDtypeStruct((total, width), BF16)
    shapes = [jax.ShapeDtypeStruct(p.shape, BF16) for p in early] + [row16] * 2
    scratch = [
        pltpu.VMEM((4, total, width), BF16),
        pltpu.VMEM((2, total, width), BF16),
        pltpu.VMEM((3, total, size), BF16),
        pltpu.VMEM((3, total, size), BF16),
        pltpu.VMEM((3, total, rest), BF16),
        pltpu.VMEM((3, rest, width), BF16),
        pltpu.VMEM((3, size, width), BF16),
    ]
    scratch += [
        pltpu.SemaphoreType.DMA((n,)) for n in (4, 2, 3, 3, 3, 3 * len(late), 3 * len(early))
    ]
    operands = [*rows, *sums, *near, *far, *more, *late]
    body = functools.partial(early_body, cap, part, len(early), len(late))
    results = kernel_call(body, shapes, micros, operands, scratch, len(operands), len(early))
    return results[: len(early)], results[len(early) :]


def widen_body(given_ref, mixed_ref, grads_ref):
    tokens = mixed_ref.shape[0]
    mixed_ref[...] = given_ref[:tokens, :].astype(F32)
    grads_ref[...] = given_ref[tokens:, :].astype(F32)


def final_body(scale, *refs):
    first, second, left, right, more_left, more_right, *outputs = refs
    part = first.shape[0] // 3
    groups = ((first, 0), (left, 0), (more_right, 3)), ((second, 0), (right, 0), (more_left, 3))
    for half, group in enumerate(groups):
        for m in range(3):
            total = sum(
                ref[(at + m) * part : (at + m + 1) * part, :].astype(F32) for ref, at in group
            )
            outputs[m][0, half * part : (half + 1) * part, :] = total * scale


def rounded_sum(a, b):
    return (a.astype(F32) + b.astype(F32)).astype(BF16)


def per_device(tokens, routes, route_gates, cotangent, gate_weight, up_weight, down_weight):
    experts = lax.axis_size("expert")
    ring = lax.axis_size("z")
    tok_rows, width = tokens.shape
    choose = routes.shape[1]
    cap = tok_rows * choose * 5 // (4 * experts)
    rows = experts * 2 * cap
    hidden = gate_weight.shape[1]
    part = hidden // 2

    def along(value, step):
        return lax.ppermute(value, "z", [(i, (i + step) % ring) for i in range(ring)])

    def opposite(value):
        return along(value, ring // 2)

    def other_core(value):
        return lax.ppermute(value, "core", [(0, 1), (1, 0)])

    def exchange(value):
        moved = lax.all_to_all(
            value.reshape(experts, 2 * cap, width), "expert", split_axis=0, concat_axis=0, tiled=True
        )
        return moved.reshape(rows, width)

    def after(value, *others):
        return lax.optimization_barrier((value, *others))[0]

    def dispatch(micros, far, *given):
        sent = jax.ShapeDtypeStruct((rows, width), BF16)
        packed = jax.ShapeDtypeStruct((2 * tok_rows + 16, width), BF16)
        shard = jax.ShapeDtypeStruct((3 * part, width), BF16)
        body = functools.partial(dispatch_body, experts, cap, far)
        return kernel_call(body, [sent] if far else [sent, packed, shard, shard], micros, given)

    def summed(outs):
        return rounded_sum(outs[0], other_core(outs[1]))

    def combine(micros, far, info, returned, share=()):
        one = jax.ShapeDtypeStruct((tok_rows, width), BF16)
        both = jax.ShapeDtypeStruct((2 * tok_rows, width), BF16)
        body = functools.partial(combine_body, experts, cap, far)
        return kernel_call(body, [both] if far else [one] * 2, micros, (*info, returned, *share))

    near_info = (routes.T, route_gates.T)
    near_sent, packed, first, second = dispatch(
        2.0, False, *near_info, tokens, cotangent, gate_weight, up_weight, down_weight
    )
    far_packed = opposite(packed)
    near = exchange(near_sent)

    left_first, right_second = along(first, 1), along(second, -1)
    far_sent = dispatch(FAR_US, True, far_packed)[0]
    far = exchange(after(far_sent, near, left_first, right_second))
    left_second, right_first = along(second, 1), along(first, -1)
    far_first, far_second = along(left_first, 1), along(right_second, -1)
    early = [first, second, left_first, right_second]
    late = [left_second, right_first, far_first, far_second]

    near_swapped = other_core(after(near, far_sent, left_first, right_second))
    near_a, near_rows, near_sums = rows_call(cap, part, False, (near, near_swapped), early, NEAR_US)
    far = after(far, near_sums[0], *late)
    far_acts, far_rows, far_outs = rows_call(cap, part, True, (far, other_core(far)), early + late, 10.0)
    both_rows = (*near_rows, *far_rows)
    (go_left, go_right), near_b = late_call(
        part, both_rows, far_acts, early, late, (2, 0, 3, 1), LATE_US
    )
    far_outs = summed((after(far_outs[0], near_b[0]), far_outs[1]))
    near_sums = [after(a, far_outs) for a in near_sums]
    early_terms, near_outs = early_call(
        cap, part, both_rows, near_sums, near_a, far_acts, near_b, early, late, EARLY_US
    )
    t_first, t_second, t_left_first, t_right_second = early_terms

    far_share = combine(MERGE_US, True, (far_packed,), exchange(far_outs))[0]
    near_sum = after(summed(near_outs), far_share)
    returned = exchange(near_sum)

    back_first, back_second = along(go_left, -1), along(go_right, 1)
    half = 3 * part
    to_left = along(rounded_sum(t_left_first, back_first[:half]), -1)
    to_right = along(rounded_sum(after(t_right_second, near_sum), back_second[:half]), 1)

    scale = float(tok_rows * choose * ring * CORES) ** (-0.5)
    grads = kernel_call(
        functools.partial(final_body, scale),
        [jax.ShapeDtypeStruct((1, hidden, width), F32)] * 3,
        2.0,
        (after(t_first, returned), t_second, to_left, to_right, back_first, back_second),
    )
    share = kernel_call(
        widen_body, [jax.ShapeDtypeStruct((tok_rows, width), F32)] * 2, SHARE_US, (opposite(far_share),)
    )
    mixed, token_grads = combine(2.0, False, near_info, returned, share)
    return (mixed, token_grads, *grads)


def solution(mesh):
    data, experts = mesh.shape["dp"], mesh.shape["expert"]
    fine = Mesh(mesh.devices.reshape(data // CORES, CORES, experts), ("z", "core", "expert"))
    by_token = P(("z", "core", "expert"), None)
    by_weight = P("expert", ("z", "core"), None)
    return jax.shard_map(
        per_device,
        mesh=fine,
        in_specs=(by_token, by_token, by_token, by_token, by_weight, by_weight, by_weight),
        out_specs=(by_token, by_token, by_weight, by_weight, by_weight),
        check_vma=False,
    )
```

time: 176 us -> 160 us (0.909)
  the two profiles are of different devices: /device:TPU:96 before, /device:TPU:1 now
where the time goes in v2:
time: 160 us; the launch traced here: 159 us
  Pallas kernels  55.8 us (35%)
  starting transfers between devices  48.5 us (30%)
  waiting for transfers between devices  43.5 us (27%)
  local copies, waits for them, and re-layouts  5.49 us (3%)
  other arithmetic  4.89 us (3%)
    pallas_call x10, Pallas kernels, kernel_call(): pl.pallas_call(body, out_shape=out_shapes, in_specs=whole(len(operands) -...  55.8 us
    ppermute x12, waiting for transfers between devices, along(): lax.ppermute(value, 'z', [(i, (i + step) % ring) for i in range(ring)])  39.2 us
    ppermute x12, starting transfers between devices, along(): lax.ppermute(value, 'z', [(i, (i + step) % ring) for i in range(ring)])  21.4 us
    all_to_all x4, starting transfers between devices, exchange(): lax.all_to_all(value.reshape(experts, 2 * cap, width), 'expert', split_ax...  21.1 us
    ppermute x4, starting transfers between devices, other_core(): return lax.ppermute(value, 'core', [(0, 1), (1, 0)])  5.97 us
    unnamed x26, local copies, waits for them, and re-layouts  5.49 us
    convert_element_type x4, other arithmetic, rounded_sum(): return (a.astype(F32) + b.astype(F32)).astype(BF16)  4.89 us
  transfers between devices with their start and end apart: 20, of which 9 were waited for; matrix products, arithmetic and copies ran while one was open for 3% of the time, Pallas kernels for 24%

profile of v2, /device:TPU:1, one launch (start us, length us, event | category | flops | bytes accessed | tf_op | source)
XLA Modules:
  0.0 159.1 jit_solution(1295512358582883341)
XLA Ops:
  0.6 3.5 %shard_map.110 = (bf16[640,768]{1,0:T(8,128)(2,1)}, bf16[272,768]{1,0:T(8,128)(2,1)}, bf16[288,768]{1,0:T(8,128)(2,1)}, bf16[288,768]{1,0:T(8,128)(2,1)}) custom-call(s32[2,128]{1,0:T(2,128)} %bitcast.18, f32[2,128]{1,0:T(2,128)} %bitcast.20, bf16[128,768]{1,0:T(8,128)(2,1)} %refs_2_.1, bf16[128,768]{1,0:T(8,128)(2,1)} %refs_3_.1, ...), custom_call_target="tpu_custom_call" | custom-call | flops 2300000000 | tf_op jit(solution)/shard_map/pallas_call | solution.py:43
  4.1 7.7 %collective-permute-start = (bf16[272,768]{1,0:T(8,128)(2,1)}, bf16[272,768]{1,0:T(8,128)(2,1)S(1)}, u32[]{:S(2)}, u32[]{:S(2)}) collective-permute-start(bf16[272,768]{1,0:T(8,128)(2,1)} %get-tuple-element.51), channel_id=1, source_target_pairs={{0,128},{32,160},{64,192},{96,224},{128,0},{160,32},{192,64},{224,... | collective-permute-start | bytes 1253384 | tf_op jit(solution)/shard_map/ppermute | solution.py:441
  11.8 6.8 %all-to-all-start = ((bf16[16,40,768]{2,1,0:T(8,128)(2,1)}), bf16[16,40,768]{2,1,0:T(8,128)(2,1)S(1)}, u32[]{:S(2)}, u32[]{:S(2)}) async-start(bf16[16,40,768]{2,1,0:T(8,128)(2,1)} %bitcast.16), calls=%async_computation | async-start | bytes 1966080 | tf_op jit(solution)/shard_map/all_to_all | solution.py:450
  18.6 0.8 collective-permute-start.1
  19.4 1.9 %collective-permute-start.2 = (bf16[288,768]{1,0:T(8,128)(2,1)}, bf16[288,768]{1,0:T(8,128)(2,1)}, u32[]{:S(2)}, u32[]{:S(2)}) collective-permute-start(bf16[288,768]{1,0:T(8,128)(2,1)} %get-tuple-element.53.refs_3_), channel_id=1, source_target_pairs={{0,224},{32,0},{64,32},{96,64},{128,96},{160,128},{192,160},{224,1... | collective-permute-start | bytes 1327112 | tf_op jit(solution)/shard_map/ppermute | solution.py:441
  21.4 0.5 collective-permute-done.refs_0_
  21.9 0.8 copy-done.12
  22.7 2.8 %shard_map.111 = bf16[640,768]{1,0:T(8,128)(2,1)} custom-call(bf16[272,768]{1,0:T(8,128)(2,1)} %copy-done.12), custom_call_target="tpu_custom_call" | custom-call | flops 5750000128 | tf_op jit(solution)/shard_map/pallas_call | solution.py:43
  25.5 14.6 %collective-permute-done.1.refs_4_ = bf16[288,768]{1,0:T(8,128)(2,1)} collective-permute-done((bf16[288,768]{1,0:T(8,128)(2,1)}, bf16[288,768]{1,0:T(8,128)(2,1)}, u32[]{:S(2)}, u32[]{:S(2)}) %collective-permute-start.1) | collective-permute-done | bytes 442400 | tf_op jit(solution)/shard_map/ppermute | solution.py:441
  40.1 0.4 collective-permute-done.2.refs_5_
  40.4 0.0 all-to-all-done
  40.4 1.5 collective-permute-start.3
  42.0 2.4 %collective-permute-start.5 = (bf16[288,768]{1,0:T(8,128)(2,1)}, bf16[288,768]{1,0:T(8,128)(2,1)S(1)}, u32[]{:S(2)}, u32[]{:S(2)}) collective-permute-start(bf16[288,768]{1,0:T(8,128)(2,1)} %get-tuple-element.52.refs_2_), channel_id=1, source_target_pairs={{0,224},{32,0},{64,32},{96,64},{128,96},{160,128},{192,160},{224,1... | collective-permute-start | bytes 1327112 | tf_op jit(solution)/shard_map/ppermute | solution.py:441
  44.3 0.0 collective-permute-start.4
  44.3 0.0 collective-permute-start.6
  44.3 2.7 %collective-permute-start.7 = (bf16[288,768]{1,0:T(8,128)(2,1)}, bf16[288,768]{1,0:T(8,128)(2,1)}, u32[]{:S(2)}, u32[]{:S(2)}) collective-permute-start(bf16[288,768]{1,0:T(8,128)(2,1)} %collective-permute-done.2.refs_5_), channel_id=1, source_target_pairs={{0,224},{32,0},{64,32},{96,64},{128,96},{160,128},{192,160},{224,1... | collective-permute-start | bytes 1327112 | tf_op jit(solution)/shard_map/ppermute | solution.py:441
  47.0 0.0 copy-done
  47.0 6.8 %all-to-all-start.1 = ((bf16[16,40,768]{2,1,0:T(8,128)(2,1)}), bf16[16,40,768]{2,1,0:T(8,128)(2,1)S(1)}, u32[]{:S(2)}, u32[]{:S(2)}) async-start(bf16[16,40,768]{2,1,0:T(8,128)(2,1)} %bitcast.12), calls=%async_computation.1 | async-start | bytes 1966080 | tf_op jit(solution)/shard_map/all_to_all | solution.py:450
  53.8 0.0 collective-permute-done.3.refs_1_
  53.8 0.0 copy-start.8
  53.8 1.0 copy-done.8
  54.8 7.3 %shard_map.112 = (bf16[640,384]{1,0:T(8,128)(2,1)}, bf16[640,384]{1,0:T(8,128)(2,1)}, bf16[640,384]{1,0:T(8,128)(2,1)}, bf16[640,768]{1,0:T(8,128)(2,1)}, bf16[6...) custom-call(bf16[640,768]{1,0:T(8,128)(2,1)} %bitcast.11, bf16[640,768]{1,0:T(8,128)(2,1)} %copy-done.8, ...), custom_call_target="tpu_custom_call" | custom-call | flops 23000000512 | tf_op jit(solution)/shard_map/pallas_call | solution.py:43
  62.1 0.0 collective-permute-done.5.refs_7_.refs_8_.refs_16_
  62.1 0.0 copy-start.10
  62.1 0.0 collective-permute-done.4.refs_6_.refs_7_.refs_15_
  62.1 4.6 %collective-permute-done.6.refs_8_.refs_9_.refs_17_ = bf16[288,768]{1,0:T(8,128)(2,1)} collective-permute-done((bf16[288,768]{1,0:T(8,128)(2,1)}, bf16[288,768]{1,0:T(8,128)(2,1)}, u32[]{:S(2)}, u32[]{:S(2)}) %collective-permute-start.6) | collective-permute-done | bytes 442400 | tf_op jit(solution)/shard_map/ppermute | solution.py:441
  66.7 0.0 collective-permute-done.7.refs_9_.refs_10_.refs_18_
  66.8 2.1 %all-to-all-done.1 = bf16[16,40,768]{2,1,0:T(8,128)(2,1)S(1)} async-done(((bf16[16,40,768]{2,1,0:T(8,128)(2,1)}), bf16[16,40,768]{2,1,0:T(8,128)(2,1)S(1)}, u32[]{:S(2)}, u32[]{:S(2)}) %all-to-all-start.1) | async-done | bytes 983072 | tf_op jit(solution)/shard_map/all_to_all | solution.py:450
  68.8 2.7 %collective-permute-start.8 = (bf16[640,768]{1,0:T(8,128)(2,1)S(1)}, bf16[640,768]{1,0:T(8,128)(2,1)S(1)}, u32[]{:S(2)}, u32[]{:S(2)}) collective-permute-start(bf16[640,768]{1,0:T(8,128)(2,1)S(1)} %bitcast.13), channel_id=1, source_target_pairs={{0,16},{16,0},{1,17},{17,1},{2,18},{18,2},{3,19},{19,3},{4,20},{20... | collective-permute-start | bytes 2949128 | tf_op jit(solution)/shard_map/ppermute | solution.py:447
  71.6 2.2 %collective-permute-done.8.refs_1_ = bf16[640,768]{1,0:T(8,128)(2,1)S(1)} collective-permute-done((bf16[640,768]{1,0:T(8,128)(2,1)S(1)}, bf16[640,768]{1,0:T(8,128)(2,1)S(1)}, u32[]{:S(2)}, u32[]{:S(2)}) %collective-permute-start.8) | collective-permute-done | bytes 983072 | tf_op jit(solution)/shard_map/ppermute | solution.py:447
  73.8 0.0 copy-done.10
  73.8 1.0 copy-done.9
  74.8 11.0 %shard_map.113 = (bf16[640,768]{1,0:T(8,128)(2,1)}, bf16[640,768]{1,0:T(8,128)(2,1)}, bf16[640,768]{1,0:T(8,128)(2,1)}, bf16[640,768]{1,0:T(8,128)(2,1)}, bf16[6...) custom-call(bf16[640,768]{1,0:T(8,128)(2,1)} %bitcast.14, bf16[640,768]{1,0:T(8,128)(2,1)} %copy-done.9, ...), custom_call_target="tpu_custom_call" | custom-call | flops 11500000256 | tf_op jit(solution)/shard_map/pallas_call | solution.py:43
  85.8 0.5 collective-permute-start.9
  86.2 9.1 %shard_map.114 = (bf16[576,768]{1,0:T(8,128)(2,1)}, bf16[576,768]{1,0:T(8,128)(2,1)}, bf16[640,384]{1,0:T(8,128)(2,1)}, bf16[640,384]{1,0:T(8,128)(2,1)}, bf16[640,384]{1,0:T(8,128)(2,1)}) custom-call(bf16[640,768]{1,0:T(8,128)(2,1)} %get-tuple-element.55.refs_0_, bf16[640,768]{1,0:T(8,128)(2,1)} %get-tuple-element.56.refs_1_, ...), custom_call_target="tpu_custom_call" | custom-call | flops 9200000000 | tf_op jit(solution)/shard_map/pallas_call | solution.py:43
  95.4 1.4 collective-permute-start.12
  96.8 0.2 collective-permute-start.14
  96.9 0.0 collective-permute-done.9
  97.0 1.2 add_convert_fusion.1
  98.1 3.9 %all-to-all-start.2 = ((bf16[16,40,768]{2,1,0:T(8,128)(2,1)}), bf16[16,40,768]{2,1,0:T(8,128)(2,1)S(1)}, u32[]{:S(2)}, u32[]{:S(2)}) async-start(bf16[16,40,768]{2,1,0:T(8,128)(2,1)} %bitcast.6), calls=%async_computation.2 | async-start | bytes 1966080 | tf_op jit(solution)/shard_map/all_to_all | solution.py:450
  102.0 11.0 %shard_map.115 = (bf16[288,768]{1,0:T(8,128)(2,1)}, bf16[288,768]{1,0:T(8,128)(2,1)}, bf16[288,768]{1,0:T(8,128)(2,1)}, bf16[288,768]{1,0:T(8,128)(2,1)}, bf16[6...) custom-call(bf16[640,768]{1,0:T(8,128)(2,1)} %get-tuple-element.55.refs_0_, bf16[640,768]{1,0:T(8,128)(2,1)} %get-tuple-element.56.refs_1_, ...), custom_call_target="tpu_custom_call" | custom-call | flops 9200000000 | tf_op jit(solution)/shard_map/pallas_call | solution.py:43
  113.0 3.9 %collective-permute-done.12.refs_4_ = bf16[576,768]{1,0:T(8,128)(2,1)S(1)} collective-permute-done((bf16[576,768]{1,0:T(8,128)(2,1)}, bf16[576,768]{1,0:T(8,128)(2,1)S(1)}, u32[]{:S(2)}, u32[]{:S(2)}) %collective-permute-start.12) | collective-permute-done | bytes 884768 | tf_op jit(solution)/shard_map/ppermute | solution.py:441
  116.9 1.4 add_convert_fusion.3
  118.3 2.5 %collective-permute-start.13 = (bf16[288,768]{1,0:T(8,128)(2,1)S(1)}, bf16[288,768]{1,0:T(8,128)(2,1)}, u32[]{:S(2)}, u32[]{:S(2)}) collective-permute-start(bf16[288,768]{1,0:T(8,128)(2,1)S(1)} %add_convert_fusion.3), channel_id=1, source_target_pairs={{0,224},{32,0},{64,32},{96,64},{128,96},{160,128},{192,160},{224,1... | collective-permute-start | bytes 1327112 | tf_op jit(solution)/shard_map/ppermute | solution.py:441
  120.8 1.3 collective-permute-start.10
  122.0 0.0 all-to-all-done.2
  122.0 1.0 copy-done.3
  123.0 3.0 %shard_map.116 = bf16[256,768]{1,0:T(8,128)(2,1)} custom-call(bf16[272,768]{1,0:T(8,128)(2,1)} %copy-done.12, bf16[640,768]{1,0:T(8,128)(2,1)} %bitcast.15), custom_call_target="tpu_custom_call" | custom-call | flops 34500001792 | tf_op jit(solution)/shard_map/pallas_call | solution.py:43
  126.0 1.8 %collective-permute-start.11 = (bf16[256,768]{1,0:T(8,128)(2,1)}, bf16[256,768]{1,0:T(8,128)(2,1)}, u32[]{:S(2)}, u32[]{:S(2)}) collective-permute-start(bf16[256,768]{1,0:T(8,128)(2,1)} %shard_map.116), channel_id=1, source_target_pairs={{0,128},{32,160},{64,192},{96,224},{128,0},{160,32},{192,64},{224,... | collective-permute-start | bytes 1179656 | tf_op jit(solution)/shard_map/ppermute | solution.py:441
  127.7 0.0 collective-permute-done.10
  127.7 1.2 add_convert_fusion
  128.9 3.8 %all-to-all-start.3 = ((bf16[16,40,768]{2,1,0:T(8,128)(2,1)}), bf16[16,40,768]{2,1,0:T(8,128)(2,1)S(1)}, u32[]{:S(2)}, u32[]{:S(2)}) async-start(bf16[16,40,768]{2,1,0:T(8,128)(2,1)} %bitcast.8), calls=%async_computation.3 | async-start | bytes 1966080 | tf_op jit(solution)/shard_map/all_to_all | solution.py:450
  132.7 0.0 collective-permute-done.14.refs_5_
  132.7 1.1 add_convert_fusion.2
  133.9 0.1 collective-permute-start.15
  134.0 14.3 %collective-permute-done.11.given_ref = bf16[256,768]{1,0:T(8,128)(2,1)} collective-permute-done((bf16[256,768]{1,0:T(8,128)(2,1)}, bf16[256,768]{1,0:T(8,128)(2,1)}, u32[]{:S(2)}, u32[]{:S(2)}) %collective-permute-start.11) | collective-permute-done | bytes 393248 | tf_op jit(solution)/shard_map/ppermute | solution.py:441
  148.2 1.9 %shard_map.117 = (f32[128,768]{1,0:T(8,128)}, f32[128,768]{1,0:T(8,128)}) custom-call(bf16[256,768]{1,0:T(8,128)(2,1)} %collective-permute-done.11.given_ref), custom_call_target="tpu_custom_call" | custom-call | flops 11500000256 | tf_op jit(solution)/shard_map/pallas_call | solution.py:43
  150.1 0.0 all-to-all-done.3
  150.1 1.0 copy-done.5
  151.1 2.9 %shard_map.118 = (bf16[128,768]{1,0:T(8,128)(2,1)}, bf16[128,768]{1,0:T(8,128)(2,1)}) custom-call(s32[2,128]{1,0:T(2,128)} %bitcast.19, f32[2,128]{1,0:T(2,128)} %bitcast.21, bf16[640,768]{1,0:T(8,128)(2,1)} %bitcast.17, f32[128,768]{1,0:T(8,128)} %get-tuple-element.80.refs_3_, f32[128,768]{1,0:T(8,128)} %get-tuple-element.81.refs_4_), custom_call_target="tpu_custom_call" | custom-call | flops 2300000000 | tf_op jit(solution)/shard_map/pallas_call | solution.py:43
  154.0 0.0 collective-permute-done.13.refs_2_
  154.0 1.0 collective-permute-done.15.refs_3_
  155.0 0.8 copy-done.11
  155.8 3.3 %shard_map.119 = (f32[1,192,768]{2,1,0:T(8,128)}, f32[1,192,768]{2,1,0:T(8,128)}, f32[1,192,768]{2,1,0:T(8,128)}) custom-call(bf16[288,768]{1,0:T(8,128)(2,1)} %get-tuple-element.85.refs_0_, bf16[288,768]{1,0:T(8,128)(2,1)} %get-tuple-element.86.refs_1_, bf16[288,768]{1,0:T(8,128)(2,1)} %collective-permute-done.13.refs_2_, bf16[288,768]{1,0:T(8,128)(2,1)} %copy-done.11, ...), custom_call_target="tpu_custom_call" | custom-call | flops 2300000000 | tf_op jit(solution)/shard_map/pallas_call | solution.py:43
  (16 shorter events, 0.0 us)
Async XLA Ops:
  4.1 17.8 %collective-permute-start = (bf16[272,768]{1,0:T(8,128)(2,1)}, bf16[272,768]{1,0:T(8,128)(2,1)S(1)}, u32[]{:S(2)}, u32[]{:S(2)}) collective-permute-start(bf16[272,768]{1,0:T(8,128)(2,1)} %get-tuple-element.51), channel_id=1, source_target_pairs={{0,128},{32,160},{64,192},{96,224},{128,0},{160,32},{192,64},{224,... | collective-permute-start | bytes 1253384 | tf_op jit(solution)/shard_map/ppermute | solution.py:441
  11.8 28.6 %all-to-all-start = ((bf16[16,40,768]{2,1,0:T(8,128)(2,1)}), bf16[16,40,768]{2,1,0:T(8,128)(2,1)S(1)}, u32[]{:S(2)}, u32[]{:S(2)}) async-start(bf16[16,40,768]{2,1,0:T(8,128)(2,1)} %bitcast.16), calls=%async_computation | async-start | bytes 1966080 | tf_op jit(solution)/shard_map/all_to_all | solution.py:450
  18.6 21.5 %collective-permute-start.1 = (bf16[288,768]{1,0:T(8,128)(2,1)}, bf16[288,768]{1,0:T(8,128)(2,1)}, u32[]{:S(2)}, u32[]{:S(2)}) collective-permute-start(bf16[288,768]{1,0:T(8,128)(2,1)} %get-tuple-element.52.refs_2_), channel_id=1, source_target_pairs={{0,32},{32,64},{64,96},{96,128},{128,160},{160,192},{192,224},{224... | collective-permute-start | bytes 1327112 | tf_op jit(solution)/shard_map/ppermute | solution.py:441
  19.4 21.0 %collective-permute-start.2 = (bf16[288,768]{1,0:T(8,128)(2,1)}, bf16[288,768]{1,0:T(8,128)(2,1)}, u32[]{:S(2)}, u32[]{:S(2)}) collective-permute-start(bf16[288,768]{1,0:T(8,128)(2,1)} %get-tuple-element.53.refs_3_), channel_id=1, source_target_pairs={{0,224},{32,0},{64,32},{96,64},{128,96},{160,128},{192,160},{224,1... | collective-permute-start | bytes 1327112 | tf_op jit(solution)/shard_map/ppermute | solution.py:441
  21.9 0.8 copy-start.12
  40.4 6.6 %copy-start = (bf16[16,40,768]{2,1,0:T(8,128)(2,1)}, bf16[16,40,768]{2,1,0:T(8,128)(2,1)S(1)}, u32[]{:S(2)}) copy-start(bf16[16,40,768]{2,1,0:T(8,128)(2,1)S(1)} %all-to-all-done) | copy-start | bytes 2949124
  40.4 13.4 %collective-permute-start.3 = (bf16[640,768]{1,0:T(8,128)(2,1)S(1)}, bf16[640,768]{1,0:T(8,128)(2,1)S(1)}, u32[]{:S(2)}, u32[]{:S(2)}) collective-permute-start(bf16[640,768]{1,0:T(8,128)(2,1)S(1)} %bitcast.10), channel_id=1, source_target_pairs={{0,16},{16,0},{1,17},{17,1},{2,18},{18,2},{3,19},{19,3},{4,20},{20... | collective-permute-start | bytes 2949128 | tf_op jit(solution)/shard_map/ppermute | solution.py:447
  42.0 20.1 %collective-permute-start.5 = (bf16[288,768]{1,0:T(8,128)(2,1)}, bf16[288,768]{1,0:T(8,128)(2,1)S(1)}, u32[]{:S(2)}, u32[]{:S(2)}) collective-permute-start(bf16[288,768]{1,0:T(8,128)(2,1)} %get-tuple-element.52.refs_2_), channel_id=1, source_target_pairs={{0,224},{32,0},{64,32},{96,64},{128,96},{160,128},{192,160},{224,1... | collective-permute-start | bytes 1327112 | tf_op jit(solution)/shard_map/ppermute | solution.py:441
  44.3 17.8 %collective-permute-start.4 = (bf16[288,768]{1,0:T(8,128)(2,1)}, bf16[288,768]{1,0:T(8,128)(2,1)}, u32[]{:S(2)}, u32[]{:S(2)}) collective-permute-start(bf16[288,768]{1,0:T(8,128)(2,1)} %get-tuple-element.53.refs_3_), channel_id=1, source_target_pairs={{0,32},{32,64},{64,96},{96,128},{128,160},{160,192},{192,224},{224... | collective-permute-start | bytes 1327112 | tf_op jit(solution)/shard_map/ppermute | solution.py:441
  44.3 22.4 %collective-permute-start.6 = (bf16[288,768]{1,0:T(8,128)(2,1)}, bf16[288,768]{1,0:T(8,128)(2,1)}, u32[]{:S(2)}, u32[]{:S(2)}) collective-permute-start(bf16[288,768]{1,0:T(8,128)(2,1)} %collective-permute-done.1.refs_4_), channel_id=1, source_target_pairs={{0,32},{32,64},{64,96},{96,128},{128,160},{160,192},{192,224},{224... | collective-permute-start | bytes 1327112 | tf_op jit(solution)/shard_map/ppermute | solution.py:441
  44.3 22.4 %collective-permute-start.7 = (bf16[288,768]{1,0:T(8,128)(2,1)}, bf16[288,768]{1,0:T(8,128)(2,1)}, u32[]{:S(2)}, u32[]{:S(2)}) collective-permute-start(bf16[288,768]{1,0:T(8,128)(2,1)} %collective-permute-done.2.refs_5_), channel_id=1, source_target_pairs={{0,224},{32,0},{64,32},{96,64},{128,96},{160,128},{192,160},{224,1... | collective-permute-start | bytes 1327112 | tf_op jit(solution)/shard_map/ppermute | solution.py:441
  47.0 21.8 %all-to-all-start.1 = ((bf16[16,40,768]{2,1,0:T(8,128)(2,1)}), bf16[16,40,768]{2,1,0:T(8,128)(2,1)S(1)}, u32[]{:S(2)}, u32[]{:S(2)}) async-start(bf16[16,40,768]{2,1,0:T(8,128)(2,1)} %bitcast.12), calls=%async_computation.1 | async-start | bytes 1966080 | tf_op jit(solution)/shard_map/all_to_all | solution.py:450
  53.8 1.0 copy-start.8
  62.1 11.7 %copy-start.10 = (bf16[288,768]{1,0:T(8,128)(2,1)}, bf16[288,768]{1,0:T(8,128)(2,1)S(1)}, u32[]{:S(2)}) copy-start(bf16[288,768]{1,0:T(8,128)(2,1)S(1)} %collective-permute-done.5.refs_7_.refs_8_.refs_16_) | copy-start | bytes 1327108
  68.8 4.9 %copy-start.2 = (bf16[16,40,768]{2,1,0:T(8,128)(2,1)}, bf16[16,40,768]{2,1,0:T(8,128)(2,1)S(1)}, u32[]{:S(2)}) copy-start(bf16[16,40,768]{2,1,0:T(8,128)(2,1)S(1)} %all-to-all-done.1) | copy-start | bytes 2949124
  68.8 4.9 %collective-permute-start.8 = (bf16[640,768]{1,0:T(8,128)(2,1)S(1)}, bf16[640,768]{1,0:T(8,128)(2,1)S(1)}, u32[]{:S(2)}, u32[]{:S(2)}) collective-permute-start(bf16[640,768]{1,0:T(8,128)(2,1)S(1)} %bitcast.13), channel_id=1, source_target_pairs={{0,16},{16,0},{1,17},{17,1},{2,18},{18,2},{3,19},{19,3},{4,20},{20... | collective-permute-start | bytes 2949128 | tf_op jit(solution)/shard_map/ppermute | solution.py:447
  73.8 1.0 copy-start.9
  85.8 11.2 %collective-permute-start.9 = (bf16[640,768]{1,0:T(8,128)(2,1)}, bf16[640,768]{1,0:T(8,128)(2,1)S(1)}, u32[]{:S(2)}, u32[]{:S(2)}) collective-permute-start(bf16[640,768]{1,0:T(8,128)(2,1)} %get-tuple-element.68), channel_id=1, source_target_pairs={{0,16},{16,0},{1,17},{17,1},{2,18},{18,2},{3,19},{19,3},{4,20},{20... | collective-permute-start | bytes 2949128 | tf_op jit(solution)/shard_map/ppermute | solution.py:447
  86.2 10.7 %copy-start.4 = (bf16[640,768]{1,0:T(8,128)(2,1)S(1)}, bf16[640,768]{1,0:T(8,128)(2,1)}, u32[]{:S(2)}) copy-start(bf16[640,768]{1,0:T(8,128)(2,1)} %get-tuple-element.67) | copy-start | bytes 2949124
  95.4 21.5 %collective-permute-start.12 = (bf16[576,768]{1,0:T(8,128)(2,1)}, bf16[576,768]{1,0:T(8,128)(2,1)S(1)}, u32[]{:S(2)}, u32[]{:S(2)}) collective-permute-start(bf16[576,768]{1,0:T(8,128)(2,1)} %get-tuple-element.88), channel_id=1, source_target_pairs={{0,224},{32,0},{64,32},{96,64},{128,96},{160,128},{192,160},{224,1... | collective-permute-start | bytes 2654216 | tf_op jit(solution)/shard_map/ppermute | solution.py:441
  96.8 36.0 %collective-permute-start.14 = (bf16[576,768]{1,0:T(8,128)(2,1)}, bf16[576,768]{1,0:T(8,128)(2,1)}, u32[]{:S(2)}, u32[]{:S(2)}) collective-permute-start(bf16[576,768]{1,0:T(8,128)(2,1)} %get-tuple-element.91), channel_id=1, source_target_pairs={{0,32},{32,64},{64,96},{96,128},{128,160},{160,192},{192,224},{224... | collective-permute-start | bytes 2654216 | tf_op jit(solution)/shard_map/ppermute | solution.py:441
  98.1 23.9 %all-to-all-start.2 = ((bf16[16,40,768]{2,1,0:T(8,128)(2,1)}), bf16[16,40,768]{2,1,0:T(8,128)(2,1)S(1)}, u32[]{:S(2)}, u32[]{:S(2)}) async-start(bf16[16,40,768]{2,1,0:T(8,128)(2,1)} %bitcast.6), calls=%async_computation.2 | async-start | bytes 1966080 | tf_op jit(solution)/shard_map/all_to_all | solution.py:450
  116.9 3.9 %copy-start.7 = (bf16[576,768]{1,0:T(8,128)(2,1)}, bf16[576,768]{1,0:T(8,128)(2,1)S(1)}, u32[]{:S(2)}) copy-start(bf16[576,768]{1,0:T(8,128)(2,1)S(1)} %collective-permute-done.12.refs_4_) | copy-start | bytes 2654212
  118.3 35.7 %collective-permute-start.13 = (bf16[288,768]{1,0:T(8,128)(2,1)S(1)}, bf16[288,768]{1,0:T(8,128)(2,1)}, u32[]{:S(2)}, u32[]{:S(2)}) collective-permute-start(bf16[288,768]{1,0:T(8,128)(2,1)S(1)} %add_convert_fusion.3), channel_id=1, source_target_pairs={{0,224},{32,0},{64,32},{96,64},{128,96},{160,128},{192,160},{224,1... | collective-permute-start | bytes 1327112 | tf_op jit(solution)/shard_map/ppermute | solution.py:441
  120.8 7.0 %collective-permute-start.10 = (bf16[640,768]{1,0:T(8,128)(2,1)}, bf16[640,768]{1,0:T(8,128)(2,1)S(1)}, u32[]{:S(2)}, u32[]{:S(2)}) collective-permute-start(bf16[640,768]{1,0:T(8,128)(2,1)} %get-tuple-element.78), channel_id=1, source_target_pairs={{0,16},{16,0},{1,17},{17,1},{2,18},{18,2},{3,19},{19,3},{4,20},{20... | collective-permute-start | bytes 2949128 | tf_op jit(solution)/shard_map/ppermute | solution.py:447
  122.0 1.0 copy-start.3
  123.0 4.8 %copy-start.1 = (bf16[640,768]{1,0:T(8,128)(2,1)S(1)}, bf16[640,768]{1,0:T(8,128)(2,1)}, u32[]{:S(2)}) copy-start(bf16[640,768]{1,0:T(8,128)(2,1)} %get-tuple-element.77) | copy-start | bytes 2949124
  126.0 22.3 %collective-permute-start.11 = (bf16[256,768]{1,0:T(8,128)(2,1)}, bf16[256,768]{1,0:T(8,128)(2,1)}, u32[]{:S(2)}, u32[]{:S(2)}) collective-permute-start(bf16[256,768]{1,0:T(8,128)(2,1)} %shard_map.116), channel_id=1, source_target_pairs={{0,128},{32,160},{64,192},{96,224},{128,0},{160,32},{192,64},{224,... | collective-permute-start | bytes 1179656 | tf_op jit(solution)/shard_map/ppermute | solution.py:441
  128.9 3.8 %copy-start.6 = (bf16[288,768]{1,0:T(8,128)(2,1)S(1)}, bf16[288,768]{1,0:T(8,128)(2,1)}, u32[]{:S(2)}) copy-start(bf16[288,768]{1,0:T(8,128)(2,1)} %get-tuple-element.90) | copy-start | bytes 1327108
  128.9 21.2 %all-to-all-start.3 = ((bf16[16,40,768]{2,1,0:T(8,128)(2,1)}), bf16[16,40,768]{2,1,0:T(8,128)(2,1)S(1)}, u32[]{:S(2)}, u32[]{:S(2)}) async-start(bf16[16,40,768]{2,1,0:T(8,128)(2,1)} %bitcast.8), calls=%async_computation.3 | async-start | bytes 1966080 | tf_op jit(solution)/shard_map/all_to_all | solution.py:450
  133.9 21.1 %collective-permute-start.15 = (bf16[288,768]{1,0:T(8,128)(2,1)S(1)}, bf16[288,768]{1,0:T(8,128)(2,1)S(1)}, u32[]{:S(2)}, u32[]{:S(2)}) collective-permute-start(bf16[288,768]{1,0:T(8,128)(2,1)S(1)} %add_convert_fusion.2), channel_id=1, source_target_pairs={{0,32},{32,64},{64,96},{96,128},{128,160},{160,192},{192,224},{224... | collective-permute-start | bytes 1327112 | tf_op jit(solution)/shard_map/ppermute | solution.py:441
  150.1 1.0 copy-start.5
  155.0 0.8 copy-start.11

commit v3 on v2

--- a/solution.py
+++ b/solution.py
@@ -480,7 +480,7 @@
 
     left_first, right_second = along(first, 1), along(second, -1)
     far_sent = dispatch(FAR_US, True, far_packed)[0]
-    far = exchange(after(far_sent, near, left_first, right_second))
+    far = exchange(after(far_sent, left_first, right_second))
     left_second, right_first = along(second, 1), along(first, -1)
     far_first, far_second = along(left_first, 1), along(right_second, -1)
     early = [first, second, left_first, right_second]
@@ -508,7 +508,7 @@
     back_first, back_second = along(go_left, -1), along(go_right, 1)
     half = 3 * part
     to_left = along(rounded_sum(t_left_first, back_first[:half]), -1)
-    to_right = along(rounded_sum(after(t_right_second, near_sum), back_second[:half]), 1)
+    to_right = along(rounded_sum(t_right_second, back_second[:half]), 1)
 
     scale = float(tok_rows * choose * ring * CORES) ** (-0.5)
     grads = kernel_call(

time: 160 us -> 158 us (0.988)
  waiting for transfers between devices: 43.5 us -> 36.9 us
  starting transfers between devices: 48.5 us -> 51.9 us
    ppermute x12, waiting for transfers between devices: 39.2 us -> 34.1 us  [along(): lax.ppermute(value, 'z', [(i, (i + step) % ring) for i in range(ring)])]
    ppermute x12, starting transfers between devices: 21.4 us -> 24.4 us  [along(): lax.ppermute(value, 'z', [(i, (i + step) % ring) for i in range(ring)])]
    all_to_all x4, starting transfers between devices: 21.1 us -> 23.3 us  [exchange(): lax.all_to_all(value.reshape(experts, 2 * cap, width), 'expert', split_ax...]
    ppermute x4, starting transfers between devices: 5.97 us -> 4.19 us  [other_core(): return lax.ppermute(value, 'core', [(0, 1), (1, 0)])]
    unnamed x26 -> x30, local copies, waits for them, and re-layouts: 5.49 us -> 7.03 us
  transfers between devices with their start and end apart: 20 -> 20, of which waited for: 9 -> 8; matrix products, arithmetic and copies ran while one was open for 3% -> 3% of each run, Pallas kernels for 24% -> 24%
where the time goes in v3:
time: 158 us; the launch traced here: 157 us
  Pallas kernels  55.8 us (35%)
  starting transfers between devices  51.9 us (33%)
  waiting for transfers between devices  36.9 us (23%)
  local copies, waits for them, and re-layouts  7.03 us (4%)
  other arithmetic  4.92 us (3%)
    pallas_call x10, Pallas kernels, kernel_call(): pl.pallas_call(body, out_shape=out_shapes, in_specs=whole(len(operands) -...  55.8 us
    ppermute x12, waiting for transfers between devices, along(): lax.ppermute(value, 'z', [(i, (i + step) % ring) for i in range(ring)])  34.1 us
    ppermute x12, starting transfers between devices, along(): lax.ppermute(value, 'z', [(i, (i + step) % ring) for i in range(ring)])  24.4 us
    all_to_all x4, starting transfers between devices, exchange(): lax.all_to_all(value.reshape(experts, 2 * cap, width), 'expert', split_ax...  23.3 us
    unnamed x30, local copies, waits for them, and re-layouts  7.03 us
    convert_element_type x4, other arithmetic, rounded_sum(): return (a.astype(F32) + b.astype(F32)).astype(BF16)  4.92 us
    ppermute x4, starting transfers between devices, other_core(): return lax.ppermute(value, 'core', [(0, 1), (1, 0)])  4.19 us
  transfers between devices with their start and end apart: 20, of which 8 were waited for; matrix products, arithmetic and copies ran while one was open for 3% of the time, Pallas kernels for 24%

profile of v3, /device:TPU:1, one launch (start us, length us, event | category | flops | bytes accessed | tf_op | source)
XLA Modules:
  0.0 157.3 jit_solution(1687622883050016584)
XLA Ops:
  0.6 3.5 %shard_map.110 = (bf16[640,768]{1,0:T(8,128)(2,1)}, bf16[272,768]{1,0:T(8,128)(2,1)}, bf16[288,768]{1,0:T(8,128)(2,1)}, bf16[288,768]{1,0:T(8,128)(2,1)}) custom-call(s32[2,128]{1,0:T(2,128)} %bitcast.18, f32[2,128]{1,0:T(2,128)} %bitcast.20, bf16[128,768]{1,0:T(8,128)(2,1)} %refs_2_.1, bf16[128,768]{1,0:T(8,128)(2,1)} %refs_3_.1, ...), custom_call_target="tpu_custom_call" | custom-call | flops 2300000000 | tf_op jit(solution)/shard_map/pallas_call | solution.py:43
  4.1 7.7 %collective-permute-start = (bf16[272,768]{1,0:T(8,128)(2,1)}, bf16[272,768]{1,0:T(8,128)(2,1)S(1)}, u32[]{:S(2)}, u32[]{:S(2)}) collective-permute-start(bf16[272,768]{1,0:T(8,128)(2,1)} %get-tuple-element.50), channel_id=1, source_target_pairs={{0,128},{32,160},{64,192},{96,224},{128,0},{160,32},{192,64},{224,... | collective-permute-start | bytes 1253384 | tf_op jit(solution)/shard_map/ppermute | solution.py:441
  11.9 6.8 %all-to-all-start = ((bf16[16,40,768]{2,1,0:T(8,128)(2,1)}), bf16[16,40,768]{2,1,0:T(8,128)(2,1)S(1)}, u32[]{:S(2)}, u32[]{:S(2)}) async-start(bf16[16,40,768]{2,1,0:T(8,128)(2,1)} %bitcast.16), calls=%async_computation | async-start | bytes 1966080 | tf_op jit(solution)/shard_map/all_to_all | solution.py:450
  18.6 0.8 collective-permute-start.1
  19.4 1.9 %collective-permute-start.2 = (bf16[288,768]{1,0:T(8,128)(2,1)}, bf16[288,768]{1,0:T(8,128)(2,1)S(1)}, u32[]{:S(2)}, u32[]{:S(2)}) collective-permute-start(bf16[288,768]{1,0:T(8,128)(2,1)} %get-tuple-element.52.refs_3_), channel_id=1, source_target_pairs={{0,224},{32,0},{64,32},{96,64},{128,96},{160,128},{192,160},{224,1... | collective-permute-start | bytes 1327112 | tf_op jit(solution)/shard_map/ppermute | solution.py:441
  21.4 0.5 collective-permute-done.refs_0_
  21.9 0.8 copy-done.14
  22.7 2.8 %shard_map.111 = bf16[640,768]{1,0:T(8,128)(2,1)} custom-call(bf16[272,768]{1,0:T(8,128)(2,1)} %copy-done.14), custom_call_target="tpu_custom_call" | custom-call | flops 5750000128 | tf_op jit(solution)/shard_map/pallas_call | solution.py:43
  25.5 14.5 %collective-permute-done.1.refs_4_ = bf16[288,768]{1,0:T(8,128)(2,1)S(1)} collective-permute-done((bf16[288,768]{1,0:T(8,128)(2,1)}, bf16[288,768]{1,0:T(8,128)(2,1)S(1)}, u32[]{:S(2)}, u32[]{:S(2)}) %collective-permute-start.1) | collective-permute-done | bytes 442400 | tf_op jit(solution)/shard_map/ppermute | solution.py:441
  40.0 0.8 copy-done.12
  40.7 0.0 collective-permute-done.2.refs_5_
  40.8 0.0 all-to-all-done
  40.8 0.0 copy-start
  40.8 0.8 copy-done.13
  41.5 1.1 collective-permute-start.3
  42.6 2.3 %collective-permute-start.5 = (bf16[288,768]{1,0:T(8,128)(2,1)}, bf16[288,768]{1,0:T(8,128)(2,1)S(1)}, u32[]{:S(2)}, u32[]{:S(2)}) collective-permute-start(bf16[288,768]{1,0:T(8,128)(2,1)} %get-tuple-element.51.refs_2_), channel_id=1, source_target_pairs={{0,224},{32,0},{64,32},{96,64},{128,96},{160,128},{192,160},{224,1... | collective-permute-start | bytes 1327112 | tf_op jit(solution)/shard_map/ppermute | solution.py:441
  45.0 0.0 collective-permute-start.4
  45.0 6.8 %all-to-all-start.1 = ((bf16[16,40,768]{2,1,0:T(8,128)(2,1)}), bf16[16,40,768]{2,1,0:T(8,128)(2,1)S(1)}, u32[]{:S(2)}, u32[]{:S(2)}) async-start(bf16[16,40,768]{2,1,0:T(8,128)(2,1)} %bitcast.12), calls=%async_computation.1 | async-start | bytes 1966080 | tf_op jit(solution)/shard_map/all_to_all | solution.py:450
  51.8 0.1 collective-permute-start.6
  51.9 2.7 %collective-permute-start.7 = (bf16[288,768]{1,0:T(8,128)(2,1)}, bf16[288,768]{1,0:T(8,128)(2,1)}, u32[]{:S(2)}, u32[]{:S(2)}) collective-permute-start(bf16[288,768]{1,0:T(8,128)(2,1)} %copy-done.13), channel_id=1, source_target_pairs={{0,224},{32,0},{64,32},{96,64},{128,96},{160,128},{192,160},{224,1... | collective-permute-start | bytes 1327112 | tf_op jit(solution)/shard_map/ppermute | solution.py:441
  54.6 0.0 collective-permute-done.3.refs_1_
  54.6 1.0 copy-done.8
  55.6 7.3 %shard_map.112 = (bf16[640,384]{1,0:T(8,128)(2,1)}, bf16[640,384]{1,0:T(8,128)(2,1)}, bf16[640,384]{1,0:T(8,128)(2,1)}, bf16[640,768]{1,0:T(8,128)(2,1)}, bf16[6...) custom-call(bf16[640,768]{1,0:T(8,128)(2,1)} %bitcast.11, bf16[640,768]{1,0:T(8,128)(2,1)} %copy-done.8, ...), custom_call_target="tpu_custom_call" | custom-call | flops 23000000512 | tf_op jit(solution)/shard_map/pallas_call | solution.py:43
  62.9 0.0 collective-permute-done.5.refs_7_.refs_8_.refs_16_
  62.9 0.0 collective-permute-done.4.refs_6_.refs_7_.refs_15_
  62.9 4.5 %collective-permute-done.6.refs_8_.refs_9_.refs_17_ = bf16[288,768]{1,0:T(8,128)(2,1)S(1)} collective-permute-done((bf16[288,768]{1,0:T(8,128)(2,1)}, bf16[288,768]{1,0:T(8,128)(2,1)S(1)}, u32[]{:S(2)}, u32[]{:S(2)}) %collective-permute-start.6) | collective-permute-done | bytes 442400 | tf_op jit(solution)/shard_map/ppermute | solution.py:441
  67.4 0.8 copy-done.11
  68.1 0.0 collective-permute-done.7.refs_9_.refs_10_.refs_18_
  68.1 0.0 all-to-all-done.1
  68.1 1.4 collective-permute-start.8
  69.5 2.2 %collective-permute-done.8.refs_1_ = bf16[640,768]{1,0:T(8,128)(2,1)S(1)} collective-permute-done((bf16[640,768]{1,0:T(8,128)(2,1)S(1)}, bf16[640,768]{1,0:T(8,128)(2,1)S(1)}, u32[]{:S(2)}, u32[]{:S(2)}) %collective-permute-start.8) | collective-permute-done | bytes 983072 | tf_op jit(solution)/shard_map/ppermute | solution.py:447
  71.7 0.0 copy-done.10
  71.7 1.0 copy-done.9
  72.8 11.0 %shard_map.113 = (bf16[640,768]{1,0:T(8,128)(2,1)}, bf16[640,768]{1,0:T(8,128)(2,1)}, bf16[640,768]{1,0:T(8,128)(2,1)}, bf16[640,768]{1,0:T(8,128)(2,1)}, bf16[6...) custom-call(bf16[640,768]{1,0:T(8,128)(2,1)} %bitcast.14, bf16[640,768]{1,0:T(8,128)(2,1)} %copy-done.9, ...), custom_call_target="tpu_custom_call" | custom-call | flops 11500000256 | tf_op jit(solution)/shard_map/pallas_call | solution.py:43
  83.7 0.5 collective-permute-start.9
  84.2 9.1 %shard_map.114 = (bf16[576,768]{1,0:T(8,128)(2,1)}, bf16[576,768]{1,0:T(8,128)(2,1)}, bf16[640,384]{1,0:T(8,128)(2,1)}, bf16[640,384]{1,0:T(8,128)(2,1)}, bf16[640,384]{1,0:T(8,128)(2,1)}) custom-call(bf16[640,768]{1,0:T(8,128)(2,1)} %get-tuple-element.54.refs_0_, bf16[640,768]{1,0:T(8,128)(2,1)} %get-tuple-element.55.refs_1_, ...), custom_call_target="tpu_custom_call" | custom-call | flops 9200000000 | tf_op jit(solution)/shard_map/pallas_call | solution.py:43
  93.3 2.8 %collective-permute-start.12 = (bf16[576,768]{1,0:T(8,128)(2,1)}, bf16[576,768]{1,0:T(8,128)(2,1)S(1)}, u32[]{:S(2)}, u32[]{:S(2)}) collective-permute-start(bf16[576,768]{1,0:T(8,128)(2,1)} %get-tuple-element.87), channel_id=1, source_target_pairs={{0,224},{32,0},{64,32},{96,64},{128,96},{160,128},{192,160},{224,1... | collective-permute-start | bytes 2654216 | tf_op jit(solution)/shard_map/ppermute | solution.py:441
  96.1 0.0 collective-permute-start.14
  96.1 0.0 collective-permute-done.9
  96.2 1.2 add_convert_fusion.1
  97.3 5.5 %all-to-all-start.2 = ((bf16[16,40,768]{2,1,0:T(8,128)(2,1)}), bf16[16,40,768]{2,1,0:T(8,128)(2,1)S(1)}, u32[]{:S(2)}, u32[]{:S(2)}) async-start(bf16[16,40,768]{2,1,0:T(8,128)(2,1)} %bitcast.6), calls=%async_computation.2 | async-start | bytes 1966080 | tf_op jit(solution)/shard_map/all_to_all | solution.py:450
  102.8 11.0 %shard_map.115 = (bf16[288,768]{1,0:T(8,128)(2,1)}, bf16[288,768]{1,0:T(8,128)(2,1)}, bf16[288,768]{1,0:T(8,128)(2,1)}, bf16[288,768]{1,0:T(8,128)(2,1)}, bf16[6...) custom-call(bf16[640,768]{1,0:T(8,128)(2,1)} %get-tuple-element.54.refs_0_, bf16[640,768]{1,0:T(8,128)(2,1)} %get-tuple-element.55.refs_1_, ...), custom_call_target="tpu_custom_call" | custom-call | flops 9200000000 | tf_op jit(solution)/shard_map/pallas_call | solution.py:43
  113.9 1.5 collective-permute-done.12.refs_4_
  115.4 1.4 add_convert_fusion.3
  116.8 3.4 %collective-permute-start.13 = (bf16[288,768]{1,0:T(8,128)(2,1)S(1)}, bf16[288,768]{1,0:T(8,128)(2,1)}, u32[]{:S(2)}, u32[]{:S(2)}) collective-permute-start(bf16[288,768]{1,0:T(8,128)(2,1)S(1)} %add_convert_fusion.3), channel_id=1, source_target_pairs={{0,224},{32,0},{64,32},{96,64},{128,96},{160,128},{192,160},{224,1... | collective-permute-start | bytes 1327112 | tf_op jit(solution)/shard_map/ppermute | solution.py:441
  120.2 1.2 collective-permute-start.10
  121.4 0.0 all-to-all-done.2
  121.4 1.0 copy-done.3
  122.4 2.9 %shard_map.116 = bf16[256,768]{1,0:T(8,128)(2,1)} custom-call(bf16[272,768]{1,0:T(8,128)(2,1)} %copy-done.14, bf16[640,768]{1,0:T(8,128)(2,1)} %bitcast.15), custom_call_target="tpu_custom_call" | custom-call | flops 34500001792 | tf_op jit(solution)/shard_map/pallas_call | solution.py:43
  125.3 2.5 %collective-permute-start.11 = (bf16[256,768]{1,0:T(8,128)(2,1)}, bf16[256,768]{1,0:T(8,128)(2,1)}, u32[]{:S(2)}, u32[]{:S(2)}) collective-permute-start(bf16[256,768]{1,0:T(8,128)(2,1)} %shard_map.116), channel_id=1, source_target_pairs={{0,128},{32,160},{64,192},{96,224},{128,0},{160,32},{192,64},{224,... | collective-permute-start | bytes 1179656 | tf_op jit(solution)/shard_map/ppermute | solution.py:441
  127.8 0.0 collective-permute-done.14.refs_5_
  127.8 1.1 add_convert_fusion.2
  128.9 0.1 collective-permute-start.15
  129.0 0.0 collective-permute-done.10
  129.0 1.2 add_convert_fusion
  130.2 4.3 %all-to-all-start.3 = ((bf16[16,40,768]{2,1,0:T(8,128)(2,1)}), bf16[16,40,768]{2,1,0:T(8,128)(2,1)S(1)}, u32[]{:S(2)}, u32[]{:S(2)}) async-start(bf16[16,40,768]{2,1,0:T(8,128)(2,1)} %bitcast.8), calls=%async_computation.3 | async-start | bytes 1966080 | tf_op jit(solution)/shard_map/all_to_all | solution.py:450
  134.5 12.9 %collective-permute-done.11.given_ref = bf16[256,768]{1,0:T(8,128)(2,1)} collective-permute-done((bf16[256,768]{1,0:T(8,128)(2,1)}, bf16[256,768]{1,0:T(8,128)(2,1)}, u32[]{:S(2)}, u32[]{:S(2)}) %collective-permute-start.11) | collective-permute-done | bytes 393248 | tf_op jit(solution)/shard_map/ppermute | solution.py:441
  147.4 1.9 %shard_map.117 = (f32[128,768]{1,0:T(8,128)}, f32[128,768]{1,0:T(8,128)}) custom-call(bf16[256,768]{1,0:T(8,128)(2,1)} %collective-permute-done.11.given_ref), custom_call_target="tpu_custom_call" | custom-call | flops 11500000256 | tf_op jit(solution)/shard_map/pallas_call | solution.py:43
  149.3 0.6 all-to-all-done.3
  149.9 1.0 copy-done.5
  150.9 2.9 %shard_map.118 = (bf16[128,768]{1,0:T(8,128)(2,1)}, bf16[128,768]{1,0:T(8,128)(2,1)}) custom-call(s32[2,128]{1,0:T(2,128)} %bitcast.19, f32[2,128]{1,0:T(2,128)} %bitcast.21, bf16[640,768]{1,0:T(8,128)(2,1)} %bitcast.17, f32[128,768]{1,0:T(8,128)} %get-tuple-element.79.refs_3_, f32[128,768]{1,0:T(8,128)} %get-tuple-element.80.refs_4_), custom_call_target="tpu_custom_call" | custom-call | flops 2300000000 | tf_op jit(solution)/shard_map/pallas_call | solution.py:43
  153.8 0.0 collective-permute-done.13.refs_2_
  153.8 0.2 collective-permute-done.15.refs_3_
  154.0 3.3 %shard_map.119 = (f32[1,192,768]{2,1,0:T(8,128)}, f32[1,192,768]{2,1,0:T(8,128)}, f32[1,192,768]{2,1,0:T(8,128)}) custom-call(bf16[288,768]{1,0:T(8,128)(2,1)} %get-tuple-element.84.refs_0_, bf16[288,768]{1,0:T(8,128)(2,1)} %get-tuple-element.85.refs_1_, bf16[288,768]{1,0:T(8,128)(2,1)} %collective-permute-done.13.refs_2_, ...), custom_call_target="tpu_custom_call" | custom-call | flops 2300000000 | tf_op jit(solution)/shard_map/pallas_call | solution.py:43
  (20 shorter events, 0.0 us)
Async XLA Ops:
  4.1 17.8 %collective-permute-start = (bf16[272,768]{1,0:T(8,128)(2,1)}, bf16[272,768]{1,0:T(8,128)(2,1)S(1)}, u32[]{:S(2)}, u32[]{:S(2)}) collective-permute-start(bf16[272,768]{1,0:T(8,128)(2,1)} %get-tuple-element.50), channel_id=1, source_target_pairs={{0,128},{32,160},{64,192},{96,224},{128,0},{160,32},{192,64},{224,... | collective-permute-start | bytes 1253384 | tf_op jit(solution)/shard_map/ppermute | solution.py:441
  11.9 28.9 %all-to-all-start = ((bf16[16,40,768]{2,1,0:T(8,128)(2,1)}), bf16[16,40,768]{2,1,0:T(8,128)(2,1)S(1)}, u32[]{:S(2)}, u32[]{:S(2)}) async-start(bf16[16,40,768]{2,1,0:T(8,128)(2,1)} %bitcast.16), calls=%async_computation | async-start | bytes 1966080 | tf_op jit(solution)/shard_map/all_to_all | solution.py:450
  18.6 21.4 %collective-permute-start.1 = (bf16[288,768]{1,0:T(8,128)(2,1)}, bf16[288,768]{1,0:T(8,128)(2,1)S(1)}, u32[]{:S(2)}, u32[]{:S(2)}) collective-permute-start(bf16[288,768]{1,0:T(8,128)(2,1)} %get-tuple-element.51.refs_2_), channel_id=1, source_target_pairs={{0,32},{32,64},{64,96},{96,128},{128,160},{160,192},{192,224},{224... | collective-permute-start | bytes 1327112 | tf_op jit(solution)/shard_map/ppermute | solution.py:441
  19.4 21.3 %collective-permute-start.2 = (bf16[288,768]{1,0:T(8,128)(2,1)}, bf16[288,768]{1,0:T(8,128)(2,1)S(1)}, u32[]{:S(2)}, u32[]{:S(2)}) collective-permute-start(bf16[288,768]{1,0:T(8,128)(2,1)} %get-tuple-element.52.refs_3_), channel_id=1, source_target_pairs={{0,224},{32,0},{64,32},{96,64},{128,96},{160,128},{192,160},{224,1... | collective-permute-start | bytes 1327112 | tf_op jit(solution)/shard_map/ppermute | solution.py:441
  21.9 0.8 copy-start.14
  40.0 0.8 copy-start.12
  40.8 0.8 copy-start.13
  40.8 4.2 %copy-start = (bf16[16,40,768]{2,1,0:T(8,128)(2,1)}, bf16[16,40,768]{2,1,0:T(8,128)(2,1)S(1)}, u32[]{:S(2)}) copy-start(bf16[16,40,768]{2,1,0:T(8,128)(2,1)S(1)} %all-to-all-done) | copy-start | bytes 2949124
  41.5 13.1 %collective-permute-start.3 = (bf16[640,768]{1,0:T(8,128)(2,1)S(1)}, bf16[640,768]{1,0:T(8,128)(2,1)S(1)}, u32[]{:S(2)}, u32[]{:S(2)}) collective-permute-start(bf16[640,768]{1,0:T(8,128)(2,1)S(1)} %bitcast.10), channel_id=1, source_target_pairs={{0,16},{16,0},{1,17},{17,1},{2,18},{18,2},{3,19},{19,3},{4,20},{20... | collective-permute-start | bytes 2949128 | tf_op jit(solution)/shard_map/ppermute | solution.py:447
  42.6 20.2 %collective-permute-start.5 = (bf16[288,768]{1,0:T(8,128)(2,1)}, bf16[288,768]{1,0:T(8,128)(2,1)S(1)}, u32[]{:S(2)}, u32[]{:S(2)}) collective-permute-start(bf16[288,768]{1,0:T(8,128)(2,1)} %get-tuple-element.51.refs_2_), channel_id=1, source_target_pairs={{0,224},{32,0},{64,32},{96,64},{128,96},{160,128},{192,160},{224,1... | collective-permute-start | bytes 1327112 | tf_op jit(solution)/shard_map/ppermute | solution.py:441
  45.0 17.9 %collective-permute-start.4 = (bf16[288,768]{1,0:T(8,128)(2,1)}, bf16[288,768]{1,0:T(8,128)(2,1)}, u32[]{:S(2)}, u32[]{:S(2)}) collective-permute-start(bf16[288,768]{1,0:T(8,128)(2,1)} %get-tuple-element.52.refs_3_), channel_id=1, source_target_pairs={{0,32},{32,64},{64,96},{96,128},{128,160},{160,192},{192,224},{224... | collective-permute-start | bytes 1327112 | tf_op jit(solution)/shard_map/ppermute | solution.py:441
  45.0 23.1 %all-to-all-start.1 = ((bf16[16,40,768]{2,1,0:T(8,128)(2,1)}), bf16[16,40,768]{2,1,0:T(8,128)(2,1)S(1)}, u32[]{:S(2)}, u32[]{:S(2)}) async-start(bf16[16,40,768]{2,1,0:T(8,128)(2,1)} %bitcast.12), calls=%async_computation.1 | async-start | bytes 1966080 | tf_op jit(solution)/shard_map/all_to_all | solution.py:450
  51.8 15.6 %collective-permute-start.6 = (bf16[288,768]{1,0:T(8,128)(2,1)}, bf16[288,768]{1,0:T(8,128)(2,1)S(1)}, u32[]{:S(2)}, u32[]{:S(2)}) collective-permute-start(bf16[288,768]{1,0:T(8,128)(2,1)} %copy-done.12), channel_id=1, source_target_pairs={{0,32},{32,64},{64,96},{96,128},{128,160},{160,192},{192,224},{224... | collective-permute-start | bytes 1327112 | tf_op jit(solution)/shard_map/ppermute | solution.py:441
  51.9 16.3 %collective-permute-start.7 = (bf16[288,768]{1,0:T(8,128)(2,1)}, bf16[288,768]{1,0:T(8,128)(2,1)}, u32[]{:S(2)}, u32[]{:S(2)}) collective-permute-start(bf16[288,768]{1,0:T(8,128)(2,1)} %copy-done.13), channel_id=1, source_target_pairs={{0,224},{32,0},{64,32},{96,64},{128,96},{160,128},{192,160},{224,1... | collective-permute-start | bytes 1327112 | tf_op jit(solution)/shard_map/ppermute | solution.py:441
  54.6 1.0 copy-start.8
  62.9 8.8 %copy-start.10 = (bf16[288,768]{1,0:T(8,128)(2,1)}, bf16[288,768]{1,0:T(8,128)(2,1)S(1)}, u32[]{:S(2)}) copy-start(bf16[288,768]{1,0:T(8,128)(2,1)S(1)} %collective-permute-done.5.refs_7_.refs_8_.refs_16_) | copy-start | bytes 1327108
  67.4 0.8 copy-start.11
  68.1 3.6 %copy-start.2 = (bf16[16,40,768]{2,1,0:T(8,128)(2,1)}, bf16[16,40,768]{2,1,0:T(8,128)(2,1)S(1)}, u32[]{:S(2)}) copy-start(bf16[16,40,768]{2,1,0:T(8,128)(2,1)S(1)} %all-to-all-done.1) | copy-start | bytes 2949124
  68.1 3.6 %collective-permute-start.8 = (bf16[640,768]{1,0:T(8,128)(2,1)S(1)}, bf16[640,768]{1,0:T(8,128)(2,1)S(1)}, u32[]{:S(2)}, u32[]{:S(2)}) collective-permute-start(bf16[640,768]{1,0:T(8,128)(2,1)S(1)} %bitcast.13), channel_id=1, source_target_pairs={{0,16},{16,0},{1,17},{17,1},{2,18},{18,2},{3,19},{19,3},{4,20},{20... | collective-permute-start | bytes 2949128 | tf_op jit(solution)/shard_map/ppermute | solution.py:447
  71.7 1.0 copy-start.9
  83.7 12.4 %collective-permute-start.9 = (bf16[640,768]{1,0:T(8,128)(2,1)}, bf16[640,768]{1,0:T(8,128)(2,1)S(1)}, u32[]{:S(2)}, u32[]{:S(2)}) collective-permute-start(bf16[640,768]{1,0:T(8,128)(2,1)} %get-tuple-element.67), channel_id=1, source_target_pairs={{0,16},{16,0},{1,17},{17,1},{2,18},{18,2},{3,19},{19,3},{4,20},{20... | collective-permute-start | bytes 2949128 | tf_op jit(solution)/shard_map/ppermute | solution.py:447
  84.2 12.0 %copy-start.4 = (bf16[640,768]{1,0:T(8,128)(2,1)S(1)}, bf16[640,768]{1,0:T(8,128)(2,1)}, u32[]{:S(2)}) copy-start(bf16[640,768]{1,0:T(8,128)(2,1)} %get-tuple-element.66) | copy-start | bytes 2949124
  93.3 22.0 %collective-permute-start.12 = (bf16[576,768]{1,0:T(8,128)(2,1)}, bf16[576,768]{1,0:T(8,128)(2,1)S(1)}, u32[]{:S(2)}, u32[]{:S(2)}) collective-permute-start(bf16[576,768]{1,0:T(8,128)(2,1)} %get-tuple-element.87), channel_id=1, source_target_pairs={{0,224},{32,0},{64,32},{96,64},{128,96},{160,128},{192,160},{224,1... | collective-permute-start | bytes 2654216 | tf_op jit(solution)/shard_map/ppermute | solution.py:441
  96.1 31.6 %collective-permute-start.14 = (bf16[576,768]{1,0:T(8,128)(2,1)}, bf16[576,768]{1,0:T(8,128)(2,1)}, u32[]{:S(2)}, u32[]{:S(2)}) collective-permute-start(bf16[576,768]{1,0:T(8,128)(2,1)} %get-tuple-element.89), channel_id=1, source_target_pairs={{0,32},{32,64},{64,96},{96,128},{128,160},{160,192},{192,224},{224... | collective-permute-start | bytes 2654216 | tf_op jit(solution)/shard_map/ppermute | solution.py:441
  97.3 24.0 %all-to-all-start.2 = ((bf16[16,40,768]{2,1,0:T(8,128)(2,1)}), bf16[16,40,768]{2,1,0:T(8,128)(2,1)S(1)}, u32[]{:S(2)}, u32[]{:S(2)}) async-start(bf16[16,40,768]{2,1,0:T(8,128)(2,1)} %bitcast.6), calls=%async_computation.2 | async-start | bytes 1966080 | tf_op jit(solution)/shard_map/all_to_all | solution.py:450
  115.4 10.0 %copy-start.7 = (bf16[576,768]{1,0:T(8,128)(2,1)}, bf16[576,768]{1,0:T(8,128)(2,1)S(1)}, u32[]{:S(2)}) copy-start(bf16[576,768]{1,0:T(8,128)(2,1)S(1)} %collective-permute-done.12.refs_4_) | copy-start | bytes 2654212
  116.8 37.1 %collective-permute-start.13 = (bf16[288,768]{1,0:T(8,128)(2,1)S(1)}, bf16[288,768]{1,0:T(8,128)(2,1)}, u32[]{:S(2)}, u32[]{:S(2)}) collective-permute-start(bf16[288,768]{1,0:T(8,128)(2,1)S(1)} %add_convert_fusion.3), channel_id=1, source_target_pairs={{0,224},{32,0},{64,32},{96,64},{128,96},{160,128},{192,160},{224,1... | collective-permute-start | bytes 1327112 | tf_op jit(solution)/shard_map/ppermute | solution.py:441
  120.2 8.8 %collective-permute-start.10 = (bf16[640,768]{1,0:T(8,128)(2,1)}, bf16[640,768]{1,0:T(8,128)(2,1)S(1)}, u32[]{:S(2)}, u32[]{:S(2)}) collective-permute-start(bf16[640,768]{1,0:T(8,128)(2,1)} %get-tuple-element.77), channel_id=1, source_target_pairs={{0,16},{16,0},{1,17},{17,1},{2,18},{18,2},{3,19},{19,3},{4,20},{20... | collective-permute-start | bytes 2949128 | tf_op jit(solution)/shard_map/ppermute | solution.py:447
  121.4 1.0 copy-start.3
  122.4 5.4 %copy-start.6 = (bf16[288,768]{1,0:T(8,128)(2,1)S(1)}, bf16[288,768]{1,0:T(8,128)(2,1)}, u32[]{:S(2)}) copy-start(bf16[288,768]{1,0:T(8,128)(2,1)} %get-tuple-element.88) | copy-start | bytes 1327108
  125.3 3.7 %copy-start.1 = (bf16[640,768]{1,0:T(8,128)(2,1)S(1)}, bf16[640,768]{1,0:T(8,128)(2,1)}, u32[]{:S(2)}) copy-start(bf16[640,768]{1,0:T(8,128)(2,1)} %get-tuple-element.76) | copy-start | bytes 2949124
  125.3 22.1 %collective-permute-start.11 = (bf16[256,768]{1,0:T(8,128)(2,1)}, bf16[256,768]{1,0:T(8,128)(2,1)}, u32[]{:S(2)}, u32[]{:S(2)}) collective-permute-start(bf16[256,768]{1,0:T(8,128)(2,1)} %shard_map.116), channel_id=1, source_target_pairs={{0,128},{32,160},{64,192},{96,224},{128,0},{160,32},{192,64},{224,... | collective-permute-start | bytes 1179656 | tf_op jit(solution)/shard_map/ppermute | solution.py:441
  128.9 25.1 %collective-permute-start.15 = (bf16[288,768]{1,0:T(8,128)(2,1)S(1)}, bf16[288,768]{1,0:T(8,128)(2,1)}, u32[]{:S(2)}, u32[]{:S(2)}) collective-permute-start(bf16[288,768]{1,0:T(8,128)(2,1)S(1)} %add_convert_fusion.2), channel_id=1, source_target_pairs={{0,32},{32,64},{64,96},{96,128},{128,160},{160,192},{192,224},{224... | collective-permute-start | bytes 1327112 | tf_op jit(solution)/shard_map/ppermute | solution.py:441
  130.2 19.7 %all-to-all-start.3 = ((bf16[16,40,768]{2,1,0:T(8,128)(2,1)}), bf16[16,40,768]{2,1,0:T(8,128)(2,1)S(1)}, u32[]{:S(2)}, u32[]{:S(2)}) async-start(bf16[16,40,768]{2,1,0:T(8,128)(2,1)} %bitcast.8), calls=%async_computation.3 | async-start | bytes 1966080 | tf_op jit(solution)/shard_map/all_to_all | solution.py:450
  149.9 1.0 copy-start.5

commit v4 on v3

--- a/solution.py
+++ b/solution.py
@@ -97,6 +97,13 @@
     return routes, jnp.concatenate(gates, axis=0)
 
 
+def pack_body(routes_ref, gates_ref, tokens_ref, cot_ref, packed_ref):
+    tokens, width = tokens_ref.shape
+    packed_ref[:tokens, :] = tokens_ref[...]
+    packed_ref[tokens : 2 * tokens, :] = cot_ref[...]
+    packed_ref[2 * tokens :, :] = pack_info(routes_ref[...], gates_ref[...], width)
+
+
 def dispatch_body(experts, cap, far, *refs):
     stride = 2 * cap
     if far:
@@ -106,8 +113,8 @@
         own = packed_ref[:tokens, :]
         cot = packed_ref[tokens : 2 * tokens, :]
     else:
-        routes_ref, gates_ref, tokens_ref, cot_ref, *w_refs, out_ref, packed_ref, first_ref, second_ref = refs
-        tokens, width = tokens_ref.shape
+        routes_ref, gates_ref, tokens_ref, cot_ref, *w_refs, out_ref, first_ref, second_ref = refs
+        tokens = tokens_ref.shape[0]
         routes, gates_row = routes_ref[...], gates_ref[...]
         own, cot = tokens_ref[...], cot_ref[...]
         part = w_refs[0].shape[1] // 2
@@ -115,9 +122,6 @@
             for m, ref in enumerate(w_refs):
                 rows = ref[0, half * part : (half + 1) * part, :]
                 half_ref[m * part : (m + 1) * part, :] = rows
-        packed_ref[:tokens, :] = own
-        packed_ref[tokens : 2 * tokens, :] = cot
-        packed_ref[2 * tokens :, :] = pack_info(routes, gates_row, width)
     slots, gates = route_info(routes, gates_row, experts, stride)
     row_ids = lax.broadcasted_iota(jnp.int32, (experts * stride, tokens), 0)
     gated = [(cot.astype(F32) * gates[k]).astype(BF16) for k in range(2)]
@@ -457,10 +461,9 @@
 
     def dispatch(micros, far, *given):
         sent = jax.ShapeDtypeStruct((rows, width), BF16)
-        packed = jax.ShapeDtypeStruct((2 * tok_rows + 16, width), BF16)
         shard = jax.ShapeDtypeStruct((3 * part, width), BF16)
         body = functools.partial(dispatch_body, experts, cap, far)
-        return kernel_call(body, [sent] if far else [sent, packed, shard, shard], micros, given)
+        return kernel_call(body, [sent] if far else [sent, shard, shard], micros, given)
 
     def summed(outs):
         return rounded_sum(outs[0], other_core(outs[1]))
@@ -472,7 +475,9 @@
         return kernel_call(body, [both] if far else [one] * 2, micros, (*info, returned, *share))
 
     near_info = (routes.T, route_gates.T)
-    near_sent, packed, first, second = dispatch(
+    packed = jax.ShapeDtypeStruct((2 * tok_rows + 16, width), BF16)
+    packed = kernel_call(pack_body, [packed], 1.0, (*near_info, tokens, cotangent))[0]
+    near_sent, first, second = dispatch(
         2.0, False, *near_info, tokens, cotangent, gate_weight, up_weight, down_weight
     )
     far_packed = opposite(packed)

time: 158 us -> 156 us (0.987)
  waiting for transfers between devices: 36.9 us -> 33.5 us
  Pallas kernels: 55.8 us -> 57.5 us
    ppermute x12, waiting for transfers between devices: 34.1 us -> 30.7 us  [along(): lax.ppermute(value, 'z', [(i, (i + step) % ring) for i in range(ring)])]
    pallas_call x10 -> x11, Pallas kernels: 55.8 us -> 57.5 us  [kernel_call(): pl.pallas_call(body, out_shape=out_shapes, in_specs=whole(len(operands) -...]
  transfers between devices with their start and end apart: 20 -> 20, of which waited for: 8 -> 7; matrix products, arithmetic and copies ran while one was open for 3% -> 3% of each run, Pallas kernels for 24% -> 27%
where the time goes in v4:
time: 156 us
  Pallas kernels  57.5 us (37%)
  starting transfers between devices  51.8 us (33%)
  waiting for transfers between devices  33.5 us (21%)
  local copies, waits for them, and re-layouts  7.03 us (5%)
  other arithmetic  4.92 us (3%)
    pallas_call x11, Pallas kernels, kernel_call(): pl.pallas_call(body, out_shape=out_shapes, in_specs=whole(len(operands) -...  57.5 us
    ppermute x12, waiting for transfers between devices, along(): lax.ppermute(value, 'z', [(i, (i + step) % ring) for i in range(ring)])  30.7 us
    ppermute x12, starting transfers between devices, along(): lax.ppermute(value, 'z', [(i, (i + step) % ring) for i in range(ring)])  24.4 us
    all_to_all x4, starting transfers between devices, exchange(): lax.all_to_all(value.reshape(experts, 2 * cap, width), 'expert', split_ax...  23.2 us
    unnamed x30, local copies, waits for them, and re-layouts  7.03 us
    convert_element_type x4, other arithmetic, rounded_sum(): return (a.astype(F32) + b.astype(F32)).astype(BF16)  4.92 us
    ppermute x4, starting transfers between devices, other_core(): return lax.ppermute(value, 'core', [(0, 1), (1, 0)])  4.2 us
  transfers between devices with their start and end apart: 20, of which 7 were waited for; matrix products, arithmetic and copies ran while one was open for 3% of the time, Pallas kernels for 27%

profile of v4, /device:TPU:1, one launch (start us, length us, event | category | flops | bytes accessed | tf_op | source)
XLA Modules:
  0.0 155.6 jit_solution(7483089427574627009)
XLA Ops:
  0.6 1.8 %shard_map.111 = bf16[272,768]{1,0:T(8,128)(2,1)} custom-call(s32[2,128]{1,0:T(2,128)} %bitcast.18, f32[2,128]{1,0:T(2,128)} %bitcast.21, bf16[128,768]{1,0:T(8,128)(2,1)} %tokens_ref.1, bf16[128,768]{1,0:T(8,128)(2,1)} %cot_ref.1), custom_call_target="tpu_custom_call" | custom-call | flops 1150000000 | tf_op jit(solution)/shard_map/pallas_call | solution.py:43
  2.5 7.7 %collective-permute-start = (bf16[272,768]{1,0:T(8,128)(2,1)}, bf16[272,768]{1,0:T(8,128)(2,1)S(1)}, u32[]{:S(2)}, u32[]{:S(2)}) collective-permute-start(bf16[272,768]{1,0:T(8,128)(2,1)} %shard_map.111), channel_id=1, source_target_pairs={{0,128},{32,160},{64,192},{96,224},{128,0},{160,32},{192,64},{224,... | collective-permute-start | bytes 1253384 | tf_op jit(solution)/shard_map/ppermute | solution.py:445
  10.2 3.4 %shard_map.110 = (bf16[640,768]{1,0:T(8,128)(2,1)}, bf16[288,768]{1,0:T(8,128)(2,1)}, bf16[288,768]{1,0:T(8,128)(2,1)}) custom-call(s32[2,128]{1,0:T(2,128)} %bitcast.19, f32[2,128]{1,0:T(2,128)} %bitcast.22, bf16[128,768]{1,0:T(8,128)(2,1)} %tokens_ref.1, bf16[128,768]{1,0:T(8,128)(2,1)} %cot_ref.1, bf16[1,192,768]{2,1,0:T(8,128)(2,1)} %refs_4_.1, ...), custom_call_target="tpu_custom_call" | custom-call | flops 2300000000 | tf_op jit(solution)/shard_map/pallas_call | solution.py:43
  13.6 6.8 %all-to-all-start = ((bf16[16,40,768]{2,1,0:T(8,128)(2,1)}), bf16[16,40,768]{2,1,0:T(8,128)(2,1)S(1)}, u32[]{:S(2)}, u32[]{:S(2)}) async-start(bf16[16,40,768]{2,1,0:T(8,128)(2,1)} %bitcast.16), calls=%async_computation | async-start | bytes 1966080 | tf_op jit(solution)/shard_map/all_to_all | solution.py:454
  20.4 0.8 collective-permute-start.1
  21.2 1.9 %collective-permute-start.2 = (bf16[288,768]{1,0:T(8,128)(2,1)}, bf16[288,768]{1,0:T(8,128)(2,1)S(1)}, u32[]{:S(2)}, u32[]{:S(2)}) collective-permute-start(bf16[288,768]{1,0:T(8,128)(2,1)} %get-tuple-element.50.refs_3_), channel_id=1, source_target_pairs={{0,224},{32,0},{64,32},{96,64},{128,96},{160,128},{192,160},{224,1... | collective-permute-start | bytes 1327112 | tf_op jit(solution)/shard_map/ppermute | solution.py:445
  23.1 0.0 collective-permute-done.refs_0_
  23.1 0.8 copy-done.14
  23.9 2.8 %shard_map.112 = bf16[640,768]{1,0:T(8,128)(2,1)} custom-call(bf16[272,768]{1,0:T(8,128)(2,1)} %copy-done.14), custom_call_target="tpu_custom_call" | custom-call | flops 5750000128 | tf_op jit(solution)/shard_map/pallas_call | solution.py:43
  26.7 11.6 %collective-permute-done.1.refs_4_ = bf16[288,768]{1,0:T(8,128)(2,1)S(1)} collective-permute-done((bf16[288,768]{1,0:T(8,128)(2,1)}, bf16[288,768]{1,0:T(8,128)(2,1)S(1)}, u32[]{:S(2)}, u32[]{:S(2)}) %collective-permute-start.1) | collective-permute-done | bytes 442400 | tf_op jit(solution)/shard_map/ppermute | solution.py:445
  38.3 0.8 copy-done.12
  39.1 0.0 collective-permute-done.2.refs_5_
  39.1 0.0 all-to-all-done
  39.1 0.8 copy-done.13
  39.9 1.1 collective-permute-start.3
  41.0 2.3 %collective-permute-start.5 = (bf16[288,768]{1,0:T(8,128)(2,1)}, bf16[288,768]{1,0:T(8,128)(2,1)S(1)}, u32[]{:S(2)}, u32[]{:S(2)}) collective-permute-start(bf16[288,768]{1,0:T(8,128)(2,1)} %get-tuple-element.49.refs_2_), channel_id=1, source_target_pairs={{0,224},{32,0},{64,32},{96,64},{128,96},{160,128},{192,160},{224,1... | collective-permute-start | bytes 1327112 | tf_op jit(solution)/shard_map/ppermute | solution.py:445
  43.4 0.0 collective-permute-start.4
  43.4 6.8 %all-to-all-start.1 = ((bf16[16,40,768]{2,1,0:T(8,128)(2,1)}), bf16[16,40,768]{2,1,0:T(8,128)(2,1)S(1)}, u32[]{:S(2)}, u32[]{:S(2)}) async-start(bf16[16,40,768]{2,1,0:T(8,128)(2,1)} %bitcast.12), calls=%async_computation.1 | async-start | bytes 1966080 | tf_op jit(solution)/shard_map/all_to_all | solution.py:454
  50.1 0.1 collective-permute-start.6
  50.2 2.7 %collective-permute-start.7 = (bf16[288,768]{1,0:T(8,128)(2,1)}, bf16[288,768]{1,0:T(8,128)(2,1)}, u32[]{:S(2)}, u32[]{:S(2)}) collective-permute-start(bf16[288,768]{1,0:T(8,128)(2,1)} %copy-done.13), channel_id=1, source_target_pairs={{0,224},{32,0},{64,32},{96,64},{128,96},{160,128},{192,160},{224,1... | collective-permute-start | bytes 1327112 | tf_op jit(solution)/shard_map/ppermute | solution.py:445
  53.0 0.0 collective-permute-done.3.refs_1_
  53.0 1.0 copy-done.8
  53.9 7.3 %shard_map.113 = (bf16[640,384]{1,0:T(8,128)(2,1)}, bf16[640,384]{1,0:T(8,128)(2,1)}, bf16[640,384]{1,0:T(8,128)(2,1)}, bf16[640,768]{1,0:T(8,128)(2,1)}, bf16[6...) custom-call(bf16[640,768]{1,0:T(8,128)(2,1)} %bitcast.11, bf16[640,768]{1,0:T(8,128)(2,1)} %copy-done.8, ...), custom_call_target="tpu_custom_call" | custom-call | flops 23000000512 | tf_op jit(solution)/shard_map/pallas_call | solution.py:43
  61.2 0.0 collective-permute-done.5.refs_7_.refs_8_.refs_16_
  61.2 0.0 copy-start.10
  61.2 0.0 collective-permute-done.4.refs_6_.refs_7_.refs_15_
  61.3 4.5 %collective-permute-done.6.refs_8_.refs_9_.refs_17_ = bf16[288,768]{1,0:T(8,128)(2,1)S(1)} collective-permute-done((bf16[288,768]{1,0:T(8,128)(2,1)}, bf16[288,768]{1,0:T(8,128)(2,1)S(1)}, u32[]{:S(2)}, u32[]{:S(2)}) %collective-permute-start.6) | collective-permute-done | bytes 442400 | tf_op jit(solution)/shard_map/ppermute | solution.py:445
  65.7 0.8 copy-done.11
  66.5 0.0 collective-permute-done.7.refs_9_.refs_10_.refs_18_
  66.5 0.0 all-to-all-done.1
  66.5 1.4 collective-permute-start.8
  67.9 2.2 %collective-permute-done.8.refs_1_ = bf16[640,768]{1,0:T(8,128)(2,1)S(1)} collective-permute-done((bf16[640,768]{1,0:T(8,128)(2,1)S(1)}, bf16[640,768]{1,0:T(8,128)(2,1)S(1)}, u32[]{:S(2)}, u32[]{:S(2)}) %collective-permute-start.8) | collective-permute-done | bytes 983072 | tf_op jit(solution)/shard_map/ppermute | solution.py:451
  70.1 1.0 copy-done.9
  71.1 11.0 %shard_map.114 = (bf16[640,768]{1,0:T(8,128)(2,1)}, bf16[640,768]{1,0:T(8,128)(2,1)}, bf16[640,768]{1,0:T(8,128)(2,1)}, bf16[640,768]{1,0:T(8,128)(2,1)}, bf16[6...) custom-call(bf16[640,768]{1,0:T(8,128)(2,1)} %bitcast.14, bf16[640,768]{1,0:T(8,128)(2,1)} %copy-done.9, ...), custom_call_target="tpu_custom_call" | custom-call | flops 11500000256 | tf_op jit(solution)/shard_map/pallas_call | solution.py:43
  82.1 0.5 collective-permute-start.9
  82.5 9.1 %shard_map.115 = (bf16[576,768]{1,0:T(8,128)(2,1)}, bf16[576,768]{1,0:T(8,128)(2,1)}, bf16[640,384]{1,0:T(8,128)(2,1)}, bf16[640,384]{1,0:T(8,128)(2,1)}, bf16[640,384]{1,0:T(8,128)(2,1)}) custom-call(bf16[640,768]{1,0:T(8,128)(2,1)} %get-tuple-element.52.refs_0_, bf16[640,768]{1,0:T(8,128)(2,1)} %get-tuple-element.53.refs_1_, ...), custom_call_target="tpu_custom_call" | custom-call | flops 9200000000 | tf_op jit(solution)/shard_map/pallas_call | solution.py:43
  91.7 2.8 %collective-permute-start.12 = (bf16[576,768]{1,0:T(8,128)(2,1)}, bf16[576,768]{1,0:T(8,128)(2,1)S(1)}, u32[]{:S(2)}, u32[]{:S(2)}) collective-permute-start(bf16[576,768]{1,0:T(8,128)(2,1)} %get-tuple-element.85), channel_id=1, source_target_pairs={{0,224},{32,0},{64,32},{96,64},{128,96},{160,128},{192,160},{224,1... | collective-permute-start | bytes 2654216 | tf_op jit(solution)/shard_map/ppermute | solution.py:445
  94.5 0.0 collective-permute-start.14
  94.5 0.0 collective-permute-done.9
  94.5 1.2 add_convert_fusion.1
  95.7 5.5 %all-to-all-start.2 = ((bf16[16,40,768]{2,1,0:T(8,128)(2,1)}), bf16[16,40,768]{2,1,0:T(8,128)(2,1)S(1)}, u32[]{:S(2)}, u32[]{:S(2)}) async-start(bf16[16,40,768]{2,1,0:T(8,128)(2,1)} %bitcast.6), calls=%async_computation.2 | async-start | bytes 1966080 | tf_op jit(solution)/shard_map/all_to_all | solution.py:454
  101.2 11.0 %shard_map.116 = (bf16[288,768]{1,0:T(8,128)(2,1)}, bf16[288,768]{1,0:T(8,128)(2,1)}, bf16[288,768]{1,0:T(8,128)(2,1)}, bf16[288,768]{1,0:T(8,128)(2,1)}, bf16[6...) custom-call(bf16[640,768]{1,0:T(8,128)(2,1)} %get-tuple-element.52.refs_0_, bf16[640,768]{1,0:T(8,128)(2,1)} %get-tuple-element.53.refs_1_, ...), custom_call_target="tpu_custom_call" | custom-call | flops 9200000000 | tf_op jit(solution)/shard_map/pallas_call | solution.py:43
  112.2 1.5 collective-permute-done.12.refs_4_
  113.7 1.4 add_convert_fusion.3
  115.1 3.4 %collective-permute-start.13 = (bf16[288,768]{1,0:T(8,128)(2,1)S(1)}, bf16[288,768]{1,0:T(8,128)(2,1)}, u32[]{:S(2)}, u32[]{:S(2)}) collective-permute-start(bf16[288,768]{1,0:T(8,128)(2,1)S(1)} %add_convert_fusion.3), channel_id=1, source_target_pairs={{0,224},{32,0},{64,32},{96,64},{128,96},{160,128},{192,160},{224,1... | collective-permute-start | bytes 1327112 | tf_op jit(solution)/shard_map/ppermute | solution.py:445
  118.5 1.2 collective-permute-start.10
  119.8 0.0 all-to-all-done.2
  119.8 1.0 copy-done.3
  120.7 2.9 %shard_map.117 = bf16[256,768]{1,0:T(8,128)(2,1)} custom-call(bf16[272,768]{1,0:T(8,128)(2,1)} %copy-done.14, bf16[640,768]{1,0:T(8,128)(2,1)} %bitcast.15), custom_call_target="tpu_custom_call" | custom-call | flops 34500001792 | tf_op jit(solution)/shard_map/pallas_call | solution.py:43
  123.7 2.4 %collective-permute-start.11 = (bf16[256,768]{1,0:T(8,128)(2,1)}, bf16[256,768]{1,0:T(8,128)(2,1)}, u32[]{:S(2)}, u32[]{:S(2)}) collective-permute-start(bf16[256,768]{1,0:T(8,128)(2,1)} %shard_map.117), channel_id=1, source_target_pairs={{0,128},{32,160},{64,192},{96,224},{128,0},{160,32},{192,64},{224,... | collective-permute-start | bytes 1179656 | tf_op jit(solution)/shard_map/ppermute | solution.py:445
  126.1 0.0 collective-permute-done.14.refs_5_
  126.1 1.1 add_convert_fusion.2
  127.3 0.1 collective-permute-start.15
  127.4 0.0 collective-permute-done.10
  127.4 1.2 add_convert_fusion
  128.6 4.3 %all-to-all-start.3 = ((bf16[16,40,768]{2,1,0:T(8,128)(2,1)}), bf16[16,40,768]{2,1,0:T(8,128)(2,1)S(1)}, u32[]{:S(2)}, u32[]{:S(2)}) async-start(bf16[16,40,768]{2,1,0:T(8,128)(2,1)} %bitcast.8), calls=%async_computation.3 | async-start | bytes 1966080 | tf_op jit(solution)/shard_map/all_to_all | solution.py:454
  132.8 12.9 %collective-permute-done.11.given_ref = bf16[256,768]{1,0:T(8,128)(2,1)} collective-permute-done((bf16[256,768]{1,0:T(8,128)(2,1)}, bf16[256,768]{1,0:T(8,128)(2,1)}, u32[]{:S(2)}, u32[]{:S(2)}) %collective-permute-start.11) | collective-permute-done | bytes 393248 | tf_op jit(solution)/shard_map/ppermute | solution.py:445
  145.8 1.9 %shard_map.118 = (f32[128,768]{1,0:T(8,128)}, f32[128,768]{1,0:T(8,128)}) custom-call(bf16[256,768]{1,0:T(8,128)(2,1)} %collective-permute-done.11.given_ref), custom_call_target="tpu_custom_call" | custom-call | flops 11500000256 | tf_op jit(solution)/shard_map/pallas_call | solution.py:43
  147.7 0.6 all-to-all-done.3
  148.3 1.0 copy-done.5
  149.2 2.9 %shard_map.119 = (bf16[128,768]{1,0:T(8,128)(2,1)}, bf16[128,768]{1,0:T(8,128)(2,1)}) custom-call(s32[2,128]{1,0:T(2,128)} %bitcast.20, f32[2,128]{1,0:T(2,128)} %bitcast.23, bf16[640,768]{1,0:T(8,128)(2,1)} %bitcast.17, f32[128,768]{1,0:T(8,128)} %get-tuple-element.77.refs_3_, f32[128,768]{1,0:T(8,128)} %get-tuple-element.78.refs_4_), custom_call_target="tpu_custom_call" | custom-call | flops 2300000000 | tf_op jit(solution)/shard_map/pallas_call | solution.py:43
  152.2 0.0 collective-permute-done.13.refs_2_
  152.2 0.2 collective-permute-done.15.refs_3_
  152.3 3.3 %shard_map.120 = (f32[1,192,768]{2,1,0:T(8,128)}, f32[1,192,768]{2,1,0:T(8,128)}, f32[1,192,768]{2,1,0:T(8,128)}) custom-call(bf16[288,768]{1,0:T(8,128)(2,1)} %get-tuple-element.82.refs_0_, bf16[288,768]{1,0:T(8,128)(2,1)} %get-tuple-element.83.refs_1_, bf16[288,768]{1,0:T(8,128)(2,1)} %collective-permute-done.13.refs_2_, ...), custom_call_target="tpu_custom_call" | custom-call | flops 2300000000 | tf_op jit(solution)/shard_map/pallas_call | solution.py:43
  (21 shorter events, 0.0 us)
Async XLA Ops:
  2.5 20.6 %collective-permute-start = (bf16[272,768]{1,0:T(8,128)(2,1)}, bf16[272,768]{1,0:T(8,128)(2,1)S(1)}, u32[]{:S(2)}, u32[]{:S(2)}) collective-permute-start(bf16[272,768]{1,0:T(8,128)(2,1)} %shard_map.111), channel_id=1, source_target_pairs={{0,128},{32,160},{64,192},{96,224},{128,0},{160,32},{192,64},{224,... | collective-permute-start | bytes 1253384 | tf_op jit(solution)/shard_map/ppermute | solution.py:445
  13.6 25.5 %all-to-all-start = ((bf16[16,40,768]{2,1,0:T(8,128)(2,1)}), bf16[16,40,768]{2,1,0:T(8,128)(2,1)S(1)}, u32[]{:S(2)}, u32[]{:S(2)}) async-start(bf16[16,40,768]{2,1,0:T(8,128)(2,1)} %bitcast.16), calls=%async_computation | async-start | bytes 1966080 | tf_op jit(solution)/shard_map/all_to_all | solution.py:454
  20.4 18.0 %collective-permute-start.1 = (bf16[288,768]{1,0:T(8,128)(2,1)}, bf16[288,768]{1,0:T(8,128)(2,1)S(1)}, u32[]{:S(2)}, u32[]{:S(2)}) collective-permute-start(bf16[288,768]{1,0:T(8,128)(2,1)} %get-tuple-element.49.refs_2_), channel_id=1, source_target_pairs={{0,32},{32,64},{64,96},{96,128},{128,160},{160,192},{192,224},{224... | collective-permute-start | bytes 1327112 | tf_op jit(solution)/shard_map/ppermute | solution.py:445
  21.2 17.9 %collective-permute-start.2 = (bf16[288,768]{1,0:T(8,128)(2,1)}, bf16[288,768]{1,0:T(8,128)(2,1)S(1)}, u32[]{:S(2)}, u32[]{:S(2)}) collective-permute-start(bf16[288,768]{1,0:T(8,128)(2,1)} %get-tuple-element.50.refs_3_), channel_id=1, source_target_pairs={{0,224},{32,0},{64,32},{96,64},{128,96},{160,128},{192,160},{224,1... | collective-permute-start | bytes 1327112 | tf_op jit(solution)/shard_map/ppermute | solution.py:445
  23.1 0.8 copy-start.14
  38.3 0.8 copy-start.12
  39.1 0.8 copy-start.13
  39.1 4.2 %copy-start = (bf16[16,40,768]{2,1,0:T(8,128)(2,1)}, bf16[16,40,768]{2,1,0:T(8,128)(2,1)S(1)}, u32[]{:S(2)}) copy-start(bf16[16,40,768]{2,1,0:T(8,128)(2,1)S(1)} %all-to-all-done) | copy-start | bytes 2949124
  39.9 13.1 %collective-permute-start.3 = (bf16[640,768]{1,0:T(8,128)(2,1)S(1)}, bf16[640,768]{1,0:T(8,128)(2,1)S(1)}, u32[]{:S(2)}, u32[]{:S(2)}) collective-permute-start(bf16[640,768]{1,0:T(8,128)(2,1)S(1)} %bitcast.10), channel_id=1, source_target_pairs={{0,16},{16,0},{1,17},{17,1},{2,18},{18,2},{3,19},{19,3},{4,20},{20... | collective-permute-start | bytes 2949128 | tf_op jit(solution)/shard_map/ppermute | solution.py:451
  41.0 20.2 %collective-permute-start.5 = (bf16[288,768]{1,0:T(8,128)(2,1)}, bf16[288,768]{1,0:T(8,128)(2,1)S(1)}, u32[]{:S(2)}, u32[]{:S(2)}) collective-permute-start(bf16[288,768]{1,0:T(8,128)(2,1)} %get-tuple-element.49.refs_2_), channel_id=1, source_target_pairs={{0,224},{32,0},{64,32},{96,64},{128,96},{160,128},{192,160},{224,1... | collective-permute-start | bytes 1327112 | tf_op jit(solution)/shard_map/ppermute | solution.py:445
  43.4 17.9 %collective-permute-start.4 = (bf16[288,768]{1,0:T(8,128)(2,1)}, bf16[288,768]{1,0:T(8,128)(2,1)}, u32[]{:S(2)}, u32[]{:S(2)}) collective-permute-start(bf16[288,768]{1,0:T(8,128)(2,1)} %get-tuple-element.50.refs_3_), channel_id=1, source_target_pairs={{0,32},{32,64},{64,96},{96,128},{128,160},{160,192},{192,224},{224... | collective-permute-start | bytes 1327112 | tf_op jit(solution)/shard_map/ppermute | solution.py:445
  43.4 23.1 %all-to-all-start.1 = ((bf16[16,40,768]{2,1,0:T(8,128)(2,1)}), bf16[16,40,768]{2,1,0:T(8,128)(2,1)S(1)}, u32[]{:S(2)}, u32[]{:S(2)}) async-start(bf16[16,40,768]{2,1,0:T(8,128)(2,1)} %bitcast.12), calls=%async_computation.1 | async-start | bytes 1966080 | tf_op jit(solution)/shard_map/all_to_all | solution.py:454
  50.1 15.6 %collective-permute-start.6 = (bf16[288,768]{1,0:T(8,128)(2,1)}, bf16[288,768]{1,0:T(8,128)(2,1)S(1)}, u32[]{:S(2)}, u32[]{:S(2)}) collective-permute-start(bf16[288,768]{1,0:T(8,128)(2,1)} %copy-done.12), channel_id=1, source_target_pairs={{0,32},{32,64},{64,96},{96,128},{128,160},{160,192},{192,224},{224... | collective-permute-start | bytes 1327112 | tf_op jit(solution)/shard_map/ppermute | solution.py:445
  50.2 16.3 %collective-permute-start.7 = (bf16[288,768]{1,0:T(8,128)(2,1)}, bf16[288,768]{1,0:T(8,128)(2,1)}, u32[]{:S(2)}, u32[]{:S(2)}) collective-permute-start(bf16[288,768]{1,0:T(8,128)(2,1)} %copy-done.13), channel_id=1, source_target_pairs={{0,224},{32,0},{64,32},{96,64},{128,96},{160,128},{192,160},{224,1... | collective-permute-start | bytes 1327112 | tf_op jit(solution)/shard_map/ppermute | solution.py:445
  53.0 1.0 copy-start.8
  61.2 8.8 %copy-start.10 = (bf16[288,768]{1,0:T(8,128)(2,1)}, bf16[288,768]{1,0:T(8,128)(2,1)S(1)}, u32[]{:S(2)}) copy-start(bf16[288,768]{1,0:T(8,128)(2,1)S(1)} %collective-permute-done.5.refs_7_.refs_8_.refs_16_) | copy-start | bytes 1327108
  65.7 0.8 copy-start.11
  66.5 3.6 %copy-start.2 = (bf16[16,40,768]{2,1,0:T(8,128)(2,1)}, bf16[16,40,768]{2,1,0:T(8,128)(2,1)S(1)}, u32[]{:S(2)}) copy-start(bf16[16,40,768]{2,1,0:T(8,128)(2,1)S(1)} %all-to-all-done.1) | copy-start | bytes 2949124
  66.5 3.6 %collective-permute-start.8 = (bf16[640,768]{1,0:T(8,128)(2,1)S(1)}, bf16[640,768]{1,0:T(8,128)(2,1)S(1)}, u32[]{:S(2)}, u32[]{:S(2)}) collective-permute-start(bf16[640,768]{1,0:T(8,128)(2,1)S(1)} %bitcast.13), channel_id=1, source_target_pairs={{0,16},{16,0},{1,17},{17,1},{2,18},{18,2},{3,19},{19,3},{4,20},{20... | collective-permute-start | bytes 2949128 | tf_op jit(solution)/shard_map/ppermute | solution.py:451
  70.1 1.0 copy-start.9
  82.1 12.4 %collective-permute-start.9 = (bf16[640,768]{1,0:T(8,128)(2,1)}, bf16[640,768]{1,0:T(8,128)(2,1)S(1)}, u32[]{:S(2)}, u32[]{:S(2)}) collective-permute-start(bf16[640,768]{1,0:T(8,128)(2,1)} %get-tuple-element.65), channel_id=1, source_target_pairs={{0,16},{16,0},{1,17},{17,1},{2,18},{18,2},{3,19},{19,3},{4,20},{20... | collective-permute-start | bytes 2949128 | tf_op jit(solution)/shard_map/ppermute | solution.py:451
  82.5 12.0 %copy-start.4 = (bf16[640,768]{1,0:T(8,128)(2,1)S(1)}, bf16[640,768]{1,0:T(8,128)(2,1)}, u32[]{:S(2)}) copy-start(bf16[640,768]{1,0:T(8,128)(2,1)} %get-tuple-element.64) | copy-start | bytes 2949124
  91.7 22.0 %collective-permute-start.12 = (bf16[576,768]{1,0:T(8,128)(2,1)}, bf16[576,768]{1,0:T(8,128)(2,1)S(1)}, u32[]{:S(2)}, u32[]{:S(2)}) collective-permute-start(bf16[576,768]{1,0:T(8,128)(2,1)} %get-tuple-element.85), channel_id=1, source_target_pairs={{0,224},{32,0},{64,32},{96,64},{128,96},{160,128},{192,160},{224,1... | collective-permute-start | bytes 2654216 | tf_op jit(solution)/shard_map/ppermute | solution.py:445
  94.5 31.6 %collective-permute-start.14 = (bf16[576,768]{1,0:T(8,128)(2,1)}, bf16[576,768]{1,0:T(8,128)(2,1)}, u32[]{:S(2)}, u32[]{:S(2)}) collective-permute-start(bf16[576,768]{1,0:T(8,128)(2,1)} %get-tuple-element.87), channel_id=1, source_target_pairs={{0,32},{32,64},{64,96},{96,128},{128,160},{160,192},{192,224},{224... | collective-permute-start | bytes 2654216 | tf_op jit(solution)/shard_map/ppermute | solution.py:445
  95.7 24.0 %all-to-all-start.2 = ((bf16[16,40,768]{2,1,0:T(8,128)(2,1)}), bf16[16,40,768]{2,1,0:T(8,128)(2,1)S(1)}, u32[]{:S(2)}, u32[]{:S(2)}) async-start(bf16[16,40,768]{2,1,0:T(8,128)(2,1)} %bitcast.6), calls=%async_computation.2 | async-start | bytes 1966080 | tf_op jit(solution)/shard_map/all_to_all | solution.py:454
  113.7 10.0 %copy-start.7 = (bf16[576,768]{1,0:T(8,128)(2,1)}, bf16[576,768]{1,0:T(8,128)(2,1)S(1)}, u32[]{:S(2)}) copy-start(bf16[576,768]{1,0:T(8,128)(2,1)S(1)} %collective-permute-done.12.refs_4_) | copy-start | bytes 2654212
  115.1 37.0 %collective-permute-start.13 = (bf16[288,768]{1,0:T(8,128)(2,1)S(1)}, bf16[288,768]{1,0:T(8,128)(2,1)}, u32[]{:S(2)}, u32[]{:S(2)}) collective-permute-start(bf16[288,768]{1,0:T(8,128)(2,1)S(1)} %add_convert_fusion.3), channel_id=1, source_target_pairs={{0,224},{32,0},{64,32},{96,64},{128,96},{160,128},{192,160},{224,1... | collective-permute-start | bytes 1327112 | tf_op jit(solution)/shard_map/ppermute | solution.py:445
  118.5 8.8 %collective-permute-start.10 = (bf16[640,768]{1,0:T(8,128)(2,1)}, bf16[640,768]{1,0:T(8,128)(2,1)S(1)}, u32[]{:S(2)}, u32[]{:S(2)}) collective-permute-start(bf16[640,768]{1,0:T(8,128)(2,1)} %get-tuple-element.75), channel_id=1, source_target_pairs={{0,16},{16,0},{1,17},{17,1},{2,18},{18,2},{3,19},{19,3},{4,20},{20... | collective-permute-start | bytes 2949128 | tf_op jit(solution)/shard_map/ppermute | solution.py:451
  119.8 1.0 copy-start.3
  120.7 5.4 %copy-start.6 = (bf16[288,768]{1,0:T(8,128)(2,1)S(1)}, bf16[288,768]{1,0:T(8,128)(2,1)}, u32[]{:S(2)}) copy-start(bf16[288,768]{1,0:T(8,128)(2,1)} %get-tuple-element.86) | copy-start | bytes 1327108
  123.7 3.7 %copy-start.1 = (bf16[640,768]{1,0:T(8,128)(2,1)S(1)}, bf16[640,768]{1,0:T(8,128)(2,1)}, u32[]{:S(2)}) copy-start(bf16[640,768]{1,0:T(8,128)(2,1)} %get-tuple-element.74) | copy-start | bytes 2949124
  123.7 22.1 %collective-permute-start.11 = (bf16[256,768]{1,0:T(8,128)(2,1)}, bf16[256,768]{1,0:T(8,128)(2,1)}, u32[]{:S(2)}, u32[]{:S(2)}) collective-permute-start(bf16[256,768]{1,0:T(8,128)(2,1)} %shard_map.117), channel_id=1, source_target_pairs={{0,128},{32,160},{64,192},{96,224},{128,0},{160,32},{192,64},{224,... | collective-permute-start | bytes 1179656 | tf_op jit(solution)/shard_map/ppermute | solution.py:445
  127.3 25.1 %collective-permute-start.15 = (bf16[288,768]{1,0:T(8,128)(2,1)S(1)}, bf16[288,768]{1,0:T(8,128)(2,1)}, u32[]{:S(2)}, u32[]{:S(2)}) collective-permute-start(bf16[288,768]{1,0:T(8,128)(2,1)S(1)} %add_convert_fusion.2), channel_id=1, source_target_pairs={{0,32},{32,64},{64,96},{96,128},{128,160},{160,192},{192,224},{224... | collective-permute-start | bytes 1327112 | tf_op jit(solution)/shard_map/ppermute | solution.py:445
  128.6 19.7 %all-to-all-start.3 = ((bf16[16,40,768]{2,1,0:T(8,128)(2,1)}), bf16[16,40,768]{2,1,0:T(8,128)(2,1)S(1)}, u32[]{:S(2)}, u32[]{:S(2)}) async-start(bf16[16,40,768]{2,1,0:T(8,128)(2,1)} %bitcast.8), calls=%async_computation.3 | async-start | bytes 1966080 | tf_op jit(solution)/shard_map/all_to_all | solution.py:454
  148.3 1.0 copy-start.5
